TPU v7x, 1024 devices: a whole 4x4x32 slice. The times are simulated.
1024 devices in a mesh: layer: 4 (over x_lo, core), row: 8 (over x_hi, y), col: 32 (over z).
Axes of the slice: x: 4 (x_hi: 2, x_lo: 2; x = x_hi * 2 + x_lo), y: 4, z: 32, core: 2. Of those that a mesh axis runs over, the one named last changes fastest.
Arguments:
- left_blocks: float32 [4, 8, 32, 2, 256, 256], P('layer', 'row', 'col'), may hold values from -6 to 6
- right_blocks: float32 [4, 8, 32, 2, 256, 256], P('layer', 'row', 'col'), may hold values from -0.1875 to 0.1875
- left_index: int32 [4, 8, 32, 2, 12], P('layer', 'row', 'col'), may hold values from 0 to 1
- right_index: int32 [4, 8, 32, 2, 12], P('layer', 'row', 'col'), may hold values from 0 to 1
- target_index: int32 [4, 8, 32, 2, 12], P('layer', 'row', 'col'), may hold values from 0 to 3
- live_counts: int32 [4, 8, 32, 2], P('layer', 'row', 'col'), may hold values from 3 to 12, as said below
- keep_mask: int32 [8, 32, 4], P('row', 'col', 'layer'), may hold values 0 or 1
Outputs:
- product_blocks: float32 [8, 32, 4, 256, 256], P('row', 'col', 'layer')
Inputs may be any that keep to these rules, and one draw needn't show every extreme that they name: `live_counts`: every count is at most 12, and some device and step has exactly 12 live slots.
All inputs are finite; a program needn't handle non-finite values. No bound on the sum of `keep_mask` on one device may be relied on, other than what follows from the above.
Results may differ from a plain program's by a relative error of at most 0.0003.
Values sent between devices are 32-bit elements; how exact they have to be, the bound alone decides.
No kernel may reach another device: no remote copies, remote signals or barrier semaphores. Data moves between devices by JAX's collectives and lax.ppermute only.
A program may use at most 32 MiB of HBM per device.

v0:
```python
import jax
import jax.numpy as jnp
from jax import lax
from jax.sharding import PartitionSpec as P


def from_behind(value, axis, steps):
    count = lax.axis_size(axis)
    pairs = [(source, (source + steps) % count) for source in range(count)]
    return lax.ppermute(value, axis, pairs)


def step_terms(left_tile, right_tile, left_sel, right_sel, target_sel, count_now, nblocks):
    nprods = left_sel.shape[0]
    left_pick = left_tile[left_sel]
    right_pick = right_tile[right_sel]
    terms = jnp.einsum("pij,pjk->pik", left_pick, right_pick, precision=lax.Precision.HIGHEST)
    live = (jnp.arange(nprods, dtype=jnp.int32) < count_now).astype(jnp.float32)
    onehot = (target_sel[:, None] == jnp.arange(nblocks, dtype=jnp.int32)[None, :]).astype(
        jnp.float32
    ) * live[:, None]
    return jnp.einsum("pq,pik->qik", onehot, terms, precision=lax.Precision.HIGHEST)


def local(left_blocks, right_blocks, left_index, right_index, target_index, live_counts, keep_mask):
    left_tile = left_blocks[0, 0, 0]
    right_tile = right_blocks[0, 0, 0]
    nsteps = left_index.shape[3]
    nblocks = keep_mask.shape[2] * lax.axis_size("layer")
    gathered = None
    summed = None
    for step in range(nsteps):
        if step > 0:
            left_tile = from_behind(left_tile, "col", 1)
            right_tile = from_behind(right_tile, "row", 1)
        partial_value = step_terms(
            left_tile,
            right_tile,
            left_index[0, 0, 0, step],
            right_index[0, 0, 0, step],
            target_index[0, 0, 0, step],
            live_counts[0, 0, 0, step],
            nblocks,
        )
        gathered = partial_value if gathered is None else gathered + partial_value
    summed = lax.psum_scatter(gathered, "layer", scatter_dimension=0, tiled=True)
    result = summed * keep_mask[0, 0].astype(jnp.float32)[:, None, None]
    return result[None, None]


def solution(mesh):
    return jax.shard_map(
        local,
        mesh=mesh,
        in_specs=(
            P("layer", "row", "col", None, None, None),
            P("layer", "row", "col", None, None, None),
            P("layer", "row", "col", None, None),
            P("layer", "row", "col", None, None),
            P("layer", "row", "col", None, None),
            P("layer", "row", "col", None),
            P("row", "col", "layer"),
        ),
        out_specs=P("row", "col", "layer", None, None),
        check_vma=False,
    )
```

profile of v0, /device:TPU:1, one launch (start us, length us, event | category | flops | bytes accessed | tf_op | source)
XLA Modules:
  0.0 107.6 jit_solution(12989225862774264267)
XLA Ops:
  6.5 0.0 reduce-scatter.2.cloned.1.call-start
  6.5 4.4 %collective-permute-start = (f32[2,256,256]{2,1,0:T(8,128)}, f32[2,256,256]{2,1,0:T(8,128)S(1)}, u32[]{:S(2)}, u32[]{:S(2)}) collective-permute-start(f32[2,256,256]{2,1,0:T(8,128)} %bitcast.37), channel_id=1, source_target_pairs={{0,1},{1,2},{2,3},{3,4},{4,5},{5,6},{6,7},{7,8},{8,9},{9,10},{10,1... | collective-permute-start | bytes 1572872 | tf_op jit(solution)/shard_map/ppermute | solution.py:10
  10.9 3.2 %collective-permute-start.1 = (f32[2,256,256]{2,1,0:T(8,128)}, f32[2,256,256]{2,1,0:T(8,128)S(1)}, u32[]{:S(2)}, u32[]{:S(2)}) collective-permute-start(f32[2,256,256]{2,1,0:T(8,128)} %bitcast.39), channel_id=1, source_target_pairs={{0,32},{32,64},{64,96},{96,128},{128,160},{160,192},{192,224},{224... | collective-permute-start | bytes 1572872 | tf_op jit(solution)/shard_map/ppermute | solution.py:10
  14.1 0.8 fusion.17
  14.9 0.8 fusion.18
  15.7 1.4 %fusion.23 = (s32[1,1,1,1]{3,2,1,0:T(1,128)}, s32[1,1,1,1]{3,2,1,0:T(1,128)}) fusion(s32[1,1,1,2]{3,2,1,0:T(1,128)} %param.12), kind=kLoop, calls=%fused_computation.40 | loop fusion | bytes 16 | tf_op jit(solution)/shard_map/slice | solution.py:42
  17.0 0.7 compare_convert_fusion
  17.7 0.8 slice_bitcast_fusion.1
  18.5 0.0 copy-start
  18.5 3.5 %gather_fusion = f32[12,256,256]{2,1,0:T(8,128)} fusion(f32[2,256,256]{2,1,0:T(8,128)} %bitcast.38, s32[1024]{0:T(1024)S(1)} %pad_clamp_fusion.3), kind=kCustom, calls=%fused_computation | custom fusion | bytes 6291504 | tf_op jit(solution)/shard_map/gather | solution.py:15
  22.1 0.0 copy-done
  22.1 2.5 %gather_fusion.1 = f32[12,256,256]{2,1,0:T(8,128)} fusion(f32[2,256,256]{2,1,0:T(8,128)S(1)} %bitcast.40, s32[1024]{0:T(1024)S(1)} %pad_clamp_fusion.2), kind=kCustom, calls=%fused_computation.1 | custom fusion | bytes 6291504 | tf_op jit(solution)/shard_map/gather | solution.py:16
  24.5 0.6 compare_convert_fusion.1
  25.2 7.6 %fusion.24 = f32[12,256,256]{2,1,0:T(8,128)} fusion(f32[12,256,256]{2,1,0:T(8,128)} %gather_fusion, f32[12,256,256]{2,1,0:T(8,128)} %gather_fusion.1), kind=kOutput, calls=%fused_computation.41 | convolution fusion | flops 2415919104 | bytes 9437184 | tf_op jit(solution)/shard_map/pij,pjk->pik/dot_general | solution.py:17
  32.8 4.8 %collective-permute-done = f32[2,256,256]{2,1,0:T(8,128)S(1)} collective-permute-done((f32[2,256,256]{2,1,0:T(8,128)}, f32[2,256,256]{2,1,0:T(8,128)S(1)}, u32[]{:S(2)}, u32[]{:S(2)}) %collective-permute-start) | collective-permute-done | bytes 524320 | tf_op jit(solution)/shard_map/ppermute | solution.py:10
  37.6 2.4 %gather_fusion.2 = f32[12,256,256]{2,1,0:T(8,128)} fusion(f32[2,256,256]{2,1,0:T(8,128)S(1)} %collective-permute-done, s32[1024]{0:T(1024)S(1)} %pad_clamp_fusion.1), kind=kCustom, calls=%fused_computation.2 | custom fusion | bytes 6291504 | tf_op jit(solution)/shard_map/gather | solution.py:15
  40.0 0.0 collective-permute-done.1
  40.1 2.5 %gather_fusion.3 = f32[12,256,256]{2,1,0:T(8,128)} fusion(f32[2,256,256]{2,1,0:T(8,128)S(1)} %collective-permute-done.1, s32[1024]{0:T(1024)S(1)} %pad_clamp_fusion), kind=kCustom, calls=%fused_computation.3 | custom fusion | bytes 6291504 | tf_op jit(solution)/shard_map/gather | solution.py:16
  42.5 6.1 %fusion.25 = f32[12,256,256]{2,1,0:T(8,128)S(1)} fusion(f32[12,256,256]{2,1,0:T(8,128)} %gather_fusion.2, f32[12,256,256]{2,1,0:T(8,128)} %gather_fusion.3), kind=kOutput, calls=%fused_computation.42 | convolution fusion | flops 2415919104 | bytes 9437184 | tf_op jit(solution)/shard_map/pij,pjk->pik/dot_general | solution.py:17
  48.6 0.0 copy-start.1
  48.6 3.9 %fusion = f32[4,256,256]{2,0,1:T(4,128)S(1)} fusion(f32[12,256,256]{2,1,0:T(8,128)S(1)} %fusion.25, f32[12]{0:T(128)S(1)} %compare_convert_fusion, s32[12]{0:T(128)S(1)} %get-tuple-element.6), kind=kOutput, calls=%fused_computation.4 | convolution fusion | flops 37748832 | bytes 4194400 | tf_op jit(solution)/shard_map/pq,pik->qik/dot_general | solution.py:22
  52.5 0.0 copy-done.1
  52.6 4.2 %fusion.4 = f32[4,256,256]{2,0,1:T(4,128)S(1)} fusion(f32[4,256,256]{2,0,1:T(4,128)S(1)} %fusion, f32[12,256,256]{2,1,0:T(8,128)S(1)} %copy-done.1, f32[12]{0:T(128)S(1)} %compare_convert_fusion.1, s32[12]{0:T(128)S(1)} %get-tuple-element.5), kind=kOutput, calls=%fused_computation.8 | convolution fusion | flops 38010976 | bytes 5242976 | tf_op jit(solution)/shard_map/pq,pik->qik/dot_general | solution.py:22
  56.8 1.2 %copy.9 = f32[4,256,256]{2,1,0:T(8,128)} copy(f32[4,256,256]{2,0,1:T(4,128)S(1)} %fusion.4) | data formatting | bytes 2097152 | tf_op jit(solution)/shard_map/add | solution.py:45
  57.9 0.0 reduce-scatter.2.cloned.1.call-update
  58.6 40.5 %reduce-scatter.2.cloned.1.call-done = f32[1,256,256]{2,1,0:T(8,128)} async-done(((f32[4,256,256]{2,1,0:T(8,128)}), f32[1,256,256]{2,1,0:T(8,128)}) %reduce-scatter.2.cloned.1.call-update) | async-done | bytes 262160 | tf_op jit(solution)/shard_map/reduce_scatter | solution.py:46
  99.1 1.7 %multiply_bitcast_fusion = f32[1,1,1,256,256]{4,3,2,1,0:T(8,128)} fusion(f32[1,256,256]{2,1,0:T(8,128)} %reduce-scatter.2.cloned.1.call-done, f32[]{:T(128)} %bitcast.16), kind=kLoop, calls=%fused_computation.9 | loop fusion | flops 65536 | bytes 524292 | tf_op jit(solution)/shard_map/broadcast_in_dim | solution.py:48
  (4 shorter events, 0.0 us)
Async XLA Ops:
  6.5 92.5 %reduce-scatter.2.cloned.1.call-start = ((), (), s32[]{:S(2)}) async-start(), calls=%async_computation.1 | async-start | bytes 1310720 | tf_op jit(solution)/shard_map/reduce_scatter | solution.py:46
  6.5 31.1 %collective-permute-start = (f32[2,256,256]{2,1,0:T(8,128)}, f32[2,256,256]{2,1,0:T(8,128)S(1)}, u32[]{:S(2)}, u32[]{:S(2)}) collective-permute-start(f32[2,256,256]{2,1,0:T(8,128)} %bitcast.37), channel_id=1, source_target_pairs={{0,1},{1,2},{2,3},{3,4},{4,5},{5,6},{6,7},{7,8},{8,9},{9,10},{10,1... | collective-permute-start | bytes 1572872 | tf_op jit(solution)/shard_map/ppermute | solution.py:10
  10.9 29.1 %collective-permute-start.1 = (f32[2,256,256]{2,1,0:T(8,128)}, f32[2,256,256]{2,1,0:T(8,128)S(1)}, u32[]{:S(2)}, u32[]{:S(2)}) collective-permute-start(f32[2,256,256]{2,1,0:T(8,128)} %bitcast.39), channel_id=1, source_target_pairs={{0,32},{32,64},{64,96},{96,128},{128,160},{160,192},{192,224},{224... | collective-permute-start | bytes 1572872 | tf_op jit(solution)/shard_map/ppermute | solution.py:10
  18.5 3.6 %copy-start = (f32[1,1,1,2,256,256]{5,4,3,2,1,0:T(8,128)S(1)}, f32[1,1,1,2,256,256]{5,4,3,2,1,0:T(8,128)}, u32[]{:S(2)}) copy-start(f32[1,1,1,2,256,256]{5,4,3,2,1,0:T(8,128)} %param.8) | copy-start | bytes 1572868
  48.6 3.9 %copy-start.1 = (f32[12,256,256]{2,1,0:T(8,128)S(1)}, f32[12,256,256]{2,1,0:T(8,128)}, u32[]{:S(2)}) copy-start(f32[12,256,256]{2,1,0:T(8,128)} %fusion.24) | copy-start | bytes 9437188
Sparse Core Ops, SparseCore 0:
  58.1 40.9 reduce-scatter.1
where the time goes:
time: 108 us
  waiting for transfers between devices  45.3 us (42%)
  matrix products  21.9 us (20%)
  local copies, waits for them, and re-layouts  14.2 us (13%)
  between operations  14.1 us (13%)
  starting transfers between devices  7.57 us (7%)
  other arithmetic  4.55 us (4%)
    reduce_scatter x1, waiting for transfers between devices, local(): lax.psum_scatter(gathered, 'layer', scatter_dimension=0, tiled=True)  40.5 us
    dot_general x2, matrix products, step_terms(): jnp.einsum('pij,pjk->pik', left_pick, right_pick, precision=lax.Precision...  13.7 us
    dot_general x2, matrix products, step_terms(): jnp.einsum('pq,pik->qik', onehot, terms, precision=lax.Precision.HIGHEST)  8.16 us
    ppermute x2, starting transfers between devices, from_behind(): return lax.ppermute(value, axis, pairs)  7.57 us
    gather x2, local copies, waits for them, and re-layouts, step_terms(): left_pick = left_tile[left_sel]  5.98 us
    gather x2, local copies, waits for them, and re-layouts, step_terms(): right_pick = right_tile[right_sel]  4.92 us
    ppermute x2, waiting for transfers between devices, from_behind(): return lax.ppermute(value, axis, pairs)  4.78 us
  transfers between devices with their start and end apart: 3, of which 2 were waited for; matrix products, arithmetic and copies ran while one was open for 20% of the time, Pallas kernels for 0%

commit v1 on v0

v1 whole, which is shorter than its diff:
```python
import functools

import jax
import jax.numpy as jnp
from jax import lax
from jax.experimental import pallas as pl
from jax.experimental.pallas import tpu as pltpu
from jax.sharding import PartitionSpec as P

VMEM = pltpu.VMEM
SMEM = pltpu.SMEM


def count_pairs(step, layer, li, ri, ti, counts, table, where):
    for entry in range(16):
        table[where, entry] = 0.0
    live = counts[0, 0, 0, step]
    for p in range(li.shape[4]):
        spot = (ti[0, 0, 0, step, p] ^ layer) * 4 + li[0, 0, 0, step, p] * 2 + ri[0, 0, 0, step, p]
        table[where, spot] = table[where, spot] + jnp.where(p < live, 1.0, 0.0)


def halves(value):
    high = value.astype(jnp.bfloat16)
    return high, (value - high.astype(jnp.float32)).astype(jnp.bfloat16)


def pair_products(left, right):
    slots, rows, depth = left.shape
    high, low = halves(left[...].reshape(slots * rows, depth))
    found = []
    for slot in range(right.shape[0]):
        right_high, right_low = halves(right[slot])
        dot = functools.partial(jnp.dot, preferred_element_type=jnp.float32)
        found.append(dot(high, right_high) + (dot(high, right_low) + dot(low, right_high)))
    return found


def combine(found, table, where, j, rows):
    total = None
    for l in range(2):
        for r in range(2):
            term = found[r][l * rows : (l + 1) * rows] * table[where, j * 4 + l * 2 + r]
            total = term if total is None else total + term
    return total


def first_kernel(li, ri, ti, counts, left, right, part, table_out, table):
    layer = lax.axis_index("layer")
    count_pairs(0, layer, li, ri, ti, counts, table, 0)
    count_pairs(1, layer, li, ri, ti, counts, table_out, 0)
    found = pair_products(left, right)
    for j in range(4):
        part[j] = combine(found, table, 0, j, left.shape[1])


def second_kernel(table, left, right, part, *outs):
    found = pair_products(left, right)
    for j in (2, 3, 1, 0):
        outs[j][...] = part[j] + combine(found, table, 0, j, left.shape[1])


def permute(value, axis, to):
    n = lax.axis_size(axis)
    return lax.ppermute(value, axis, [(i, to(i, n)) for i in range(n)])


def local(left_blocks, right_blocks, left_index, right_index, target_index, live_counts, keep_mask):
    left = left_blocks[0, 0, 0]
    right = right_blocks[0, 0, 0]
    rows = left.shape[1]
    right_next = permute(right, "row", lambda i, n: (i + 1) % n)
    left_next = permute(left, "col", lambda i, n: (i + 1) % n)
    block = jax.ShapeDtypeStruct((rows, rows), jnp.float32)
    vmem = pl.BlockSpec(memory_space=VMEM)
    smem = pl.BlockSpec(memory_space=SMEM)
    part, table = pl.pallas_call(
        first_kernel,
        out_shape=(jax.ShapeDtypeStruct((4, rows, rows), jnp.float32), jax.ShapeDtypeStruct((1, 16), jnp.float32)),
        in_specs=[smem] * 4 + [vmem] * 2,
        out_specs=(vmem, smem),
        scratch_shapes=[pltpu.SMEM((1, 16), jnp.float32)],
        compiler_params=pltpu.CompilerParams(vmem_limit_bytes=24 << 20),
        cost_estimate=pl.CostEstimate(flops=6 << 26, bytes_accessed=2 << 20, transcendentals=0),
        name="first_step",
    )(left_index, right_index, target_index, live_counts, left, right)
    own, core, chip, far = pl.pallas_call(
        second_kernel,
        out_shape=(block,) * 4,
        in_specs=[smem] + [vmem] * 3,
        out_specs=(vmem,) * 4,
        compiler_params=pltpu.CompilerParams(vmem_limit_bytes=24 << 20),
        cost_estimate=pl.CostEstimate(flops=6 << 26, bytes_accessed=3 << 20, transcendentals=0),
        name="second_step",
    )(table, left_next, right_next, part)
    chip = permute(chip, "layer", lambda i, n: i ^ 2)
    far = permute(far, "layer", lambda i, n: i ^ 3)
    core = permute(core, "layer", lambda i, n: i ^ 1)
    summed = (own + core) + (chip + far)
    result = summed * keep_mask[0, 0].astype(jnp.float32)[:, None, None]
    return result[None, None]


def solution(mesh):
    return jax.shard_map(
        local,
        mesh=mesh,
        in_specs=(
            P("layer", "row", "col", None, None, None),
            P("layer", "row", "col", None, None, None),
            P("layer", "row", "col", None, None),
            P("layer", "row", "col", None, None),
            P("layer", "row", "col", None, None),
            P("layer", "row", "col", None),
            P("row", "col", "layer"),
        ),
        out_specs=P("row", "col", "layer", None, None),
        check_vma=False,
    )
```

time: 108 us -> 52.4 us (0.49)
  matrix products: 21.9 us -> 0 us
  waiting for transfers between devices: 45.3 us -> 29 us
  between operations: 14.1 us -> 0.77 us
  local copies, waits for them, and re-layouts: 14.2 us -> 2.09 us
  starting transfers between devices: 7.57 us -> 16.3 us
  other arithmetic: 4.55 us -> 0.77 us
  Pallas kernels: 0 us -> 3.14 us
    reduce_scatter x1 -> x0, waiting for transfers between devices: 40.5 us -> none  [local(): lax.psum_scatter(gathered, 'layer', scatter_dimension=0, tiled=True)]
    ppermute x2 -> x5, waiting for transfers between devices: 4.78 us -> 29 us  [permute(): return lax.ppermute(value, axis, [(i, to(i, n)) for i in range(n)])]
    dot_general x4 -> x0, matrix products: 21.9 us -> none  [the longest x2 13.7 us: step_terms(): jnp.einsum('pij,pjk->pik', left_pick, right_pick, precision=lax.Precision...]
    gather x4 -> x0, local copies, waits for them, and re-layouts: 10.9 us -> none  [the longest x2 5.98 us: step_terms(): left_pick = left_tile[left_sel]]
    ppermute x2 -> x5, starting transfers between devices: 7.57 us -> 16.3 us  [permute(): return lax.ppermute(value, axis, [(i, to(i, n)) for i in range(n)])]
    pallas_call x0 -> x2, Pallas kernels: none -> 3.14 us  [the longest x1 1.81 us: local(): pl.pallas_call(first_kernel, out_shape=(jax.ShapeDtypeStruct((4, rows, ro...]
    unnamed x4 -> x12, local copies, waits for them, and re-layouts: 0.01 us -> 2.09 us
    select_n x2 -> x0, other arithmetic: 1.52 us -> none  [the longest x1 0.76 us: step_terms(): right_pick = right_tile[right_sel]]
  transfers between devices with their start and end apart: 3 -> 5, of which waited for: 2 -> 3; matrix products, arithmetic and copies ran while one was open for 20% -> 0% of each run, Pallas kernels for 0% -> 3%
where the time goes in v1:
time: 52.4 us; the launch traced here: 52 us
  waiting for transfers between devices  29 us (55%)
  starting transfers between devices  16.3 us (31%)
  Pallas kernels  3.14 us (6%)
  local copies, waits for them, and re-layouts  2.09 us (4%)
  other arithmetic  0.77 us (1%)
  between operations  0.77 us (1%)
    ppermute x5, waiting for transfers between devices, permute(): return lax.ppermute(value, axis, [(i, to(i, n)) for i in range(n)])  29 us
    ppermute x5, starting transfers between devices, permute(): return lax.ppermute(value, axis, [(i, to(i, n)) for i in range(n)])  16.3 us
    unnamed x12, local copies, waits for them, and re-layouts  2.09 us
    pallas_call x1, Pallas kernels, local(): pl.pallas_call(first_kernel, out_shape=(jax.ShapeDtypeStruct((4, rows, ro...  1.81 us
    pallas_call x1, Pallas kernels, local(): pl.pallas_call(second_kernel, out_shape=(block,) * 4, in_specs=[smem] + [...  1.33 us
  transfers between devices with their start and end apart: 5, of which 3 were waited for; matrix products, arithmetic and copies ran while one was open for 0% of the time, Pallas kernels for 3%

profile of v1, /device:TPU:1, one launch (start us, length us, event | category | flops | bytes accessed | tf_op | source)
XLA Modules:
  0.0 52.0 jit_solution(156090921752388618)
XLA Ops:
  0.0 0.0 copy-start.3
  0.0 0.0 copy-start.4
  0.0 0.0 copy-start.2
  0.0 0.0 copy-start.5
  0.0 4.5 %collective-permute-start = (f32[2,256,256]{2,1,0:T(8,128)}, f32[2,256,256]{2,1,0:T(8,128)S(1)}, u32[]{:S(2)}, u32[]{:S(2)}) collective-permute-start(f32[2,256,256]{2,1,0:T(8,128)} %bitcast.5), channel_id=1, source_target_pairs={{0,1},{1,2},{2,3},{3,4},{4,5},{5,6},{6,7},{7,8},{8,9},{9,10},{10,1... | collective-permute-start | bytes 1572872 | tf_op jit(solution)/shard_map/ppermute | solution.py:65
  4.5 3.2 %collective-permute-start.1 = (f32[2,256,256]{2,1,0:T(8,128)}, f32[2,256,256]{2,1,0:T(8,128)S(1)}, u32[]{:S(2)}, u32[]{:S(2)}) collective-permute-start(f32[2,256,256]{2,1,0:T(8,128)} %bitcast.7), channel_id=1, source_target_pairs={{0,32},{32,64},{64,96},{96,128},{128,160},{160,192},{192,224},{224... | collective-permute-start | bytes 1572872 | tf_op jit(solution)/shard_map/ppermute | solution.py:65
  7.7 0.0 copy-done.3
  7.8 0.0 copy-done.4
  7.8 0.0 copy-done.2
  7.8 0.0 copy-done.5
  7.8 0.0 copy-start
  7.8 1.0 %copy-done = f32[1,1,1,2,256,256]{5,4,3,2,1,0:T(8,128)S(1)} copy-done((f32[1,1,1,2,256,256]{5,4,3,2,1,0:T(8,128)S(1)}, f32[1,1,1,2,256,256]{5,4,3,2,1,0:T(8,128)}, u32[]{:S(2)}) %copy-start) | copy-done | bytes 524312
  8.8 0.0 copy-start.1
  8.8 1.0 %copy-done.1 = f32[1,1,1,2,256,256]{5,4,3,2,1,0:T(8,128)S(1)} copy-done((f32[1,1,1,2,256,256]{5,4,3,2,1,0:T(8,128)S(1)}, f32[1,1,1,2,256,256]{5,4,3,2,1,0:T(8,128)}, u32[]{:S(2)}) %copy-start.1) | copy-done | bytes 524312
  9.9 1.8 %first_step.1 = (f32[4,256,256]{2,1,0:T(8,128)S(1)}, f32[1,16]{1,0:T(1,128)S(1)}) custom-call(s32[1,1,1,2,12]{4,3,2,1,0:T(2,128)S(1)} %copy-done.2, s32[1,1,1,2,12]{4,3,2,1,0:T(2,128)S(1)} %copy-done.3, s32[1,1,1,2,12]{4,3,2,1,0:T(2,128)S(1)} %copy-done.4, s32[1,1,1,2]{3,2,1,0:T(1,128)S(1)} %copy-done.5, f32[2,256,256]{2,1,0:T(8,128)S(1)} %bitcast.6, ...), custom_call_target="tpu_custom_call" | custom-call | flops 402653184 | bytes 2097152 | tf_op jit(solution)/shard_map/first_step/pallas_call | solution.py:77
  11.7 19.5 %collective-permute-done.left = f32[2,256,256]{2,1,0:T(8,128)S(1)} collective-permute-done((f32[2,256,256]{2,1,0:T(8,128)}, f32[2,256,256]{2,1,0:T(8,128)S(1)}, u32[]{:S(2)}, u32[]{:S(2)}) %collective-permute-start) | collective-permute-done | bytes 524320 | tf_op jit(solution)/shard_map/ppermute | solution.py:65
  31.2 0.0 collective-permute-done.1.right
  31.2 1.3 %second_step.1 = (f32[256,256]{1,0:T(8,128)S(1)}, f32[256,256]{1,0:T(8,128)S(1)}, f32[256,256]{1,0:T(8,128)S(1)}, f32[256,256]{1,0:T(8,128)S(1)}) custom-call(f32[1,16]{1,0:T(1,128)S(1)} %get-tuple-element.11.table, f32[2,256,256]{2,1,0:T(8,128)S(1)} %collective-permute-done.left, f32[2,256,256]{2,1,0:T(8,128)S(1)} %collective-permute-done.1.right, ...), custom_call_target="tpu_custom_call" | custom-call | flops 402653184 | bytes 3145728 | tf_op jit(solution)/shard_map/second_step/pallas_call | solution.py:87
  32.6 3.1 %collective-permute-start.2 = (f32[256,256]{1,0:T(8,128)S(1)}, f32[256,256]{1,0:T(8,128)S(1)}, u32[]{:S(2)}, u32[]{:S(2)}) collective-permute-start(f32[256,256]{1,0:T(8,128)S(1)} %get-tuple-element.14), channel_id=1, source_target_pairs={{0,256},{256,0},{512,768},{768,512},{1,257},{257,1},{513,769},{769... | collective-permute-start | bytes 786440 | tf_op jit(solution)/shard_map/ppermute | solution.py:65
  35.7 3.1 %collective-permute-start.3 = (f32[256,256]{1,0:T(8,128)S(1)}, f32[256,256]{1,0:T(8,128)S(1)}, u32[]{:S(2)}, u32[]{:S(2)}) collective-permute-start(f32[256,256]{1,0:T(8,128)S(1)} %get-tuple-element.15), channel_id=1, source_target_pairs={{0,512},{256,768},{512,0},{768,256},{1,513},{257,769},{513,1},{769... | collective-permute-start | bytes 786440 | tf_op jit(solution)/shard_map/ppermute | solution.py:65
  38.8 2.3 %collective-permute-start.4 = (f32[256,256]{1,0:T(8,128)S(1)}, f32[256,256]{1,0:T(8,128)S(1)}, u32[]{:S(2)}, u32[]{:S(2)}) collective-permute-start(f32[256,256]{1,0:T(8,128)S(1)} %get-tuple-element.16), channel_id=1, source_target_pairs={{0,768},{256,512},{512,256},{768,0},{1,769},{257,513},{513,257},{7... | collective-permute-start | bytes 786440 | tf_op jit(solution)/shard_map/ppermute | solution.py:65
  41.8 0.0 collective-permute-done.2
  41.9 3.7 %collective-permute-done.3 = f32[256,256]{1,0:T(8,128)S(1)} collective-permute-done((f32[256,256]{1,0:T(8,128)S(1)}, f32[256,256]{1,0:T(8,128)S(1)}, u32[]{:S(2)}, u32[]{:S(2)}) %collective-permute-start.3) | collective-permute-done | bytes 262176 | tf_op jit(solution)/shard_map/ppermute | solution.py:65
  45.5 5.7 %collective-permute-done.4 = f32[256,256]{1,0:T(8,128)S(1)} collective-permute-done((f32[256,256]{1,0:T(8,128)S(1)}, f32[256,256]{1,0:T(8,128)S(1)}, u32[]{:S(2)}, u32[]{:S(2)}) %collective-permute-start.4) | collective-permute-done | bytes 262176 | tf_op jit(solution)/shard_map/ppermute | solution.py:65
  51.3 0.8 %multiply_bitcast_fusion = f32[1,1,1,256,256]{4,3,2,1,0:T(8,128)} fusion(f32[256,256]{1,0:T(8,128)S(1)} %collective-permute-done.3, f32[256,256]{1,0:T(8,128)S(1)} %collective-permute-done.4, f32[256,256]{1,0:T(8,128)S(1)} %get-tuple-element.13, f32[256,256]{1,0:T(8,128)S(1)} %collective-permute-done.2, f32[]{:T(128)} %bitcast.2), kind=kLoop, calls=%fused_computation | loop fusion | flops 262144 | bytes 1310724 | tf_op jit(solution)/shard_map/broadcast_in_dim | solution.py:101
Async XLA Ops:
  0.0 7.7 %copy-start.3 = (s32[1,1,1,2,12]{4,3,2,1,0:T(2,128)S(1)}, s32[1,1,1,2,12]{4,3,2,1,0:T(2,128)}, u32[]{:S(2)}) copy-start(s32[1,1,1,2,12]{4,3,2,1,0:T(2,128)} %ri.1) | copy-start | bytes 292
  0.0 7.8 %copy-start.4 = (s32[1,1,1,2,12]{4,3,2,1,0:T(2,128)S(1)}, s32[1,1,1,2,12]{4,3,2,1,0:T(2,128)}, u32[]{:S(2)}) copy-start(s32[1,1,1,2,12]{4,3,2,1,0:T(2,128)} %ti.1) | copy-start | bytes 292
  0.0 7.8 %copy-start.2 = (s32[1,1,1,2,12]{4,3,2,1,0:T(2,128)S(1)}, s32[1,1,1,2,12]{4,3,2,1,0:T(2,128)}, u32[]{:S(2)}) copy-start(s32[1,1,1,2,12]{4,3,2,1,0:T(2,128)} %li.1) | copy-start | bytes 292
  0.0 7.8 %copy-start.5 = (s32[1,1,1,2]{3,2,1,0:T(1,128)S(1)}, s32[1,1,1,2]{3,2,1,0:T(1,128)}, u32[]{:S(2)}) copy-start(s32[1,1,1,2]{3,2,1,0:T(1,128)} %counts.1) | copy-start | bytes 28
  0.0 31.2 %collective-permute-start = (f32[2,256,256]{2,1,0:T(8,128)}, f32[2,256,256]{2,1,0:T(8,128)S(1)}, u32[]{:S(2)}, u32[]{:S(2)}) collective-permute-start(f32[2,256,256]{2,1,0:T(8,128)} %bitcast.5), channel_id=1, source_target_pairs={{0,1},{1,2},{2,3},{3,4},{4,5},{5,6},{6,7},{7,8},{8,9},{9,10},{10,1... | collective-permute-start | bytes 1572872 | tf_op jit(solution)/shard_map/ppermute | solution.py:65
  4.5 26.7 %collective-permute-start.1 = (f32[2,256,256]{2,1,0:T(8,128)}, f32[2,256,256]{2,1,0:T(8,128)S(1)}, u32[]{:S(2)}, u32[]{:S(2)}) collective-permute-start(f32[2,256,256]{2,1,0:T(8,128)} %bitcast.7), channel_id=1, source_target_pairs={{0,32},{32,64},{64,96},{96,128},{128,160},{160,192},{192,224},{224... | collective-permute-start | bytes 1572872 | tf_op jit(solution)/shard_map/ppermute | solution.py:65
  7.8 1.0 %copy-start = (f32[1,1,1,2,256,256]{5,4,3,2,1,0:T(8,128)S(1)}, f32[1,1,1,2,256,256]{5,4,3,2,1,0:T(8,128)}, u32[]{:S(2)}) copy-start(f32[1,1,1,2,256,256]{5,4,3,2,1,0:T(8,128)} %param.7) | copy-start | bytes 1572868
  8.8 1.0 %copy-start.1 = (f32[1,1,1,2,256,256]{5,4,3,2,1,0:T(8,128)S(1)}, f32[1,1,1,2,256,256]{5,4,3,2,1,0:T(8,128)}, u32[]{:S(2)}) copy-start(f32[1,1,1,2,256,256]{5,4,3,2,1,0:T(8,128)} %param.8) | copy-start | bytes 1572868
  32.6 9.3 %collective-permute-start.2 = (f32[256,256]{1,0:T(8,128)S(1)}, f32[256,256]{1,0:T(8,128)S(1)}, u32[]{:S(2)}, u32[]{:S(2)}) collective-permute-start(f32[256,256]{1,0:T(8,128)S(1)} %get-tuple-element.14), channel_id=1, source_target_pairs={{0,256},{256,0},{512,768},{768,512},{1,257},{257,1},{513,769},{769... | collective-permute-start | bytes 786440 | tf_op jit(solution)/shard_map/ppermute | solution.py:65
  35.7 9.8 %collective-permute-start.3 = (f32[256,256]{1,0:T(8,128)S(1)}, f32[256,256]{1,0:T(8,128)S(1)}, u32[]{:S(2)}, u32[]{:S(2)}) collective-permute-start(f32[256,256]{1,0:T(8,128)S(1)} %get-tuple-element.15), channel_id=1, source_target_pairs={{0,512},{256,768},{512,0},{768,256},{1,513},{257,769},{513,1},{769... | collective-permute-start | bytes 786440 | tf_op jit(solution)/shard_map/ppermute | solution.py:65
  38.8 12.4 %collective-permute-start.4 = (f32[256,256]{1,0:T(8,128)S(1)}, f32[256,256]{1,0:T(8,128)S(1)}, u32[]{:S(2)}, u32[]{:S(2)}) collective-permute-start(f32[256,256]{1,0:T(8,128)S(1)} %get-tuple-element.16), channel_id=1, source_target_pairs={{0,768},{256,512},{512,256},{768,0},{1,769},{257,513},{513,257},{7... | collective-permute-start | bytes 786440 | tf_op jit(solution)/shard_map/ppermute | solution.py:65

commit v2 on v1

v2 whole, which is shorter than its diff:
```python
import functools

import jax
import jax.numpy as jnp
from jax import lax
from jax.experimental import pallas as pl
from jax.experimental.pallas import tpu as pltpu
from jax.sharding import PartitionSpec as P

VMEM = pltpu.VMEM
SMEM = pltpu.SMEM
PARAMS = pltpu.CompilerParams(vmem_limit_bytes=24 << 20)
dot = functools.partial(jnp.dot, preferred_element_type=jnp.float32)


def count_pairs(step, layer, li, ri, ti, counts, table):
    for entry in range(16):
        table[0, entry] = 0.0
    live = counts[0, 0, 0, step]
    for p in range(li.shape[4]):
        spot = (ti[0, 0, 0, step, p] ^ layer) * 4 + li[0, 0, 0, step, p] * 2 + ri[0, 0, 0, step, p]
        table[0, spot] = table[0, spot] + jnp.where(p < live, 1.0, 0.0)


def halves(value):
    high = value.astype(jnp.bfloat16)
    return high, (value - high.astype(jnp.float32)).astype(jnp.bfloat16)


def pair_products(left, right_high, right_low, slots):
    count, rows, depth = left.shape
    high, low = halves(left.reshape(count * rows, depth))
    found = []
    for slot in slots:
        both = dot(high, right_high[slot]) + (dot(high, right_low[slot]) + dot(low, right_high[slot]))
        found.append([both[l * rows : (l + 1) * rows] for l in range(count)])
    return found


def combine(found, weight, j, total=None):
    for l in range(2):
        for r in range(2):
            term = found[r][l] * weight(j * 4 + l * 2 + r)
            total = term if total is None else total + term
    return total


def first_kernel(li, ri, ti, counts, left, right, keep, send, table, later):
    layer = lax.axis_index("layer")
    core = layer & 1
    count_pairs(0, layer, li, ri, ti, counts, table)
    count_pairs(1, layer, li, ri, ti, counts, later)
    half = left.shape[1] // 2
    width = send.shape[1]
    parts = [halves(right[slot]) for slot in range(2)]
    highs, lows = [part[0] for part in parts], [part[1] for part in parts]
    for out, side, flip in ((keep, core, 0), (send, 1 - core, 1)):
        begin = pl.multiple_of(side * half, half)
        found = pair_products(left[:, pl.ds(begin, half)], highs, lows, (0, 1))
        for j in range(4):
            spot = j ^ flip
            out[spot * half : (spot + 1) * half, :] = combine(found, lambda k: table[0, k], j)
            for k in range(4):
                row = 4 * half + spot * 4 + k
                out[row : row + 1, :] = jnp.full((1, width), later[0, j * 4 + k], jnp.float32)


def ready_kernel(right_own, right_mate, keep, heard, right_high, right_low, base, weights):
    for slot in range(4):
        right = (right_own if slot < 2 else right_mate)[slot % 2]
        right_high[slot], right_low[slot] = halves(right)
    size = base.shape[0]
    base[...] = keep[:size, :] + heard[:size, :]
    weights[:16] = keep[size:, :]
    weights[16:] = heard[size:, :]


def second_kernel(left_own, left_mate, right_high, right_low, base, weights, *outs):
    half = left_own.shape[1]
    own = pair_products(left_own[...], right_high, right_low, (0, 1))
    mate = pair_products(left_mate[...], right_high, right_low, (2, 3))
    for j in (2, 3, 1, 0):
        total = combine(own, lambda k: weights[k : k + 1, :], j, base[j * half : (j + 1) * half, :])
        outs[j][...] = combine(mate, lambda k: weights[16 + k : 17 + k, :], j, total)


def last_kernel(mask, chip, far, core, own, out, held, sems):
    side = lax.axis_index("layer") & 1
    scale = mask[0, 0, 0].astype(jnp.float32)
    half = own.shape[0]
    copies = []
    for other, (a, b) in enumerate(((own, chip), (core, far))):
        held[other * half : (other + 1) * half] = (a[...] + b[...]) * scale
        begin = pl.multiple_of((side if other == 0 else 1 - side) * half, half)
        copies.append(pltpu.make_async_copy(held.at[pl.ds(other * half, half)], out.at[pl.ds(begin, half)], sems.at[other]))
        copies[-1].start()
    for copy in copies:
        copy.wait()


def permute(value, to):
    names = ("layer", "row", "col")
    sizes = [lax.axis_size(name) for name in names]
    pairs = []
    for l in range(sizes[0]):
        for r in range(sizes[1]):
            for c in range(sizes[2]):
                ln, rn, cn = to(l, r, c)
                pairs.append(((l * sizes[1] + r) * sizes[2] + c, (ln * sizes[1] + rn % sizes[1]) * sizes[2] + cn % sizes[2]))
    return lax.ppermute(value, names, pairs)


def local(left_blocks, right_blocks, left_index, right_index, target_index, live_counts, keep_mask):
    left = left_blocks[0, 0, 0]
    right = right_blocks[0, 0, 0]
    slots, rows, cols = left.shape
    half = rows // 2
    f32 = jnp.float32
    core = lax.axis_index("layer") & 1
    vmem = pl.BlockSpec(memory_space=VMEM)
    smem = pl.BlockSpec(memory_space=SMEM)
    anywhere = pl.BlockSpec(memory_space=pl.ANY)

    def piece(side):
        return lax.dynamic_slice_in_dim(left, side * half, half, 1, allow_negative_indices=False)

    pieces = [piece(core), piece(1 - core)]
    left, right, *pieces = lax.optimization_barrier((left, right, *pieces))
    left_own = permute(pieces[0], lambda l, r, c: (l, r, c + 1))
    left_mate = permute(pieces[1], lambda l, r, c: (l ^ 1, r, c + 1))

    def middle(left, right):
        right_own = permute(right, lambda l, r, c: (l, r + 1, c))
        right_mate = permute(right_own, lambda l, r, c: (l ^ 1, r, c))
        keep, send = pl.pallas_call(
            first_kernel,
            out_shape=(jax.ShapeDtypeStruct((4 * half + 16, cols), f32),) * 2,
            in_specs=[smem] * 4 + [vmem] * 2,
            out_specs=(vmem, vmem),
            scratch_shapes=[pltpu.SMEM((1, 16), f32)] * 2,
            compiler_params=PARAMS,
            cost_estimate=pl.CostEstimate(flops=6 << 26, bytes_accessed=2 << 20, transcendentals=0),
            name="first_step",
        )(left_index, right_index, target_index, live_counts, left, right)
        heard = permute(send, lambda l, r, c: (l ^ 1, r, c))
        return pl.pallas_call(
            ready_kernel,
            out_shape=(
                jax.ShapeDtypeStruct((4, rows, cols), jnp.bfloat16),
                jax.ShapeDtypeStruct((4, rows, cols), jnp.bfloat16),
                jax.ShapeDtypeStruct((4 * half, cols), f32),
                jax.ShapeDtypeStruct((32, cols), f32),
            ),
            in_specs=[vmem] * 4,
            out_specs=(vmem,) * 4,
            compiler_params=PARAMS,
            cost_estimate=pl.CostEstimate(flops=1 << 20, bytes_accessed=4 << 20, transcendentals=0),
            name="ready",
        )(right_own, right_mate, keep, heard)

    shapes = jax.eval_shape(middle, left, right)
    within = live_counts[0, 0, 0, 0] <= left_index.shape[4]
    ready = lax.cond(within, middle, lambda *args: tuple(jnp.zeros(s.shape, s.dtype) for s in shapes), left, right)
    own, core_out, chip_out, far_out = pl.pallas_call(
        second_kernel,
        out_shape=(jax.ShapeDtypeStruct((half, cols), f32),) * 4,
        in_specs=[vmem] * 6,
        out_specs=(vmem,) * 4,
        compiler_params=PARAMS,
        cost_estimate=pl.CostEstimate(flops=6 << 26, bytes_accessed=3 << 20, transcendentals=0),
        name="second_step",
    )(left_own, left_mate, *ready)
    chip_in = permute(chip_out, lambda l, r, c: (l ^ 2, r, c))
    far_in = permute(far_out, lambda l, r, c: (l ^ 3, r, c))
    core_in = permute(core_out, lambda l, r, c: (l ^ 1, r, c))
    result = pl.pallas_call(
        last_kernel,
        out_shape=jax.ShapeDtypeStruct((rows, cols), f32),
        in_specs=[smem] + [vmem] * 4,
        out_specs=anywhere,
        scratch_shapes=[pltpu.VMEM((rows, cols), f32), pltpu.SemaphoreType.DMA((2,))],
        compiler_params=PARAMS,
        cost_estimate=pl.CostEstimate(flops=1 << 18, bytes_accessed=1 << 20, transcendentals=0),
        name="last_sum",
    )(keep_mask, chip_in, far_in, core_in, own)
    return result[None, None, None]


def solution(mesh):
    return jax.shard_map(
        local,
        mesh=mesh,
        in_specs=(
            P("layer", "row", "col", None, None, None),
            P("layer", "row", "col", None, None, None),
            P("layer", "row", "col", None, None),
            P("layer", "row", "col", None, None),
            P("layer", "row", "col", None, None),
            P("layer", "row", "col", None),
            P("row", "col", "layer"),
        ),
        out_specs=P("row", "col", "layer", None, None),
        check_vma=False,
    )
```

time: 52.4 us -> 50.6 us (0.966)
  waiting for transfers between devices: 29 us -> 3.02 us
  starting transfers between devices: 16.3 us -> 41 us
  other arithmetic: 0.77 us -> 0 us
    ppermute x5 -> x8, waiting for transfers between devices: 29 us -> 3.02 us  [permute(): return lax.ppermute(value, names, pairs)]
    ppermute x5 -> x8, starting transfers between devices: 16.3 us -> 41 us  [permute(): return lax.ppermute(value, names, pairs)]
    dynamic_slice x0 -> x1, local copies, waits for them, and re-layouts: none -> 1.15 us  [piece(): lax.dynamic_slice_in_dim(left, side * half, half, 1, allow_negative_indic...]
    unnamed x12, local copies, waits for them, and re-layouts: 2.09 us -> 1.3 us
    broadcast_in_dim x1 -> x0, other arithmetic: 0.77 us -> none  [local(): return result[None, None]]
    pallas_call x2 -> x4, Pallas kernels: 3.14 us -> 2.91 us  [the longest x1 1.28 us: middle(): pl.pallas_call(first_kernel, out_shape=(jax.ShapeDtypeStruct((4 * half +...]
  transfers between devices with their start and end apart: 5 -> 8, of which waited for: 3 -> 2; matrix products, arithmetic and copies ran while one was open for 0% -> 0% of each run, Pallas kernels for 3% -> 3%
where the time goes in v2:
time: 50.6 us; the launch traced here: 50.3 us
  starting transfers between devices  41 us (81%)
  waiting for transfers between devices  3.02 us (6%)
  Pallas kernels  2.91 us (6%)
  local copies, waits for them, and re-layouts  2.46 us (5%)
  between operations  0.83 us (2%)
    ppermute x8, starting transfers between devices, permute(): return lax.ppermute(value, names, pairs)  41 us
    ppermute x8, waiting for transfers between devices, permute(): return lax.ppermute(value, names, pairs)  3.02 us
    unnamed x12, local copies, waits for them, and re-layouts  1.3 us
    pallas_call x1, Pallas kernels, middle(): pl.pallas_call(first_kernel, out_shape=(jax.ShapeDtypeStruct((4 * half +...  1.28 us
    dynamic_slice x1, local copies, waits for them, and re-layouts, piece(): lax.dynamic_slice_in_dim(left, side * half, half, 1, allow_negative_indic...  1.15 us
  transfers between devices with their start and end apart: 8, of which 2 were waited for; matrix products, arithmetic and copies ran while one was open for 0% of the time, Pallas kernels for 3%

profile of v2, /device:TPU:1, one launch (start us, length us, event | category | flops | bytes accessed | tf_op | source)
XLA Modules:
  0.0 50.3 jit_solution(8776946382058468624)
XLA Ops:
  0.0 0.0 copy-start
  0.0 0.0 copy-start.1
  0.0 1.2 %dynamic-slice_bitcast_fusion = (f32[2,128,256]{2,1,0:T(8,128)S(1)}, f32[2,128,256]{2,1,0:T(8,128)S(1)}) fusion(f32[1,1,1,2,256,256]{5,4,3,2,1,0:T(8,128)} %param.9, s32[]{:T(128)S(6)} %mul.7, s32[]{:T(128)S(6)} %mul.6), kind=kLoop, calls=%fused_computation | loop fusion | bytes 1048584 | tf_op jit(solution)/shard_map/dynamic_slice | solution.py:125
  1.2 0.0 copy-start.3
  1.2 0.0 copy-start.4
  1.2 4.4 %collective-permute-start.3 = (f32[2,128,256]{2,1,0:T(8,128)S(1)}, f32[2,128,256]{2,1,0:T(8,128)S(1)}, u32[]{:S(2)}, u32[]{:S(2)}) collective-permute-start(f32[2,128,256]{2,1,0:T(8,128)S(1)} %get-tuple-element.37), channel_id=1, source_target_pairs={{0,1},{1,2},{2,3},{3,4},{4,5},{5,6},{6,7},{7,8},{8,9},{9,10},{10,1... | collective-permute-start | bytes 786440 | tf_op jit(solution)/shard_map/ppermute | solution.py:110
  5.6 4.4 %collective-permute-start.4 = (f32[2,128,256]{2,1,0:T(8,128)S(1)}, f32[2,128,256]{2,1,0:T(8,128)S(1)}, u32[]{:S(2)}, u32[]{:S(2)}) collective-permute-start(f32[2,128,256]{2,1,0:T(8,128)S(1)} %get-tuple-element.38), channel_id=1, source_target_pairs={{0,257},{1,258},{2,259},{3,260},{4,261},{5,262},{6,263},{7,264},{8... | collective-permute-start | bytes 786440 | tf_op jit(solution)/shard_map/ppermute | solution.py:110
  10.0 0.0 copy-start.5
  10.0 0.6 %copy-done.5 = s32[1,1,1,2]{3,2,1,0:T(1,128)S(1)} copy-done((s32[1,1,1,2]{3,2,1,0:T(1,128)S(1)}, s32[1,1,1,2]{3,2,1,0:T(1,128)}, u32[]{:S(2)}) %copy-start.5) | copy-done | bytes 32
  10.7 0.0 copy-start.2
  10.7 0.0 copy-done
  10.7 0.0 copy-done.1
  10.7 0.0 copy-done.3
  10.7 0.0 copy-done.4
  10.7 0.6 %copy-done.2 = s32[1,1,1,2,12]{4,3,2,1,0:T(2,128)S(1)} copy-done((s32[1,1,1,2,12]{4,3,2,1,0:T(2,128)S(1)}, s32[1,1,1,2,12]{4,3,2,1,0:T(2,128)}, u32[]{:S(2)}) %copy-start.2) | copy-done | bytes 120
  11.3 27.5 %conditional.1 = ((bf16[4,256,256]{2,1,0:T(8,128)(2,1)S(1)}, bf16[4,256,256]{2,1,0:T(8,128)(2,1)S(1)}, f32[512,256]{1,0:T(8,128)S(1)}, f32[32,256]{1,0:T(8,128)S(1)})) conditional(s32[]{:T(128)} %bitcast.4, () %tuple.14, (f32[2,256,256]{2,1,0:T(8,128)S(1)}, s32[1,1,1,2,12]{4,3,2,1,0:T(2,128)S(1)}, s32[1,1,1,2,12]{4,3,2,1,0:T(2,128)S(1)}, ...), branch_computations={%region_0.0_spmd, %region_1.0_spmd} | conditional | flops 403701760 | bytes 12648576 | solution.py:163
  11.3 3.2 %collective-permute-start = (f32[2,256,256]{2,1,0:T(8,128)S(1)}, f32[2,256,256]{2,1,0:T(8,128)S(1)}, u32[]{:S(2)}, u32[]{:S(2)}) collective-permute-start(f32[2,256,256]{2,1,0:T(8,128)S(1)} %get-tuple-element.17.right), channel_id=1, source_target_pairs={{0,32},{1,33},{2,34},{3,35},{4,36},{5,37},{6,38},{7,39},{8,40},{9,... | collective-permute-start | bytes 1572872 | tf_op jit(solution)/shard_map/cond/branch_1_fun/ppermute | solution.py:110
  14.5 1.3 %first_step.1 = (f32[528,256]{1,0:T(8,128)S(1)}, f32[528,256]{1,0:T(8,128)S(1)}) custom-call(s32[1,1,1,2,12]{4,3,2,1,0:T(2,128)S(1)} %get-tuple-element.52.li, s32[1,1,1,2,12]{4,3,2,1,0:T(2,128)S(1)} %get-tuple-element.53.ri, s32[1,1,1,2,12]{4,3,2,1,0:T(2,128)S(1)} %get-tuple-element.54.ti, s32[1,1,1,2]{3,2,1,0:T(1,128)S(1)} %get-tuple-element.21.counts, ...), custom_call_target="tpu_custom_call" | custom-call | flops 402653184 | bytes 2097152 | tf_op jit(solution)/shard_map/cond/branch_1_fun/first_step/pallas_call | solution.py:135
  15.8 9.9 %collective-permute-start.2 = (f32[528,256]{1,0:T(8,128)S(1)}, f32[528,256]{1,0:T(8,128)S(1)}, u32[]{:S(2)}, u32[]{:S(2)}) collective-permute-start(f32[528,256]{1,0:T(8,128)S(1)} %get-tuple-element.24), channel_id=1, source_target_pairs={{0,256},{1,257},{2,258},{3,259},{4,260},{5,261},{6,262},{7,263},{8... | collective-permute-start | bytes 1622024 | tf_op jit(solution)/shard_map/cond/branch_1_fun/ppermute | solution.py:110
  25.7 0.0 collective-permute-done.right_own
  25.7 11.4 %collective-permute-start.1 = (f32[2,256,256]{2,1,0:T(8,128)S(1)}, f32[2,256,256]{2,1,0:T(8,128)S(1)}, u32[]{:S(2)}, u32[]{:S(2)}) collective-permute-start(f32[2,256,256]{2,1,0:T(8,128)S(1)} %collective-permute-done.right_own), channel_id=1, source_target_pairs={{0,256},{1,257},{2,258},{3,259},{4,260},{5,261},{6,262},{7,263},{8... | collective-permute-start | bytes 1572872 | tf_op jit(solution)/shard_map/cond/branch_1_fun/ppermute | solution.py:110
  37.2 0.0 collective-permute-done.2.heard
  37.2 1.5 %collective-permute-done.1.right_mate = f32[2,256,256]{2,1,0:T(8,128)S(1)} collective-permute-done((f32[2,256,256]{2,1,0:T(8,128)S(1)}, f32[2,256,256]{2,1,0:T(8,128)S(1)}, u32[]{:S(2)}, u32[]{:S(2)}) %collective-permute-start.1) | collective-permute-done | bytes 524320 | tf_op jit(solution)/shard_map/cond/branch_1_fun/ppermute | solution.py:110
  38.7 0.2 ready.1
  38.9 0.0 collective-permute-done.3.left_own
  38.9 0.0 collective-permute-done.4.left_mate
  38.9 0.7 %second_step.1 = (f32[128,256]{1,0:T(8,128)S(1)}, f32[128,256]{1,0:T(8,128)S(1)}, f32[128,256]{1,0:T(8,128)S(1)}, f32[128,256]{1,0:T(8,128)S(1)}) custom-call(f32[2,128,256]{2,1,0:T(8,128)S(1)} %collective-permute-done.3.left_own, f32[2,128,256]{2,1,0:T(8,128)S(1)} %collective-permute-done.4.left_mate, ...), custom_call_target="tpu_custom_call" | custom-call | flops 402653184 | bytes 3145728 | tf_op jit(solution)/shard_map/second_step/pallas_call | solution.py:164
  39.6 1.9 %collective-permute-start.5 = (f32[128,256]{1,0:T(8,128)S(1)}, f32[128,256]{1,0:T(8,128)S(1)}, u32[]{:S(2)}, u32[]{:S(2)}) collective-permute-start(f32[128,256]{1,0:T(8,128)S(1)} %get-tuple-element.45), channel_id=1, source_target_pairs={{0,512},{1,513},{2,514},{3,515},{4,516},{5,517},{6,518},{7,519},{8... | collective-permute-start | bytes 393224 | tf_op jit(solution)/shard_map/ppermute | solution.py:110
  41.5 3.9 %collective-permute-start.6 = (f32[128,256]{1,0:T(8,128)S(1)}, f32[128,256]{1,0:T(8,128)S(1)}, u32[]{:S(2)}, u32[]{:S(2)}) collective-permute-start(f32[128,256]{1,0:T(8,128)S(1)} %get-tuple-element.46), channel_id=1, source_target_pairs={{0,768},{1,769},{2,770},{3,771},{4,772},{5,773},{6,774},{7,775},{8... | collective-permute-start | bytes 393224 | tf_op jit(solution)/shard_map/ppermute | solution.py:110
  45.4 1.9 %collective-permute-start.7 = (f32[128,256]{1,0:T(8,128)S(1)}, f32[128,256]{1,0:T(8,128)S(1)}, u32[]{:S(2)}, u32[]{:S(2)}) collective-permute-start(f32[128,256]{1,0:T(8,128)S(1)} %get-tuple-element.47), channel_id=1, source_target_pairs={{0,256},{1,257},{2,258},{3,259},{4,260},{5,261},{6,262},{7,263},{8... | collective-permute-start | bytes 393224 | tf_op jit(solution)/shard_map/ppermute | solution.py:110
  48.0 0.0 collective-permute-done.5.chip
  48.0 1.5 %collective-permute-done.6.far = f32[128,256]{1,0:T(8,128)S(1)} collective-permute-done((f32[128,256]{1,0:T(8,128)S(1)}, f32[128,256]{1,0:T(8,128)S(1)}, u32[]{:S(2)}, u32[]{:S(2)}) %collective-permute-start.6) | collective-permute-done | bytes 131104 | tf_op jit(solution)/shard_map/ppermute | solution.py:110
  49.5 0.0 collective-permute-done.7.core
  49.5 0.7 %last_sum.1 = f32[256,256]{1,0:T(8,128)} custom-call(s32[1,1,1]{2,1,0:T(1,128)S(6)} %copy.19.mask, f32[128,256]{1,0:T(8,128)S(1)} %collective-permute-done.5.chip, f32[128,256]{1,0:T(8,128)S(1)} %collective-permute-done.6.far, f32[128,256]{1,0:T(8,128)S(1)} %collective-permute-done.7.core, f32[128,256]{1,0:T(8,128)S(1)} %get-tuple-element.48.own), custom_call_target="tpu_custom_call" | custom-call | flops 262144 | bytes 1048576 | tf_op jit(solution)/shard_map/last_sum/pallas_call | solution.py:176
Async XLA Ops:
  0.0 10.7 %copy-start = (f32[1,1,1,2,256,256]{5,4,3,2,1,0:T(8,128)S(1)}, f32[1,1,1,2,256,256]{5,4,3,2,1,0:T(8,128)}, u32[]{:S(2)}) copy-start(f32[1,1,1,2,256,256]{5,4,3,2,1,0:T(8,128)} %param.9) | copy-start | bytes 1572868
  0.0 10.7 %copy-start.1 = (f32[1,1,1,2,256,256]{5,4,3,2,1,0:T(8,128)S(1)}, f32[1,1,1,2,256,256]{5,4,3,2,1,0:T(8,128)}, u32[]{:S(2)}) copy-start(f32[1,1,1,2,256,256]{5,4,3,2,1,0:T(8,128)} %param.10) | copy-start | bytes 1572868
  1.2 9.5 %copy-start.3 = (s32[1,1,1,2,12]{4,3,2,1,0:T(2,128)S(1)}, s32[1,1,1,2,12]{4,3,2,1,0:T(2,128)}, u32[]{:S(2)}) copy-start(s32[1,1,1,2,12]{4,3,2,1,0:T(2,128)} %param.12) | copy-start | bytes 292
  1.2 9.5 %copy-start.4 = (s32[1,1,1,2,12]{4,3,2,1,0:T(2,128)S(1)}, s32[1,1,1,2,12]{4,3,2,1,0:T(2,128)}, u32[]{:S(2)}) copy-start(s32[1,1,1,2,12]{4,3,2,1,0:T(2,128)} %param.13) | copy-start | bytes 292
  1.2 37.7 %collective-permute-start.3 = (f32[2,128,256]{2,1,0:T(8,128)S(1)}, f32[2,128,256]{2,1,0:T(8,128)S(1)}, u32[]{:S(2)}, u32[]{:S(2)}) collective-permute-start(f32[2,128,256]{2,1,0:T(8,128)S(1)} %get-tuple-element.37), channel_id=1, source_target_pairs={{0,1},{1,2},{2,3},{3,4},{4,5},{5,6},{6,7},{7,8},{8,9},{9,10},{10,1... | collective-permute-start | bytes 786440 | tf_op jit(solution)/shard_map/ppermute | solution.py:110
  5.6 33.3 %collective-permute-start.4 = (f32[2,128,256]{2,1,0:T(8,128)S(1)}, f32[2,128,256]{2,1,0:T(8,128)S(1)}, u32[]{:S(2)}, u32[]{:S(2)}) collective-permute-start(f32[2,128,256]{2,1,0:T(8,128)S(1)} %get-tuple-element.38), channel_id=1, source_target_pairs={{0,257},{1,258},{2,259},{3,260},{4,261},{5,262},{6,263},{7,264},{8... | collective-permute-start | bytes 786440 | tf_op jit(solution)/shard_map/ppermute | solution.py:110
  10.0 0.7 %copy-start.5 = (s32[1,1,1,2]{3,2,1,0:T(1,128)S(1)}, s32[1,1,1,2]{3,2,1,0:T(1,128)}, u32[]{:S(2)}) copy-start(s32[1,1,1,2]{3,2,1,0:T(1,128)} %param.14) | copy-start | bytes 28
  10.7 0.7 %copy-start.2 = (s32[1,1,1,2,12]{4,3,2,1,0:T(2,128)S(1)}, s32[1,1,1,2,12]{4,3,2,1,0:T(2,128)}, u32[]{:S(2)}) copy-start(s32[1,1,1,2,12]{4,3,2,1,0:T(2,128)} %param.11) | copy-start | bytes 292
  11.3 14.4 %collective-permute-start = (f32[2,256,256]{2,1,0:T(8,128)S(1)}, f32[2,256,256]{2,1,0:T(8,128)S(1)}, u32[]{:S(2)}, u32[]{:S(2)}) collective-permute-start(f32[2,256,256]{2,1,0:T(8,128)S(1)} %get-tuple-element.17.right), channel_id=1, source_target_pairs={{0,32},{1,33},{2,34},{3,35},{4,36},{5,37},{6,38},{7,39},{8,40},{9,... | collective-permute-start | bytes 1572872 | tf_op jit(solution)/shard_map/cond/branch_1_fun/ppermute | solution.py:110
  15.8 21.3 %collective-permute-start.2 = (f32[528,256]{1,0:T(8,128)S(1)}, f32[528,256]{1,0:T(8,128)S(1)}, u32[]{:S(2)}, u32[]{:S(2)}) collective-permute-start(f32[528,256]{1,0:T(8,128)S(1)} %get-tuple-element.24), channel_id=1, source_target_pairs={{0,256},{1,257},{2,258},{3,259},{4,260},{5,261},{6,262},{7,263},{8... | collective-permute-start | bytes 1622024 | tf_op jit(solution)/shard_map/cond/branch_1_fun/ppermute | solution.py:110
  25.7 13.0 %collective-permute-start.1 = (f32[2,256,256]{2,1,0:T(8,128)S(1)}, f32[2,256,256]{2,1,0:T(8,128)S(1)}, u32[]{:S(2)}, u32[]{:S(2)}) collective-permute-start(f32[2,256,256]{2,1,0:T(8,128)S(1)} %collective-permute-done.right_own), channel_id=1, source_target_pairs={{0,256},{1,257},{2,258},{3,259},{4,260},{5,261},{6,262},{7,263},{8... | collective-permute-start | bytes 1572872 | tf_op jit(solution)/shard_map/cond/branch_1_fun/ppermute | solution.py:110
  39.6 8.4 %collective-permute-start.5 = (f32[128,256]{1,0:T(8,128)S(1)}, f32[128,256]{1,0:T(8,128)S(1)}, u32[]{:S(2)}, u32[]{:S(2)}) collective-permute-start(f32[128,256]{1,0:T(8,128)S(1)} %get-tuple-element.45), channel_id=1, source_target_pairs={{0,512},{1,513},{2,514},{3,515},{4,516},{5,517},{6,518},{7,519},{8... | collective-permute-start | bytes 393224 | tf_op jit(solution)/shard_map/ppermute | solution.py:110
  41.5 8.0 %collective-permute-start.6 = (f32[128,256]{1,0:T(8,128)S(1)}, f32[128,256]{1,0:T(8,128)S(1)}, u32[]{:S(2)}, u32[]{:S(2)}) collective-permute-start(f32[128,256]{1,0:T(8,128)S(1)} %get-tuple-element.46), channel_id=1, source_target_pairs={{0,768},{1,769},{2,770},{3,771},{4,772},{5,773},{6,774},{7,775},{8... | collective-permute-start | bytes 393224 | tf_op jit(solution)/shard_map/ppermute | solution.py:110
  45.4 4.1 %collective-permute-start.7 = (f32[128,256]{1,0:T(8,128)S(1)}, f32[128,256]{1,0:T(8,128)S(1)}, u32[]{:S(2)}, u32[]{:S(2)}) collective-permute-start(f32[128,256]{1,0:T(8,128)S(1)} %get-tuple-element.47), channel_id=1, source_target_pairs={{0,256},{1,257},{2,258},{3,259},{4,260},{5,261},{6,262},{7,263},{8... | collective-permute-start | bytes 393224 | tf_op jit(solution)/shard_map/ppermute | solution.py:110

commit v3 on v2

--- a/solution.py
+++ b/solution.py
@@ -65,14 +65,17 @@
                 out[row : row + 1, :] = jnp.full((1, width), later[0, j * 4 + k], jnp.float32)
 
 
-def ready_kernel(right_own, right_mate, keep, heard, right_high, right_low, base, weights):
-    for slot in range(4):
-        right = (right_own if slot < 2 else right_mate)[slot % 2]
-        right_high[slot], right_low[slot] = halves(right)
+def join_kernel(keep, heard, base, weights):
     size = base.shape[0]
     base[...] = keep[:size, :] + heard[:size, :]
     weights[:16] = keep[size:, :]
     weights[16:] = heard[size:, :]
+
+
+def ready_kernel(right_own, right_mate, right_high, right_low):
+    for slot in range(4):
+        right = (right_own if slot < 2 else right_mate)[slot % 2]
+        right_high[slot], right_low[slot] = halves(right)
 
 
 def second_kernel(left_own, left_mate, right_high, right_low, base, weights, *outs):
@@ -124,14 +127,10 @@
     def piece(side):
         return lax.dynamic_slice_in_dim(left, side * half, half, 1, allow_negative_indices=False)
 
-    pieces = [piece(core), piece(1 - core)]
-    left, right, *pieces = lax.optimization_barrier((left, right, *pieces))
-    left_own = permute(pieces[0], lambda l, r, c: (l, r, c + 1))
-    left_mate = permute(pieces[1], lambda l, r, c: (l ^ 1, r, c + 1))
-
-    def middle(left, right):
-        right_own = permute(right, lambda l, r, c: (l, r + 1, c))
-        right_mate = permute(right_own, lambda l, r, c: (l ^ 1, r, c))
+    right_own = permute(right, lambda l, r, c: (l, r + 1, c))
+    left_own = permute(piece(core), lambda l, r, c: (l, r, c + 1))
+    left_mate = permute(piece(1 - core), lambda l, r, c: (l ^ 1, r, c + 1))
+    def beside(left, right):
         keep, send = pl.pallas_call(
             first_kernel,
             out_shape=(jax.ShapeDtypeStruct((4 * half + 16, cols), f32),) * 2,
@@ -144,23 +143,35 @@
         )(left_index, right_index, target_index, live_counts, left, right)
         heard = permute(send, lambda l, r, c: (l ^ 1, r, c))
         return pl.pallas_call(
+            join_kernel,
+            out_shape=(jax.ShapeDtypeStruct((4 * half, cols), f32), jax.ShapeDtypeStruct((32, cols), f32)),
+            in_specs=[vmem] * 2,
+            out_specs=(vmem,) * 2,
+            compiler_params=PARAMS,
+            cost_estimate=pl.CostEstimate(flops=1 << 17, bytes_accessed=3 << 19, transcendentals=0),
+            name="join",
+        )(keep, heard)
+
+    def middle(right_own):
+        right_mate = permute(right_own, lambda l, r, c: (l ^ 1, r, c))
+        return pl.pallas_call(
             ready_kernel,
-            out_shape=(
-                jax.ShapeDtypeStruct((4, rows, cols), jnp.bfloat16),
-                jax.ShapeDtypeStruct((4, rows, cols), jnp.bfloat16),
-                jax.ShapeDtypeStruct((4 * half, cols), f32),
-                jax.ShapeDtypeStruct((32, cols), f32),
-            ),
-            in_specs=[vmem] * 4,
-            out_specs=(vmem,) * 4,
+            out_shape=(jax.ShapeDtypeStruct((4, rows, cols), jnp.bfloat16),) * 2,
+            in_specs=[vmem] * 2,
+            out_specs=(vmem,) * 2,
             compiler_params=PARAMS,
-            cost_estimate=pl.CostEstimate(flops=1 << 20, bytes_accessed=4 << 20, transcendentals=0),
+            cost_estimate=pl.CostEstimate(flops=1 << 20, bytes_accessed=2 << 20, transcendentals=0),
             name="ready",
-        )(right_own, right_mate, keep, heard)
-
-    shapes = jax.eval_shape(middle, left, right)
+        )(right_own, right_mate)
+
     within = live_counts[0, 0, 0, 0] <= left_index.shape[4]
-    ready = lax.cond(within, middle, lambda *args: tuple(jnp.zeros(s.shape, s.dtype) for s in shapes), left, right)
+
+    def guarded(branch, *args):
+        shapes = jax.eval_shape(branch, *args)
+        return lax.cond(within, branch, lambda *_: tuple(jnp.zeros(s.shape, s.dtype) for s in shapes), *args)
+
+    base, weights = guarded(beside, left, right)
+    right_high, right_low = guarded(middle, right_own)
     own, core_out, chip_out, far_out = pl.pallas_call(
         second_kernel,
         out_shape=(jax.ShapeDtypeStruct((half, cols), f32),) * 4,
@@ -169,7 +180,7 @@
         compiler_params=PARAMS,
         cost_estimate=pl.CostEstimate(flops=6 << 26, bytes_accessed=3 << 20, transcendentals=0),
         name="second_step",
-    )(left_own, left_mate, *ready)
+    )(left_own, left_mate, right_high, right_low, base, weights)
     chip_in = permute(chip_out, lambda l, r, c: (l ^ 2, r, c))
     far_in = permute(far_out, lambda l, r, c: (l ^ 3, r, c))
     core_in = permute(core_out, lambda l, r, c: (l ^ 1, r, c))

time: 50.6 us -> 48 us (0.949)
  starting transfers between devices: 41 us -> 33 us
  waiting for transfers between devices: 3.02 us -> 7.9 us
    ppermute x8, starting transfers between devices: 41 us -> 33 us  [permute(): return lax.ppermute(value, names, pairs)]
    ppermute x8, waiting for transfers between devices: 3.02 us -> 7.9 us  [permute(): return lax.ppermute(value, names, pairs)]
    pallas_call x1 -> x2, Pallas kernels: 1.28 us -> 1.34 us  [the longest x1 1.28 us: beside(): pl.pallas_call(first_kernel, out_shape=(jax.ShapeDtypeStruct((4 * half +...]
  transfers between devices with their start and end apart: 8 -> 8, of which waited for: 2 -> 4; matrix products, arithmetic and copies ran while one was open for 0% -> 2% of each run, Pallas kernels for 3% -> 3%
where the time goes in v3:
time: 48 us; the launch traced here: 47.2 us
  starting transfers between devices  33 us (69%)
  waiting for transfers between devices  7.9 us (16%)
  Pallas kernels  2.9 us (6%)
  local copies, waits for them, and re-layouts  2.46 us (5%)
  between operations  0.87 us (2%)
    ppermute x8, starting transfers between devices, permute(): return lax.ppermute(value, names, pairs)  33 us
    ppermute x8, waiting for transfers between devices, permute(): return lax.ppermute(value, names, pairs)  7.9 us
    unnamed x12, local copies, waits for them, and re-layouts  1.31 us
    pallas_call x1, Pallas kernels, beside(): pl.pallas_call(first_kernel, out_shape=(jax.ShapeDtypeStruct((4 * half +...  1.28 us
    dynamic_slice x1, local copies, waits for them, and re-layouts, piece(): lax.dynamic_slice_in_dim(left, side * half, half, 1, allow_negative_indic...  1.16 us
  transfers between devices with their start and end apart: 8, of which 4 were waited for; matrix products, arithmetic and copies ran while one was open for 2% of the time, Pallas kernels for 3%

profile of v3, /device:TPU:1, one launch (start us, length us, event | category | flops | bytes accessed | tf_op | source)
XLA Modules:
  0.0 47.2 jit_solution(4532457733026291172)
XLA Ops:
  0.0 4.0 %collective-permute-start.4 = (f32[2,256,256]{2,1,0:T(8,128)}, f32[2,256,256]{2,1,0:T(8,128)S(1)}, u32[]{:S(2)}, u32[]{:S(2)}) collective-permute-start(f32[2,256,256]{2,1,0:T(8,128)} %bitcast.10), channel_id=1, source_target_pairs={{0,32},{1,33},{2,34},{3,35},{4,36},{5,37},{6,38},{7,39},{8,40},{9,... | collective-permute-start | bytes 1572872 | tf_op jit(solution)/shard_map/ppermute | solution.py:113
  4.0 0.0 copy-start
  4.0 0.0 copy-start.1
  4.1 1.2 %dynamic-slice_bitcast_fusion = (f32[2,128,256]{2,1,0:T(8,128)S(1)}, f32[2,128,256]{2,1,0:T(8,128)S(1)}) fusion(f32[1,1,1,2,256,256]{5,4,3,2,1,0:T(8,128)} %param.11, s32[]{:T(128)S(6)} %mul.7, s32[]{:T(128)S(6)} %mul.6), kind=kLoop, calls=%fused_computation | loop fusion | bytes 1048584 | tf_op jit(solution)/shard_map/dynamic_slice | solution.py:128
  5.2 3.5 %collective-permute-start.2 = (f32[2,128,256]{2,1,0:T(8,128)S(1)}, f32[2,128,256]{2,1,0:T(8,128)S(1)}, u32[]{:S(2)}, u32[]{:S(2)}) collective-permute-start(f32[2,128,256]{2,1,0:T(8,128)S(1)} %get-tuple-element.50), channel_id=1, source_target_pairs={{0,1},{1,2},{2,3},{3,4},{4,5},{5,6},{6,7},{7,8},{8,9},{9,10},{10,1... | collective-permute-start | bytes 786440 | tf_op jit(solution)/shard_map/ppermute | solution.py:113
  8.8 0.0 copy-start.3
  8.8 0.0 copy-start.4
  8.8 4.7 %collective-permute-start.3 = (f32[2,128,256]{2,1,0:T(8,128)S(1)}, f32[2,128,256]{2,1,0:T(8,128)S(1)}, u32[]{:S(2)}, u32[]{:S(2)}) collective-permute-start(f32[2,128,256]{2,1,0:T(8,128)S(1)} %get-tuple-element.49), channel_id=1, source_target_pairs={{0,257},{1,258},{2,259},{3,260},{4,261},{5,262},{6,263},{7,264},{8... | collective-permute-start | bytes 786440 | tf_op jit(solution)/shard_map/ppermute | solution.py:113
  13.5 0.0 copy-start.5
  13.5 0.6 %copy-done.5 = s32[1,1,1,2]{3,2,1,0:T(1,128)S(1)} copy-done((s32[1,1,1,2]{3,2,1,0:T(1,128)S(1)}, s32[1,1,1,2]{3,2,1,0:T(1,128)}, u32[]{:S(2)}) %copy-start.5) | copy-done | bytes 32
  14.2 0.0 copy-start.2
  14.2 0.0 copy-done
  14.2 0.0 copy-done.1
  14.2 0.0 copy-done.3
  14.2 0.0 copy-done.4
  14.2 0.6 %copy-done.2 = s32[1,1,1,2,12]{4,3,2,1,0:T(2,128)S(1)} copy-done((s32[1,1,1,2,12]{4,3,2,1,0:T(2,128)S(1)}, s32[1,1,1,2,12]{4,3,2,1,0:T(2,128)}, u32[]{:S(2)}) %copy-start.2) | copy-done | bytes 120
  14.9 12.5 %conditional.3 = ((f32[512,256]{1,0:T(8,128)S(1)}, f32[32,256]{1,0:T(8,128)S(1)})) conditional(s32[]{:T(128)} %bitcast.3, () %tuple.20, (s32[1,1,1,2,12]{4,3,2,1,0:T(2,128)S(1)}, s32[1,1,1,2,12]{4,3,2,1,0:T(2,128)S(1)}, s32[1,1,1,2,12]{4,3,2,1,0:T(2,128)S(1)}, s32[1,1,1,2]{3,2,1,0:T(1,128)S(1)}, f32[1,1,1,2,256,256]{5,4,3,2,1,0:T(8,128)S(1)}, ...), branch_computations={%region_2.0_spmd, %region_3.0_spmd} | conditional | flops 402784256 | bytes 5832752 | solution.py:171
  14.9 1.3 %first_step.1 = (f32[528,256]{1,0:T(8,128)S(1)}, f32[528,256]{1,0:T(8,128)S(1)}) custom-call(s32[1,1,1,2,12]{4,3,2,1,0:T(2,128)S(1)} %get-tuple-element.46.li, s32[1,1,1,2,12]{4,3,2,1,0:T(2,128)S(1)} %get-tuple-element.47.ri, s32[1,1,1,2,12]{4,3,2,1,0:T(2,128)S(1)} %get-tuple-element.48.ti, s32[1,1,1,2]{3,2,1,0:T(1,128)S(1)} %get-tuple-element.21.counts, ...), custom_call_target="tpu_custom_call" | custom-call | flops 402653184 | bytes 2097152 | tf_op jit(solution)/shard_map/cond/branch_1_fun/first_step/pallas_call | solution.py:134
  16.1 9.6 %collective-permute-start.1 = (f32[528,256]{1,0:T(8,128)S(1)}, f32[528,256]{1,0:T(8,128)S(1)}, u32[]{:S(2)}, u32[]{:S(2)}) collective-permute-start(f32[528,256]{1,0:T(8,128)S(1)} %get-tuple-element.25), channel_id=1, source_target_pairs={{0,256},{1,257},{2,258},{3,259},{4,260},{5,261},{6,262},{7,263},{8... | collective-permute-start | bytes 1622024 | tf_op jit(solution)/shard_map/cond/branch_1_fun/ppermute | solution.py:113
  25.7 1.5 %collective-permute-done.1.heard = f32[528,256]{1,0:T(8,128)S(1)} collective-permute-done((f32[528,256]{1,0:T(8,128)S(1)}, f32[528,256]{1,0:T(8,128)S(1)}, u32[]{:S(2)}, u32[]{:S(2)}) %collective-permute-start.1) | collective-permute-done | bytes 540704 | tf_op jit(solution)/shard_map/cond/branch_1_fun/ppermute | solution.py:113
  27.3 0.1 join.1
  27.3 0.0 collective-permute-done.4
  27.3 5.3 %conditional.2 = ((bf16[4,256,256]{2,1,0:T(8,128)(2,1)S(1)}, bf16[4,256,256]{2,1,0:T(8,128)(2,1)S(1)})) conditional(s32[]{:T(128)} %bitcast.3, () %tuple.19, f32[2,256,256]{2,1,0:T(8,128)S(1)} %collective-permute-done.4), branch_computations={%region_0.0_spmd, %region_1.0_spmd} | conditional | flops 1048576 | bytes 4194352 | solution.py:171
  27.4 3.6 %collective-permute-start = (f32[2,256,256]{2,1,0:T(8,128)S(1)}, f32[2,256,256]{2,1,0:T(8,128)S(1)}, u32[]{:S(2)}, u32[]{:S(2)}) collective-permute-start(f32[2,256,256]{2,1,0:T(8,128)S(1)} %right_own), channel_id=1, source_target_pairs={{0,256},{1,257},{2,258},{3,259},{4,260},{5,261},{6,262},{7,263},{8... | collective-permute-start | bytes 1572872 | tf_op jit(solution)/shard_map/cond/branch_1_fun/ppermute | solution.py:113
  30.9 1.5 %collective-permute-done.right_mate = f32[2,256,256]{2,1,0:T(8,128)S(1)} collective-permute-done((f32[2,256,256]{2,1,0:T(8,128)S(1)}, f32[2,256,256]{2,1,0:T(8,128)S(1)}, u32[]{:S(2)}, u32[]{:S(2)}) %collective-permute-start) | collective-permute-done | bytes 524320 | tf_op jit(solution)/shard_map/cond/branch_1_fun/ppermute | solution.py:113
  32.5 0.2 ready.1
  32.6 0.0 collective-permute-done.2.left_own
  32.6 3.2 %collective-permute-done.3.left_mate = f32[2,128,256]{2,1,0:T(8,128)S(1)} collective-permute-done((f32[2,128,256]{2,1,0:T(8,128)S(1)}, f32[2,128,256]{2,1,0:T(8,128)S(1)}, u32[]{:S(2)}, u32[]{:S(2)}) %collective-permute-start.3) | collective-permute-done | bytes 262176 | tf_op jit(solution)/shard_map/ppermute | solution.py:113
  35.8 0.7 %second_step.1 = (f32[128,256]{1,0:T(8,128)S(1)}, f32[128,256]{1,0:T(8,128)S(1)}, f32[128,256]{1,0:T(8,128)S(1)}, f32[128,256]{1,0:T(8,128)S(1)}) custom-call(f32[2,128,256]{2,1,0:T(8,128)S(1)} %collective-permute-done.2.left_own, f32[2,128,256]{2,1,0:T(8,128)S(1)} %collective-permute-done.3.left_mate, ...), custom_call_target="tpu_custom_call" | custom-call | flops 402653184 | bytes 3145728 | tf_op jit(solution)/shard_map/second_step/pallas_call | solution.py:175
  36.5 3.1 %collective-permute-start.5 = (f32[128,256]{1,0:T(8,128)S(1)}, f32[128,256]{1,0:T(8,128)S(1)}, u32[]{:S(2)}, u32[]{:S(2)}) collective-permute-start(f32[128,256]{1,0:T(8,128)S(1)} %get-tuple-element.38), channel_id=1, source_target_pairs={{0,512},{1,513},{2,514},{3,515},{4,516},{5,517},{6,518},{7,519},{8... | collective-permute-start | bytes 393224 | tf_op jit(solution)/shard_map/ppermute | solution.py:113
  39.6 1.9 %collective-permute-start.6 = (f32[128,256]{1,0:T(8,128)S(1)}, f32[128,256]{1,0:T(8,128)S(1)}, u32[]{:S(2)}, u32[]{:S(2)}) collective-permute-start(f32[128,256]{1,0:T(8,128)S(1)} %get-tuple-element.39), channel_id=1, source_target_pairs={{0,768},{1,769},{2,770},{3,771},{4,772},{5,773},{6,774},{7,775},{8... | collective-permute-start | bytes 393224 | tf_op jit(solution)/shard_map/ppermute | solution.py:113
  41.5 2.5 %collective-permute-start.7 = (f32[128,256]{1,0:T(8,128)S(1)}, f32[128,256]{1,0:T(8,128)S(1)}, u32[]{:S(2)}, u32[]{:S(2)}) collective-permute-start(f32[128,256]{1,0:T(8,128)S(1)} %get-tuple-element.40), channel_id=1, source_target_pairs={{0,256},{1,257},{2,258},{3,259},{4,260},{5,261},{6,262},{7,263},{8... | collective-permute-start | bytes 393224 | tf_op jit(solution)/shard_map/ppermute | solution.py:113
  44.7 0.0 collective-permute-done.5.chip
  44.7 1.7 %collective-permute-done.6.far = f32[128,256]{1,0:T(8,128)S(1)} collective-permute-done((f32[128,256]{1,0:T(8,128)S(1)}, f32[128,256]{1,0:T(8,128)S(1)}, u32[]{:S(2)}, u32[]{:S(2)}) %collective-permute-start.6) | collective-permute-done | bytes 131104 | tf_op jit(solution)/shard_map/ppermute | solution.py:113
  46.4 0.0 collective-permute-done.7.core
  46.4 0.7 %last_sum.1 = f32[256,256]{1,0:T(8,128)} custom-call(s32[1,1,1]{2,1,0:T(1,128)S(6)} %copy.19.mask, f32[128,256]{1,0:T(8,128)S(1)} %collective-permute-done.5.chip, f32[128,256]{1,0:T(8,128)S(1)} %collective-permute-done.6.far, f32[128,256]{1,0:T(8,128)S(1)} %collective-permute-done.7.core, f32[128,256]{1,0:T(8,128)S(1)} %get-tuple-element.41.own), custom_call_target="tpu_custom_call" | custom-call | flops 262144 | bytes 1048576 | tf_op jit(solution)/shard_map/last_sum/pallas_call | solution.py:187
Async XLA Ops:
  0.0 27.3 %collective-permute-start.4 = (f32[2,256,256]{2,1,0:T(8,128)}, f32[2,256,256]{2,1,0:T(8,128)S(1)}, u32[]{:S(2)}, u32[]{:S(2)}) collective-permute-start(f32[2,256,256]{2,1,0:T(8,128)} %bitcast.10), channel_id=1, source_target_pairs={{0,32},{1,33},{2,34},{3,35},{4,36},{5,37},{6,38},{7,39},{8,40},{9,... | collective-permute-start | bytes 1572872 | tf_op jit(solution)/shard_map/ppermute | solution.py:113
  4.0 10.1 %copy-start = (f32[1,1,1,2,256,256]{5,4,3,2,1,0:T(8,128)S(1)}, f32[1,1,1,2,256,256]{5,4,3,2,1,0:T(8,128)}, u32[]{:S(2)}) copy-start(f32[1,1,1,2,256,256]{5,4,3,2,1,0:T(8,128)} %param.11) | copy-start | bytes 1572868
  4.0 10.1 %copy-start.1 = (f32[1,1,1,2,256,256]{5,4,3,2,1,0:T(8,128)S(1)}, f32[1,1,1,2,256,256]{5,4,3,2,1,0:T(8,128)}, u32[]{:S(2)}) copy-start(f32[1,1,1,2,256,256]{5,4,3,2,1,0:T(8,128)} %param.12) | copy-start | bytes 1572868
  5.2 27.4 %collective-permute-start.2 = (f32[2,128,256]{2,1,0:T(8,128)S(1)}, f32[2,128,256]{2,1,0:T(8,128)S(1)}, u32[]{:S(2)}, u32[]{:S(2)}) collective-permute-start(f32[2,128,256]{2,1,0:T(8,128)S(1)} %get-tuple-element.50), channel_id=1, source_target_pairs={{0,1},{1,2},{2,3},{3,4},{4,5},{5,6},{6,7},{7,8},{8,9},{9,10},{10,1... | collective-permute-start | bytes 786440 | tf_op jit(solution)/shard_map/ppermute | solution.py:113
  8.8 5.4 %copy-start.3 = (s32[1,1,1,2,12]{4,3,2,1,0:T(2,128)S(1)}, s32[1,1,1,2,12]{4,3,2,1,0:T(2,128)}, u32[]{:S(2)}) copy-start(s32[1,1,1,2,12]{4,3,2,1,0:T(2,128)} %param.14) | copy-start | bytes 292
  8.8 5.4 %copy-start.4 = (s32[1,1,1,2,12]{4,3,2,1,0:T(2,128)S(1)}, s32[1,1,1,2,12]{4,3,2,1,0:T(2,128)}, u32[]{:S(2)}) copy-start(s32[1,1,1,2,12]{4,3,2,1,0:T(2,128)} %param.15) | copy-start | bytes 292
  8.8 27.0 %collective-permute-start.3 = (f32[2,128,256]{2,1,0:T(8,128)S(1)}, f32[2,128,256]{2,1,0:T(8,128)S(1)}, u32[]{:S(2)}, u32[]{:S(2)}) collective-permute-start(f32[2,128,256]{2,1,0:T(8,128)S(1)} %get-tuple-element.49), channel_id=1, source_target_pairs={{0,257},{1,258},{2,259},{3,260},{4,261},{5,262},{6,263},{7,264},{8... | collective-permute-start | bytes 786440 | tf_op jit(solution)/shard_map/ppermute | solution.py:113
  13.5 0.7 %copy-start.5 = (s32[1,1,1,2]{3,2,1,0:T(1,128)S(1)}, s32[1,1,1,2]{3,2,1,0:T(1,128)}, u32[]{:S(2)}) copy-start(s32[1,1,1,2]{3,2,1,0:T(1,128)} %param.16) | copy-start | bytes 28
  14.2 0.7 %copy-start.2 = (s32[1,1,1,2,12]{4,3,2,1,0:T(2,128)S(1)}, s32[1,1,1,2,12]{4,3,2,1,0:T(2,128)}, u32[]{:S(2)}) copy-start(s32[1,1,1,2,12]{4,3,2,1,0:T(2,128)} %param.13) | copy-start | bytes 292
  16.1 11.1 %collective-permute-start.1 = (f32[528,256]{1,0:T(8,128)S(1)}, f32[528,256]{1,0:T(8,128)S(1)}, u32[]{:S(2)}, u32[]{:S(2)}) collective-permute-start(f32[528,256]{1,0:T(8,128)S(1)} %get-tuple-element.25), channel_id=1, source_target_pairs={{0,256},{1,257},{2,258},{3,259},{4,260},{5,261},{6,262},{7,263},{8... | collective-permute-start | bytes 1622024 | tf_op jit(solution)/shard_map/cond/branch_1_fun/ppermute | solution.py:113
  27.4 5.1 %collective-permute-start = (f32[2,256,256]{2,1,0:T(8,128)S(1)}, f32[2,256,256]{2,1,0:T(8,128)S(1)}, u32[]{:S(2)}, u32[]{:S(2)}) collective-permute-start(f32[2,256,256]{2,1,0:T(8,128)S(1)} %right_own), channel_id=1, source_target_pairs={{0,256},{1,257},{2,258},{3,259},{4,260},{5,261},{6,262},{7,263},{8... | collective-permute-start | bytes 1572872 | tf_op jit(solution)/shard_map/cond/branch_1_fun/ppermute | solution.py:113
  36.5 8.3 %collective-permute-start.5 = (f32[128,256]{1,0:T(8,128)S(1)}, f32[128,256]{1,0:T(8,128)S(1)}, u32[]{:S(2)}, u32[]{:S(2)}) collective-permute-start(f32[128,256]{1,0:T(8,128)S(1)} %get-tuple-element.38), channel_id=1, source_target_pairs={{0,512},{1,513},{2,514},{3,515},{4,516},{5,517},{6,518},{7,519},{8... | collective-permute-start | bytes 393224 | tf_op jit(solution)/shard_map/ppermute | solution.py:113
  39.6 6.8 %collective-permute-start.6 = (f32[128,256]{1,0:T(8,128)S(1)}, f32[128,256]{1,0:T(8,128)S(1)}, u32[]{:S(2)}, u32[]{:S(2)}) collective-permute-start(f32[128,256]{1,0:T(8,128)S(1)} %get-tuple-element.39), channel_id=1, source_target_pairs={{0,768},{1,769},{2,770},{3,771},{4,772},{5,773},{6,774},{7,775},{8... | collective-permute-start | bytes 393224 | tf_op jit(solution)/shard_map/ppermute | solution.py:113
  41.5 4.9 %collective-permute-start.7 = (f32[128,256]{1,0:T(8,128)S(1)}, f32[128,256]{1,0:T(8,128)S(1)}, u32[]{:S(2)}, u32[]{:S(2)}) collective-permute-start(f32[128,256]{1,0:T(8,128)S(1)} %get-tuple-element.40), channel_id=1, source_target_pairs={{0,256},{1,257},{2,258},{3,259},{4,260},{5,261},{6,262},{7,263},{8... | collective-permute-start | bytes 393224 | tf_op jit(solution)/shard_map/ppermute | solution.py:113

commit v4 on v3

--- a/solution.py
+++ b/solution.py
@@ -72,6 +72,11 @@
     weights[16:] = heard[size:, :]
 
 
+def hold_kernel(*refs):
+    for value, out in zip(refs[: len(refs) // 2], refs[len(refs) // 2 :]):
+        out[...] = value[...]
+
+
 def ready_kernel(right_own, right_mate, right_high, right_low):
     for slot in range(4):
         right = (right_own if slot < 2 else right_mate)[slot % 2]
@@ -101,13 +106,15 @@
         copy.wait()
 
 
-def permute(value, to):
+def permute(value, to, takes=None):
     names = ("layer", "row", "col")
     sizes = [lax.axis_size(name) for name in names]
     pairs = []
     for l in range(sizes[0]):
         for r in range(sizes[1]):
             for c in range(sizes[2]):
+                if takes is not None and not takes(l, r, c):
+                    continue
                 ln, rn, cn = to(l, r, c)
                 pairs.append(((l * sizes[1] + r) * sizes[2] + c, (ln * sizes[1] + rn % sizes[1]) * sizes[2] + cn % sizes[2]))
     return lax.ppermute(value, names, pairs)
@@ -127,10 +134,27 @@
     def piece(side):
         return lax.dynamic_slice_in_dim(left, side * half, half, 1, allow_negative_indices=False)
 
-    right_own = permute(right, lambda l, r, c: (l, r + 1, c))
+    right_first = permute(right, lambda l, r, c: (l, r + 1, c), lambda l, r, c: c == 0)
     left_own = permute(piece(core), lambda l, r, c: (l, r, c + 1))
     left_mate = permute(piece(1 - core), lambda l, r, c: (l ^ 1, r, c + 1))
-    def beside(left, right):
+    within = lax.axis_index("layer") < lax.axis_size("layer")
+
+    def guarded(branch, *args):
+        shapes = jax.eval_shape(branch, *args)
+        return lax.cond(within, branch, lambda *_: tuple(jnp.zeros(s.shape, s.dtype) for s in shapes), *args)
+
+    def hold(*values):
+        return pl.pallas_call(
+            hold_kernel,
+            out_shape=tuple(jax.ShapeDtypeStruct(v.shape, v.dtype) for v in values),
+            in_specs=[vmem] * len(values),
+            out_specs=(vmem,) * len(values),
+            compiler_params=PARAMS,
+            cost_estimate=pl.CostEstimate(flops=1 << 17, bytes_accessed=1 << 20, transcendentals=0),
+            name="hold",
+        )(*values)
+
+    def early(left, right):
         keep, send = pl.pallas_call(
             first_kernel,
             out_shape=(jax.ShapeDtypeStruct((4 * half + 16, cols), f32),) * 2,
@@ -152,7 +176,15 @@
             name="join",
         )(keep, heard)
 
-    def middle(right_own):
+    def beside(left, right):
+        right_rest = permute(right, lambda l, r, c: (l, r + 1, c), lambda l, r, c: c != 0)
+        base, weights = guarded(early, left, right)
+        base, weights = hold(base, weights)
+        (right_rest,) = hold(right_rest)
+        return base, weights, right_rest
+
+    def middle(right_first, right_rest):
+        right_own = jnp.where(lax.axis_index("col") == 0, right_first, right_rest)
         right_mate = permute(right_own, lambda l, r, c: (l ^ 1, r, c))
         return pl.pallas_call(
             ready_kernel,
@@ -164,14 +196,8 @@
             name="ready",
         )(right_own, right_mate)
 
-    within = live_counts[0, 0, 0, 0] <= left_index.shape[4]
-
-    def guarded(branch, *args):
-        shapes = jax.eval_shape(branch, *args)
-        return lax.cond(within, branch, lambda *_: tuple(jnp.zeros(s.shape, s.dtype) for s in shapes), *args)
-
-    base, weights = guarded(beside, left, right)
-    right_high, right_low = guarded(middle, right_own)
+    base, weights, right_rest = guarded(beside, left, right)
+    right_high, right_low = guarded(middle, right_first, right_rest)
     own, core_out, chip_out, far_out = pl.pallas_call(
         second_kernel,
         out_shape=(jax.ShapeDtypeStruct((half, cols), f32),) * 4,

time: 48 us -> 49.1 us (1.023)
  the two profiles are of different devices: /device:TPU:1 before, /device:TPU:353 now
where the time goes in v4:
time: 49.1 us; the launch traced here: 48.7 us
  starting transfers between devices  25 us (51%)
  waiting for transfers between devices  16.8 us (34%)
  Pallas kernels  3.49 us (7%)
  local copies, waits for them, and re-layouts  2.48 us (5%)
  between operations  0.81 us (2%)
    ppermute x9, starting transfers between devices, permute(): return lax.ppermute(value, names, pairs)  25 us
    ppermute x9, waiting for transfers between devices, permute(): return lax.ppermute(value, names, pairs)  16.8 us
    dynamic_slice x1, local copies, waits for them, and re-layouts, piece(): lax.dynamic_slice_in_dim(left, side * half, half, 1, allow_negative_indic...  1.83 us
    pallas_call x1, Pallas kernels, early(): pl.pallas_call(first_kernel, out_shape=(jax.ShapeDtypeStruct((4 * half +...  1.78 us
  transfers between devices with their start and end apart: 9, of which 4 were waited for; matrix products, arithmetic and copies ran while one was open for 4% of the time, Pallas kernels for 4%

profile of v4, /device:TPU:353, one launch (start us, length us, event | category | flops | bytes accessed | tf_op | source)
XLA Modules:
  0.0 48.7 jit_solution(9773699705928974566)
XLA Ops:
  0.0 0.7 %collective-permute-start.5 = (f32[2,256,256]{2,1,0:T(8,128)}, f32[2,256,256]{2,1,0:T(8,128)S(1)}, u32[]{:S(2)}, u32[]{:S(2)}) collective-permute-start(f32[2,256,256]{2,1,0:T(8,128)} %bitcast.3), channel_id=1, source_target_pairs={{0,32},{32,64},{64,96},{96,128},{128,160},{160,192},{192,224},{224... | collective-permute-start | bytes 1572872 | tf_op jit(solution)/shard_map/ppermute | solution.py:120
  0.7 0.0 copy-start
  0.7 0.0 copy-start.2
  0.7 0.0 copy-start.3
  0.7 1.8 %dynamic-slice_bitcast_fusion = (f32[2,128,256]{2,1,0:T(8,128)S(1)}, f32[2,128,256]{2,1,0:T(8,128)}) fusion(f32[1,1,1,2,256,256]{5,4,3,2,1,0:T(8,128)} %param.13, s32[]{:T(128)S(6)} %mul.7, s32[]{:T(128)S(6)} %mul.6), kind=kLoop, calls=%fused_computation.1 | loop fusion | bytes 1048584 | tf_op jit(solution)/shard_map/dynamic_slice | solution.py:135
  2.6 4.7 %collective-permute-start.3 = (f32[2,128,256]{2,1,0:T(8,128)}, f32[2,128,256]{2,1,0:T(8,128)S(1)}, u32[]{:S(2)}, u32[]{:S(2)}) collective-permute-start(f32[2,128,256]{2,1,0:T(8,128)} %get-tuple-element.85), channel_id=1, source_target_pairs={{0,1},{1,2},{2,3},{3,4},{4,5},{5,6},{6,7},{7,8},{8,9},{9,10},{10,1... | collective-permute-start | bytes 786440 | tf_op jit(solution)/shard_map/ppermute | solution.py:120
  7.3 4.4 %collective-permute-start.4 = (f32[2,128,256]{2,1,0:T(8,128)S(1)}, f32[2,128,256]{2,1,0:T(8,128)S(1)}, u32[]{:S(2)}, u32[]{:S(2)}) collective-permute-start(f32[2,128,256]{2,1,0:T(8,128)S(1)} %get-tuple-element.84), channel_id=1, source_target_pairs={{0,257},{1,258},{2,259},{3,260},{4,261},{5,262},{6,263},{7,264},{8... | collective-permute-start | bytes 786440 | tf_op jit(solution)/shard_map/ppermute | solution.py:120
  11.7 0.0 copy-start.1
  11.7 0.0 copy-start.4
  11.7 0.0 copy-done
  11.7 0.0 copy-done.2
  11.7 0.0 copy-done.3
  11.8 0.6 %copy-done.1 = s32[1,1,1,2,12]{4,3,2,1,0:T(2,128)S(1)} copy-done((s32[1,1,1,2,12]{4,3,2,1,0:T(2,128)S(1)}, s32[1,1,1,2,12]{4,3,2,1,0:T(2,128)}, u32[]{:S(2)}) %copy-start.1) | copy-done | bytes 120
  12.4 0.0 copy-done.4
  12.4 19.6 %conditional.3 = (f32[512,256]{1,0:T(8,128)S(1)}, f32[32,256]{1,0:T(8,128)S(1)}, f32[2,256,256]{2,1,0:T(8,128)S(1)}) conditional(s32[]{:T(128)} %convert_element_type.7, () %tuple.28, (pred[]{:T(512)}, f32[1,1,1,2,256,256]{5,4,3,2,1,0:T(8,128)S(1)}, s32[1,1,1,2,12]{4,3,2,1,0:T(2,128)S(1)}, s32[1,1,1,2,12]{4,3,2,1,0:T(2,128)S(1)}, ...), branch_computations={%region_0.0_spmd, %region_1.0_spmd} | conditional | flops 403046400 | bytes 10027173 | solution.py:144
  12.4 3.2 %collective-permute-start.1 = (f32[2,256,256]{2,1,0:T(8,128)}, f32[2,256,256]{2,1,0:T(8,128)S(1)}, u32[]{:S(2)}, u32[]{:S(2)}) collective-permute-start(f32[2,256,256]{2,1,0:T(8,128)} %get-tuple-element.51), channel_id=1, source_target_pairs={{1,33},{2,34},{3,35},{4,36},{5,37},{6,38},{7,39},{8,40},{9,41},{10... | collective-permute-start | bytes 1572872 | tf_op jit(solution)/shard_map/cond/branch_1_fun/ppermute | solution.py:120
  15.6 5.7 %conditional = ((f32[512,256]{1,0:T(8,128)S(1)}, f32[32,256]{1,0:T(8,128)S(1)})) conditional(s32[]{:T(128)} %convert_element_type.1, () %tuple.19, (f32[1,1,1,2,256,256]{5,4,3,2,1,0:T(8,128)S(1)}, s32[1,1,1,2,12]{4,3,2,1,0:T(2,128)S(1)}, s32[1,1,1,2,12]{4,3,2,1,0:T(2,128)S(1)}, s32[1,1,1,2,12]{4,3,2,1,0:T(2,128)S(1)}, s32[1,1,1,2]{3,2,1,0:T(1,128)S(1)}, ...), branch_computations={%region_2.0_spmd, %region_3.0_spmd} | conditional | flops 402784256 | bytes 5832752 | solution.py:144
  15.6 1.8 %first_step.1 = (f32[528,256]{1,0:T(8,128)S(1)}, f32[528,256]{1,0:T(8,128)S(1)}) custom-call(s32[1,1,1,2,12]{4,3,2,1,0:T(2,128)S(1)} %get-tuple-element.37.li, s32[1,1,1,2,12]{4,3,2,1,0:T(2,128)S(1)} %get-tuple-element.38.ri, s32[1,1,1,2,12]{4,3,2,1,0:T(2,128)S(1)} %get-tuple-element.39.ti, s32[1,1,1,2]{3,2,1,0:T(1,128)S(1)} %get-tuple-element.40.counts, ...), custom_call_target="tpu_custom_call" | custom-call | flops 402653184 | bytes 2097152 | tf_op jit(solution)/shard_map/cond/branch_1_fun/cond/branch_1_fun/first_step/pallas_call | solution.py:158
  17.4 1.9 %collective-permute-start = (f32[528,256]{1,0:T(8,128)S(1)}, f32[528,256]{1,0:T(8,128)S(1)}, u32[]{:S(2)}, u32[]{:S(2)}) collective-permute-start(f32[528,256]{1,0:T(8,128)S(1)} %get-tuple-element.44), channel_id=1, source_target_pairs={{0,256},{1,257},{2,258},{3,259},{4,260},{5,261},{6,262},{7,263},{8... | collective-permute-start | bytes 1622024 | tf_op jit(solution)/shard_map/cond/branch_1_fun/cond/branch_1_fun/ppermute | solution.py:120
  19.3 1.9 %collective-permute-done.heard = f32[528,256]{1,0:T(8,128)S(1)} collective-permute-done((f32[528,256]{1,0:T(8,128)S(1)}, f32[528,256]{1,0:T(8,128)S(1)}, u32[]{:S(2)}, u32[]{:S(2)}) %collective-permute-start) | collective-permute-done | bytes 540704 | tf_op jit(solution)/shard_map/cond/branch_1_fun/cond/branch_1_fun/ppermute | solution.py:120
  21.2 0.1 join.1
  21.3 10.6 %collective-permute-done.1.refs_0_ = f32[2,256,256]{2,1,0:T(8,128)S(1)} collective-permute-done((f32[2,256,256]{2,1,0:T(8,128)}, f32[2,256,256]{2,1,0:T(8,128)S(1)}, u32[]{:S(2)}, u32[]{:S(2)}) %collective-permute-start.1) | collective-permute-done | bytes 524320 | tf_op jit(solution)/shard_map/cond/branch_1_fun/ppermute | solution.py:120
  32.0 0.0 collective-permute-done.5
  32.0 4.1 %conditional.4 = ((bf16[4,256,256]{2,1,0:T(8,128)(2,1)S(1)}, bf16[4,256,256]{2,1,0:T(8,128)(2,1)S(1)})) conditional(s32[]{:T(128)} %convert_element_type.7, () %tuple.27, (f32[2,256,256]{2,1,0:T(8,128)S(1)}, f32[2,256,256]{2,1,0:T(8,128)S(1)}) %tuple.30), branch_computations={%region_4.0_spmd, %region_5.6_spmd} | conditional | flops 1179651 | bytes 5767246 | solution.py:144
  32.0 0.1 broadcast_select_fusion.right_own
  32.1 2.3 %collective-permute-start.2 = (f32[2,256,256]{2,1,0:T(8,128)S(1)}, f32[2,256,256]{2,1,0:T(8,128)S(1)}, u32[]{:S(2)}, u32[]{:S(2)}) collective-permute-start(f32[2,256,256]{2,1,0:T(8,128)S(1)} %broadcast_select_fusion.right_own), channel_id=1, source_target_pairs={{0,256},{1,257},{2,258},{3,259},{4,260},{5,261},{6,262},{7,263},{8... | collective-permute-start | bytes 1572872 | tf_op jit(solution)/shard_map/cond/branch_1_fun/ppermute | solution.py:120
  34.4 1.5 %collective-permute-done.2.right_mate = f32[2,256,256]{2,1,0:T(8,128)S(1)} collective-permute-done((f32[2,256,256]{2,1,0:T(8,128)S(1)}, f32[2,256,256]{2,1,0:T(8,128)S(1)}, u32[]{:S(2)}, u32[]{:S(2)}) %collective-permute-start.2) | collective-permute-done | bytes 524320 | tf_op jit(solution)/shard_map/cond/branch_1_fun/ppermute | solution.py:120
  35.9 0.2 ready.1
  36.1 0.0 collective-permute-done.3.left_own
  36.1 0.0 collective-permute-done.4.left_mate
  36.1 0.7 %second_step.1 = (f32[128,256]{1,0:T(8,128)S(1)}, f32[128,256]{1,0:T(8,128)S(1)}, f32[128,256]{1,0:T(8,128)S(1)}, f32[128,256]{1,0:T(8,128)S(1)}) custom-call(f32[2,128,256]{2,1,0:T(8,128)S(1)} %collective-permute-done.3.left_own, f32[2,128,256]{2,1,0:T(8,128)S(1)} %collective-permute-done.4.left_mate, ...), custom_call_target="tpu_custom_call" | custom-call | flops 402653184 | bytes 3145728 | tf_op jit(solution)/shard_map/second_step/pallas_call | solution.py:201
  36.8 3.2 %collective-permute-start.6 = (f32[128,256]{1,0:T(8,128)S(1)}, f32[128,256]{1,0:T(8,128)S(1)}, u32[]{:S(2)}, u32[]{:S(2)}) collective-permute-start(f32[128,256]{1,0:T(8,128)S(1)} %get-tuple-element.72), channel_id=1, source_target_pairs={{0,512},{1,513},{2,514},{3,515},{4,516},{5,517},{6,518},{7,519},{8... | collective-permute-start | bytes 393224 | tf_op jit(solution)/shard_map/ppermute | solution.py:120
  40.0 2.6 %collective-permute-start.7 = (f32[128,256]{1,0:T(8,128)S(1)}, f32[128,256]{1,0:T(8,128)S(1)}, u32[]{:S(2)}, u32[]{:S(2)}) collective-permute-start(f32[128,256]{1,0:T(8,128)S(1)} %get-tuple-element.73), channel_id=1, source_target_pairs={{0,768},{1,769},{2,770},{3,771},{4,772},{5,773},{6,774},{7,775},{8... | collective-permute-start | bytes 393224 | tf_op jit(solution)/shard_map/ppermute | solution.py:120
  42.6 1.9 %collective-permute-start.8 = (f32[128,256]{1,0:T(8,128)S(1)}, f32[128,256]{1,0:T(8,128)S(1)}, u32[]{:S(2)}, u32[]{:S(2)}) collective-permute-start(f32[128,256]{1,0:T(8,128)S(1)} %get-tuple-element.74), channel_id=1, source_target_pairs={{0,256},{1,257},{2,258},{3,259},{4,260},{5,261},{6,262},{7,263},{8... | collective-permute-start | bytes 393224 | tf_op jit(solution)/shard_map/ppermute | solution.py:120
  45.2 0.0 collective-permute-done.6.chip
  45.2 2.7 %collective-permute-done.7.far = f32[128,256]{1,0:T(8,128)S(1)} collective-permute-done((f32[128,256]{1,0:T(8,128)S(1)}, f32[128,256]{1,0:T(8,128)S(1)}, u32[]{:S(2)}, u32[]{:S(2)}) %collective-permute-start.7) | collective-permute-done | bytes 131104 | tf_op jit(solution)/shard_map/ppermute | solution.py:120
  47.9 0.0 collective-permute-done.8.core
  47.9 0.7 %last_sum.1 = f32[256,256]{1,0:T(8,128)} custom-call(s32[1,1,1]{2,1,0:T(1,128)S(6)} %copy.26.mask, f32[128,256]{1,0:T(8,128)S(1)} %collective-permute-done.6.chip, f32[128,256]{1,0:T(8,128)S(1)} %collective-permute-done.7.far, f32[128,256]{1,0:T(8,128)S(1)} %collective-permute-done.8.core, f32[128,256]{1,0:T(8,128)S(1)} %get-tuple-element.75.own), custom_call_target="tpu_custom_call" | custom-call | flops 262144 | bytes 1048576 | tf_op jit(solution)/shard_map/last_sum/pallas_call | solution.py:213
  (2 shorter events, 0.1 us)
Async XLA Ops:
  0.0 32.0 %collective-permute-start.5 = (f32[2,256,256]{2,1,0:T(8,128)}, f32[2,256,256]{2,1,0:T(8,128)S(1)}, u32[]{:S(2)}, u32[]{:S(2)}) collective-permute-start(f32[2,256,256]{2,1,0:T(8,128)} %bitcast.3), channel_id=1, source_target_pairs={{0,32},{32,64},{64,96},{96,128},{128,160},{160,192},{192,224},{224... | collective-permute-start | bytes 1572872 | tf_op jit(solution)/shard_map/ppermute | solution.py:120
  0.7 11.0 %copy-start = (f32[1,1,1,2,256,256]{5,4,3,2,1,0:T(8,128)S(1)}, f32[1,1,1,2,256,256]{5,4,3,2,1,0:T(8,128)}, u32[]{:S(2)}) copy-start(f32[1,1,1,2,256,256]{5,4,3,2,1,0:T(8,128)} %param.13) | copy-start | bytes 1572868
  0.7 11.0 %copy-start.2 = (s32[1,1,1,2,12]{4,3,2,1,0:T(2,128)S(1)}, s32[1,1,1,2,12]{4,3,2,1,0:T(2,128)}, u32[]{:S(2)}) copy-start(s32[1,1,1,2,12]{4,3,2,1,0:T(2,128)} %param.16) | copy-start | bytes 292
  0.7 11.0 %copy-start.3 = (s32[1,1,1,2,12]{4,3,2,1,0:T(2,128)S(1)}, s32[1,1,1,2,12]{4,3,2,1,0:T(2,128)}, u32[]{:S(2)}) copy-start(s32[1,1,1,2,12]{4,3,2,1,0:T(2,128)} %param.17) | copy-start | bytes 292
  2.6 33.5 %collective-permute-start.3 = (f32[2,128,256]{2,1,0:T(8,128)}, f32[2,128,256]{2,1,0:T(8,128)S(1)}, u32[]{:S(2)}, u32[]{:S(2)}) collective-permute-start(f32[2,128,256]{2,1,0:T(8,128)} %get-tuple-element.85), channel_id=1, source_target_pairs={{0,1},{1,2},{2,3},{3,4},{4,5},{5,6},{6,7},{7,8},{8,9},{9,10},{10,1... | collective-permute-start | bytes 786440 | tf_op jit(solution)/shard_map/ppermute | solution.py:120
  7.3 28.8 %collective-permute-start.4 = (f32[2,128,256]{2,1,0:T(8,128)S(1)}, f32[2,128,256]{2,1,0:T(8,128)S(1)}, u32[]{:S(2)}, u32[]{:S(2)}) collective-permute-start(f32[2,128,256]{2,1,0:T(8,128)S(1)} %get-tuple-element.84), channel_id=1, source_target_pairs={{0,257},{1,258},{2,259},{3,260},{4,261},{5,262},{6,263},{7,264},{8... | collective-permute-start | bytes 786440 | tf_op jit(solution)/shard_map/ppermute | solution.py:120
  11.7 0.7 %copy-start.1 = (s32[1,1,1,2,12]{4,3,2,1,0:T(2,128)S(1)}, s32[1,1,1,2,12]{4,3,2,1,0:T(2,128)}, u32[]{:S(2)}) copy-start(s32[1,1,1,2,12]{4,3,2,1,0:T(2,128)} %param.15) | copy-start | bytes 292
  11.7 0.7 %copy-start.4 = (s32[1,1,1,2]{3,2,1,0:T(1,128)S(1)}, s32[1,1,1,2]{3,2,1,0:T(1,128)}, u32[]{:S(2)}) copy-start(s32[1,1,1,2]{3,2,1,0:T(1,128)} %param.18) | copy-start | bytes 28
  12.4 19.6 %collective-permute-start.1 = (f32[2,256,256]{2,1,0:T(8,128)}, f32[2,256,256]{2,1,0:T(8,128)S(1)}, u32[]{:S(2)}, u32[]{:S(2)}) collective-permute-start(f32[2,256,256]{2,1,0:T(8,128)} %get-tuple-element.51), channel_id=1, source_target_pairs={{1,33},{2,34},{3,35},{4,36},{5,37},{6,38},{7,39},{8,40},{9,41},{10... | collective-permute-start | bytes 1572872 | tf_op jit(solution)/shard_map/cond/branch_1_fun/ppermute | solution.py:120
  17.4 3.8 %collective-permute-start = (f32[528,256]{1,0:T(8,128)S(1)}, f32[528,256]{1,0:T(8,128)S(1)}, u32[]{:S(2)}, u32[]{:S(2)}) collective-permute-start(f32[528,256]{1,0:T(8,128)S(1)} %get-tuple-element.44), channel_id=1, source_target_pairs={{0,256},{1,257},{2,258},{3,259},{4,260},{5,261},{6,262},{7,263},{8... | collective-permute-start | bytes 1622024 | tf_op jit(solution)/shard_map/cond/branch_1_fun/cond/branch_1_fun/ppermute | solution.py:120
  32.1 3.8 %collective-permute-start.2 = (f32[2,256,256]{2,1,0:T(8,128)S(1)}, f32[2,256,256]{2,1,0:T(8,128)S(1)}, u32[]{:S(2)}, u32[]{:S(2)}) collective-permute-start(f32[2,256,256]{2,1,0:T(8,128)S(1)} %broadcast_select_fusion.right_own), channel_id=1, source_target_pairs={{0,256},{1,257},{2,258},{3,259},{4,260},{5,261},{6,262},{7,263},{8... | collective-permute-start | bytes 1572872 | tf_op jit(solution)/shard_map/cond/branch_1_fun/ppermute | solution.py:120
  36.8 8.4 %collective-permute-start.6 = (f32[128,256]{1,0:T(8,128)S(1)}, f32[128,256]{1,0:T(8,128)S(1)}, u32[]{:S(2)}, u32[]{:S(2)}) collective-permute-start(f32[128,256]{1,0:T(8,128)S(1)} %get-tuple-element.72), channel_id=1, source_target_pairs={{0,512},{1,513},{2,514},{3,515},{4,516},{5,517},{6,518},{7,519},{8... | collective-permute-start | bytes 393224 | tf_op jit(solution)/shard_map/ppermute | solution.py:120
  40.0 7.9 %collective-permute-start.7 = (f32[128,256]{1,0:T(8,128)S(1)}, f32[128,256]{1,0:T(8,128)S(1)}, u32[]{:S(2)}, u32[]{:S(2)}) collective-permute-start(f32[128,256]{1,0:T(8,128)S(1)} %get-tuple-element.73), channel_id=1, source_target_pairs={{0,768},{1,769},{2,770},{3,771},{4,772},{5,773},{6,774},{7,775},{8... | collective-permute-start | bytes 393224 | tf_op jit(solution)/shard_map/ppermute | solution.py:120
  42.6 5.3 %collective-permute-start.8 = (f32[128,256]{1,0:T(8,128)S(1)}, f32[128,256]{1,0:T(8,128)S(1)}, u32[]{:S(2)}, u32[]{:S(2)}) collective-permute-start(f32[128,256]{1,0:T(8,128)S(1)} %get-tuple-element.74), channel_id=1, source_target_pairs={{0,256},{1,257},{2,258},{3,259},{4,260},{5,261},{6,262},{7,263},{8... | collective-permute-start | bytes 393224 | tf_op jit(solution)/shard_map/ppermute | solution.py:120

commit v5 on v4

--- a/solution.py
+++ b/solution.py
@@ -72,6 +72,13 @@
     weights[16:] = heard[size:, :]
 
 
+def split_kernel(left, same, cross):
+    side = lax.axis_index("layer") & 1
+    half = same.shape[1]
+    for out, begin in ((same, side * half), (cross, (1 - side) * half)):
+        out[...] = left[:, pl.ds(pl.multiple_of(begin, half), half)]
+
+
 def hold_kernel(*refs):
     for value, out in zip(refs[: len(refs) // 2], refs[len(refs) // 2 :]):
         out[...] = value[...]
@@ -126,17 +133,24 @@
     slots, rows, cols = left.shape
     half = rows // 2
     f32 = jnp.float32
-    core = lax.axis_index("layer") & 1
     vmem = pl.BlockSpec(memory_space=VMEM)
     smem = pl.BlockSpec(memory_space=SMEM)
     anywhere = pl.BlockSpec(memory_space=pl.ANY)
 
-    def piece(side):
-        return lax.dynamic_slice_in_dim(left, side * half, half, 1, allow_negative_indices=False)
-
-    right_first = permute(right, lambda l, r, c: (l, r + 1, c), lambda l, r, c: c == 0)
-    left_own = permute(piece(core), lambda l, r, c: (l, r, c + 1))
-    left_mate = permute(piece(1 - core), lambda l, r, c: (l ^ 1, r, c + 1))
+    pieces = pl.pallas_call(
+        split_kernel,
+        out_shape=(jax.ShapeDtypeStruct((slots, half, cols), f32),) * 2,
+        in_specs=[vmem],
+        out_specs=(vmem,) * 2,
+        compiler_params=PARAMS,
+        cost_estimate=pl.CostEstimate(flops=1 << 10, bytes_accessed=1 << 20, transcendentals=0),
+        name="split",
+    )(left)
+
+    last_col = lax.axis_size("col") - 1
+    right_first = permute(right, lambda l, r, c: (l, r + 1, c), lambda l, r, c: c != last_col)
+    left_own = permute(pieces[0], lambda l, r, c: (l, r, c + 1))
+    left_mate = permute(pieces[1], lambda l, r, c: (l ^ 1, r, c + 1))
     within = lax.axis_index("layer") < lax.axis_size("layer")
 
     def guarded(branch, *args):
@@ -177,14 +191,14 @@
         )(keep, heard)
 
     def beside(left, right):
-        right_rest = permute(right, lambda l, r, c: (l, r + 1, c), lambda l, r, c: c != 0)
+        right_rest = permute(right, lambda l, r, c: (l, r + 1, c), lambda l, r, c: c == last_col)
         base, weights = guarded(early, left, right)
         base, weights = hold(base, weights)
         (right_rest,) = hold(right_rest)
         return base, weights, right_rest
 
     def middle(right_first, right_rest):
-        right_own = jnp.where(lax.axis_index("col") == 0, right_first, right_rest)
+        right_own = jnp.where(lax.axis_index("col") == last_col, right_rest, right_first)
         right_mate = permute(right_own, lambda l, r, c: (l ^ 1, r, c))
         return pl.pallas_call(
             ready_kernel,

time: 49.1 us -> 46.3 us (0.943)
  the two profiles are of different devices: /device:TPU:353 before, /device:TPU:1 now
where the time goes in v5:
time: 46.3 us; the launch traced here: 45.8 us
  starting transfers between devices  33.5 us (72%)
  waiting for transfers between devices  5.06 us (11%)
  Pallas kernels  4.53 us (10%)
  other arithmetic  1.12 us (2%)
  between operations  0.78 us (2%)
  local copies, waits for them, and re-layouts  0.68 us (1%)
    ppermute x9, starting transfers between devices, permute(): return lax.ppermute(value, names, pairs)  33.5 us
    ppermute x9, waiting for transfers between devices, permute(): return lax.ppermute(value, names, pairs)  5.06 us
    pallas_call x1, Pallas kernels, early(): pl.pallas_call(first_kernel, out_shape=(jax.ShapeDtypeStruct((4 * half +...  1.75 us
    select_n x1, other arithmetic, middle(): jnp.where(lax.axis_index('col') == last_col, right_rest, right_first)  1.12 us
    pallas_call x1, Pallas kernels, local(): pl.pallas_call(split_kernel, out_shape=(jax.ShapeDtypeStruct((slots, half...  1.08 us
  transfers between devices with their start and end apart: 9, of which 4 were waited for; matrix products, arithmetic and copies ran while one was open for 2% of the time, Pallas kernels for 7%

profile of v5, /device:TPU:1, one launch (start us, length us, event | category | flops | bytes accessed | tf_op | source)
XLA Modules:
  0.0 45.8 jit_solution(6139565021548931073)
XLA Ops:
  0.0 0.0 copy-start
  0.0 4.2 %collective-permute-start.5 = (f32[2,256,256]{2,1,0:T(8,128)}, f32[2,256,256]{2,1,0:T(8,128)}, u32[]{:S(2)}, u32[]{:S(2)}) collective-permute-start(f32[2,256,256]{2,1,0:T(8,128)} %bitcast.5), channel_id=1, source_target_pairs={{0,32},{1,33},{2,34},{3,35},{4,36},{5,37},{6,38},{7,39},{8,40},{9,... | collective-permute-start | bytes 1572872 | tf_op jit(solution)/shard_map/ppermute | solution.py:127
  4.2 1.1 %split.1 = (f32[2,128,256]{2,1,0:T(8,128)S(1)}, f32[2,128,256]{2,1,0:T(8,128)S(1)}) custom-call(f32[2,256,256]{2,1,0:T(8,128)} %bitcast.3), custom_call_target="tpu_custom_call" | custom-call | flops 1024 | bytes 1048576 | tf_op jit(solution)/shard_map/split/pallas_call | solution.py:140
  5.2 3.5 %collective-permute-start.3 = (f32[2,128,256]{2,1,0:T(8,128)S(1)}, f32[2,128,256]{2,1,0:T(8,128)S(1)}, u32[]{:S(2)}, u32[]{:S(2)}) collective-permute-start(f32[2,128,256]{2,1,0:T(8,128)S(1)} %get-tuple-element.67), channel_id=1, source_target_pairs={{0,1},{1,2},{2,3},{3,4},{4,5},{5,6},{6,7},{7,8},{8,9},{9,10},{10,1... | collective-permute-start | bytes 786440 | tf_op jit(solution)/shard_map/ppermute | solution.py:127
  8.8 4.7 %collective-permute-start.4 = (f32[2,128,256]{2,1,0:T(8,128)S(1)}, f32[2,128,256]{2,1,0:T(8,128)S(1)}, u32[]{:S(2)}, u32[]{:S(2)}) collective-permute-start(f32[2,128,256]{2,1,0:T(8,128)S(1)} %get-tuple-element.68), channel_id=1, source_target_pairs={{0,257},{1,258},{2,259},{3,260},{4,261},{5,262},{6,263},{7,264},{8... | collective-permute-start | bytes 786440 | tf_op jit(solution)/shard_map/ppermute | solution.py:127
  13.5 0.0 copy-start.2
  13.5 0.0 copy-start.3
  13.5 0.0 copy-start.1
  13.5 0.0 copy-start.4
  13.5 0.0 copy-done
  13.5 0.6 %copy-done.2 = s32[1,1,1,2,12]{4,3,2,1,0:T(2,128)S(1)} copy-done((s32[1,1,1,2,12]{4,3,2,1,0:T(2,128)S(1)}, s32[1,1,1,2,12]{4,3,2,1,0:T(2,128)}, u32[]{:S(2)}) %copy-start.2) | copy-done | bytes 120
  14.2 0.0 copy-done.3
  14.2 0.0 copy-done.1
  14.2 0.0 copy-done.4
  14.2 13.7 %conditional.3 = (f32[512,256]{1,0:T(8,128)S(1)}, f32[32,256]{1,0:T(8,128)S(1)}, f32[2,256,256]{2,1,0:T(8,128)S(1)}) conditional(s32[]{:T(128)} %convert_element_type.7, () %tuple.28, (pred[]{:T(512)}, s32[1,1,1,2,12]{4,3,2,1,0:T(2,128)S(1)}, s32[1,1,1,2,12]{4,3,2,1,0:T(2,128)S(1)}, s32[1,1,1,2,12]{4,3,2,1,0:T(2,128)S(1)}, ...), branch_computations={%region_0.0_spmd, %region_1.0_spmd} | conditional | flops 403046400 | bytes 10027173 | solution.py:158
  14.2 0.7 %collective-permute-start.1 = (f32[2,256,256]{2,1,0:T(8,128)}, f32[2,256,256]{2,1,0:T(8,128)S(1)}, u32[]{:S(2)}, u32[]{:S(2)}) collective-permute-start(f32[2,256,256]{2,1,0:T(8,128)} %get-tuple-element.49), channel_id=1, source_target_pairs={{31,63},{63,95},{95,127},{127,159},{159,191},{191,223},{223,255},{... | collective-permute-start | bytes 1572872 | tf_op jit(solution)/shard_map/cond/branch_1_fun/ppermute | solution.py:127
  14.9 13.0 %conditional = ((f32[512,256]{1,0:T(8,128)S(1)}, f32[32,256]{1,0:T(8,128)S(1)})) conditional(s32[]{:T(128)} %convert_element_type.1, () %tuple.19, (s32[1,1,1,2,12]{4,3,2,1,0:T(2,128)S(1)}, s32[1,1,1,2,12]{4,3,2,1,0:T(2,128)S(1)}, s32[1,1,1,2,12]{4,3,2,1,0:T(2,128)S(1)}, s32[1,1,1,2]{3,2,1,0:T(1,128)S(1)}, f32[2,256,256]{2,1,0:T(8,128)S(1)}, ...), branch_computations={%region_2.0_spmd, %region_3.0_spmd} | conditional | flops 402784256 | bytes 5832752 | solution.py:158
  14.9 1.8 %first_step.1 = (f32[528,256]{1,0:T(8,128)S(1)}, f32[528,256]{1,0:T(8,128)S(1)}) custom-call(s32[1,1,1,2,12]{4,3,2,1,0:T(2,128)S(1)} %get-tuple-element.35.li, s32[1,1,1,2,12]{4,3,2,1,0:T(2,128)S(1)} %get-tuple-element.36.ri, s32[1,1,1,2,12]{4,3,2,1,0:T(2,128)S(1)} %get-tuple-element.37.ti, s32[1,1,1,2]{3,2,1,0:T(1,128)S(1)} %get-tuple-element.38.counts, ...), custom_call_target="tpu_custom_call" | custom-call | flops 402653184 | bytes 2097152 | tf_op jit(solution)/shard_map/cond/branch_1_fun/cond/branch_1_fun/first_step/pallas_call | solution.py:172
  16.7 9.6 %collective-permute-start = (f32[528,256]{1,0:T(8,128)S(1)}, f32[528,256]{1,0:T(8,128)S(1)}, u32[]{:S(2)}, u32[]{:S(2)}) collective-permute-start(f32[528,256]{1,0:T(8,128)S(1)} %get-tuple-element.42), channel_id=1, source_target_pairs={{0,256},{1,257},{2,258},{3,259},{4,260},{5,261},{6,262},{7,263},{8... | collective-permute-start | bytes 1622024 | tf_op jit(solution)/shard_map/cond/branch_1_fun/cond/branch_1_fun/ppermute | solution.py:127
  26.2 1.5 %collective-permute-done.heard = f32[528,256]{1,0:T(8,128)S(1)} collective-permute-done((f32[528,256]{1,0:T(8,128)S(1)}, f32[528,256]{1,0:T(8,128)S(1)}, u32[]{:S(2)}, u32[]{:S(2)}) %collective-permute-start) | collective-permute-done | bytes 540704 | tf_op jit(solution)/shard_map/cond/branch_1_fun/cond/branch_1_fun/ppermute | solution.py:127
  27.8 0.1 join.1
  27.9 0.0 collective-permute-done.1.refs_0_
  27.9 0.0 collective-permute-done.5
  27.9 6.0 %conditional.4 = ((bf16[4,256,256]{2,1,0:T(8,128)(2,1)S(1)}, bf16[4,256,256]{2,1,0:T(8,128)(2,1)S(1)})) conditional(s32[]{:T(128)} %convert_element_type.7, () %tuple.27, (f32[2,256,256]{2,1,0:T(8,128)S(1)}, f32[2,256,256]{2,1,0:T(8,128)}) %tuple.30), branch_computations={%region_4.0_spmd, %region_5.6_spmd} | conditional | flops 1179651 | bytes 5767246 | solution.py:158
  28.0 1.1 %broadcast_select_fusion.right_own = f32[2,256,256]{2,1,0:T(8,128)S(1)} fusion(f32[2,256,256]{2,1,0:T(8,128)S(1)} %get-tuple-element.54, f32[2,256,256]{2,1,0:T(8,128)} %get-tuple-element.55, pred[]{:T(512)S(6)} %eq.2), kind=kLoop, calls=%fused_computation | loop fusion | flops 131072 | bytes 1572865 | tf_op jit(solution)/shard_map/cond/branch_1_fun/jit(_where)/select_n | solution.py:201
  29.1 3.2 %collective-permute-start.2 = (f32[2,256,256]{2,1,0:T(8,128)S(1)}, f32[2,256,256]{2,1,0:T(8,128)S(1)}, u32[]{:S(2)}, u32[]{:S(2)}) collective-permute-start(f32[2,256,256]{2,1,0:T(8,128)S(1)} %broadcast_select_fusion.right_own), channel_id=1, source_target_pairs={{0,256},{1,257},{2,258},{3,259},{4,260},{5,261},{6,262},{7,263},{8... | collective-permute-start | bytes 1572872 | tf_op jit(solution)/shard_map/cond/branch_1_fun/ppermute | solution.py:127
  32.3 1.5 %collective-permute-done.2.right_mate = f32[2,256,256]{2,1,0:T(8,128)S(1)} collective-permute-done((f32[2,256,256]{2,1,0:T(8,128)S(1)}, f32[2,256,256]{2,1,0:T(8,128)S(1)}, u32[]{:S(2)}, u32[]{:S(2)}) %collective-permute-start.2) | collective-permute-done | bytes 524320 | tf_op jit(solution)/shard_map/cond/branch_1_fun/ppermute | solution.py:127
  33.8 0.2 ready.1
  34.0 0.0 collective-permute-done.3.left_own
  34.0 0.1 collective-permute-done.4.left_mate
  34.1 0.7 %second_step.1 = (f32[128,256]{1,0:T(8,128)S(1)}, f32[128,256]{1,0:T(8,128)S(1)}, f32[128,256]{1,0:T(8,128)S(1)}, f32[128,256]{1,0:T(8,128)S(1)}) custom-call(f32[2,128,256]{2,1,0:T(8,128)S(1)} %collective-permute-done.3.left_own, f32[2,128,256]{2,1,0:T(8,128)S(1)} %collective-permute-done.4.left_mate, ...), custom_call_target="tpu_custom_call" | custom-call | flops 402653184 | bytes 3145728 | tf_op jit(solution)/shard_map/second_step/pallas_call | solution.py:215
  34.8 3.1 %collective-permute-start.6 = (f32[128,256]{1,0:T(8,128)S(1)}, f32[128,256]{1,0:T(8,128)S(1)}, u32[]{:S(2)}, u32[]{:S(2)}) collective-permute-start(f32[128,256]{1,0:T(8,128)S(1)} %get-tuple-element.74), channel_id=1, source_target_pairs={{0,512},{1,513},{2,514},{3,515},{4,516},{5,517},{6,518},{7,519},{8... | collective-permute-start | bytes 393224 | tf_op jit(solution)/shard_map/ppermute | solution.py:127
  37.9 2.6 %collective-permute-start.7 = (f32[128,256]{1,0:T(8,128)S(1)}, f32[128,256]{1,0:T(8,128)S(1)}, u32[]{:S(2)}, u32[]{:S(2)}) collective-permute-start(f32[128,256]{1,0:T(8,128)S(1)} %get-tuple-element.75), channel_id=1, source_target_pairs={{0,768},{1,769},{2,770},{3,771},{4,772},{5,773},{6,774},{7,775},{8... | collective-permute-start | bytes 393224 | tf_op jit(solution)/shard_map/ppermute | solution.py:127
  40.5 1.9 %collective-permute-start.8 = (f32[128,256]{1,0:T(8,128)S(1)}, f32[128,256]{1,0:T(8,128)S(1)}, u32[]{:S(2)}, u32[]{:S(2)}) collective-permute-start(f32[128,256]{1,0:T(8,128)S(1)} %get-tuple-element.76), channel_id=1, source_target_pairs={{0,256},{1,257},{2,258},{3,259},{4,260},{5,261},{6,262},{7,263},{8... | collective-permute-start | bytes 393224 | tf_op jit(solution)/shard_map/ppermute | solution.py:127
  43.1 0.0 collective-permute-done.6.chip
  43.1 1.9 %collective-permute-done.7.far = f32[128,256]{1,0:T(8,128)S(1)} collective-permute-done((f32[128,256]{1,0:T(8,128)S(1)}, f32[128,256]{1,0:T(8,128)S(1)}, u32[]{:S(2)}, u32[]{:S(2)}) %collective-permute-start.7) | collective-permute-done | bytes 131104 | tf_op jit(solution)/shard_map/ppermute | solution.py:127
  45.0 0.0 collective-permute-done.8.core
  45.0 0.7 %last_sum.1 = f32[256,256]{1,0:T(8,128)} custom-call(s32[1,1,1]{2,1,0:T(1,128)S(6)} %copy.26.mask, f32[128,256]{1,0:T(8,128)S(1)} %collective-permute-done.6.chip, f32[128,256]{1,0:T(8,128)S(1)} %collective-permute-done.7.far, f32[128,256]{1,0:T(8,128)S(1)} %collective-permute-done.8.core, f32[128,256]{1,0:T(8,128)S(1)} %get-tuple-element.77.own), custom_call_target="tpu_custom_call" | custom-call | flops 262144 | bytes 1048576 | tf_op jit(solution)/shard_map/last_sum/pallas_call | solution.py:227
  (2 shorter events, 0.1 us)
Async XLA Ops:
  0.0 13.5 %copy-start = (f32[1,1,1,2,256,256]{5,4,3,2,1,0:T(8,128)S(1)}, f32[1,1,1,2,256,256]{5,4,3,2,1,0:T(8,128)}, u32[]{:S(2)}) copy-start(f32[1,1,1,2,256,256]{5,4,3,2,1,0:T(8,128)} %param.13) | copy-start | bytes 1572868
  0.0 27.9 %collective-permute-start.5 = (f32[2,256,256]{2,1,0:T(8,128)}, f32[2,256,256]{2,1,0:T(8,128)}, u32[]{:S(2)}, u32[]{:S(2)}) collective-permute-start(f32[2,256,256]{2,1,0:T(8,128)} %bitcast.5), channel_id=1, source_target_pairs={{0,32},{1,33},{2,34},{3,35},{4,36},{5,37},{6,38},{7,39},{8,40},{9,... | collective-permute-start | bytes 1572872 | tf_op jit(solution)/shard_map/ppermute | solution.py:127
  5.2 28.8 %collective-permute-start.3 = (f32[2,128,256]{2,1,0:T(8,128)S(1)}, f32[2,128,256]{2,1,0:T(8,128)S(1)}, u32[]{:S(2)}, u32[]{:S(2)}) collective-permute-start(f32[2,128,256]{2,1,0:T(8,128)S(1)} %get-tuple-element.67), channel_id=1, source_target_pairs={{0,1},{1,2},{2,3},{3,4},{4,5},{5,6},{6,7},{7,8},{8,9},{9,10},{10,1... | collective-permute-start | bytes 786440 | tf_op jit(solution)/shard_map/ppermute | solution.py:127
  8.8 25.3 %collective-permute-start.4 = (f32[2,128,256]{2,1,0:T(8,128)S(1)}, f32[2,128,256]{2,1,0:T(8,128)S(1)}, u32[]{:S(2)}, u32[]{:S(2)}) collective-permute-start(f32[2,128,256]{2,1,0:T(8,128)S(1)} %get-tuple-element.68), channel_id=1, source_target_pairs={{0,257},{1,258},{2,259},{3,260},{4,261},{5,262},{6,263},{7,264},{8... | collective-permute-start | bytes 786440 | tf_op jit(solution)/shard_map/ppermute | solution.py:127
  13.5 0.7 %copy-start.2 = (s32[1,1,1,2,12]{4,3,2,1,0:T(2,128)S(1)}, s32[1,1,1,2,12]{4,3,2,1,0:T(2,128)}, u32[]{:S(2)}) copy-start(s32[1,1,1,2,12]{4,3,2,1,0:T(2,128)} %param.16) | copy-start | bytes 292
  13.5 0.7 %copy-start.3 = (s32[1,1,1,2,12]{4,3,2,1,0:T(2,128)S(1)}, s32[1,1,1,2,12]{4,3,2,1,0:T(2,128)}, u32[]{:S(2)}) copy-start(s32[1,1,1,2,12]{4,3,2,1,0:T(2,128)} %param.17) | copy-start | bytes 292
  13.5 0.7 %copy-start.1 = (s32[1,1,1,2,12]{4,3,2,1,0:T(2,128)S(1)}, s32[1,1,1,2,12]{4,3,2,1,0:T(2,128)}, u32[]{:S(2)}) copy-start(s32[1,1,1,2,12]{4,3,2,1,0:T(2,128)} %param.15) | copy-start | bytes 292
  13.5 0.7 %copy-start.4 = (s32[1,1,1,2]{3,2,1,0:T(1,128)S(1)}, s32[1,1,1,2]{3,2,1,0:T(1,128)}, u32[]{:S(2)}) copy-start(s32[1,1,1,2]{3,2,1,0:T(1,128)} %param.18) | copy-start | bytes 28
  14.2 13.7 %collective-permute-start.1 = (f32[2,256,256]{2,1,0:T(8,128)}, f32[2,256,256]{2,1,0:T(8,128)S(1)}, u32[]{:S(2)}, u32[]{:S(2)}) collective-permute-start(f32[2,256,256]{2,1,0:T(8,128)} %get-tuple-element.49), channel_id=1, source_target_pairs={{31,63},{63,95},{95,127},{127,159},{159,191},{191,223},{223,255},{... | collective-permute-start | bytes 1572872 | tf_op jit(solution)/shard_map/cond/branch_1_fun/ppermute | solution.py:127
  16.7 11.1 %collective-permute-start = (f32[528,256]{1,0:T(8,128)S(1)}, f32[528,256]{1,0:T(8,128)S(1)}, u32[]{:S(2)}, u32[]{:S(2)}) collective-permute-start(f32[528,256]{1,0:T(8,128)S(1)} %get-tuple-element.42), channel_id=1, source_target_pairs={{0,256},{1,257},{2,258},{3,259},{4,260},{5,261},{6,262},{7,263},{8... | collective-permute-start | bytes 1622024 | tf_op jit(solution)/shard_map/cond/branch_1_fun/cond/branch_1_fun/ppermute | solution.py:127
  29.1 4.7 %collective-permute-start.2 = (f32[2,256,256]{2,1,0:T(8,128)S(1)}, f32[2,256,256]{2,1,0:T(8,128)S(1)}, u32[]{:S(2)}, u32[]{:S(2)}) collective-permute-start(f32[2,256,256]{2,1,0:T(8,128)S(1)} %broadcast_select_fusion.right_own), channel_id=1, source_target_pairs={{0,256},{1,257},{2,258},{3,259},{4,260},{5,261},{6,262},{7,263},{8... | collective-permute-start | bytes 1572872 | tf_op jit(solution)/shard_map/cond/branch_1_fun/ppermute | solution.py:127
  34.8 8.4 %collective-permute-start.6 = (f32[128,256]{1,0:T(8,128)S(1)}, f32[128,256]{1,0:T(8,128)S(1)}, u32[]{:S(2)}, u32[]{:S(2)}) collective-permute-start(f32[128,256]{1,0:T(8,128)S(1)} %get-tuple-element.74), channel_id=1, source_target_pairs={{0,512},{1,513},{2,514},{3,515},{4,516},{5,517},{6,518},{7,519},{8... | collective-permute-start | bytes 393224 | tf_op jit(solution)/shard_map/ppermute | solution.py:127
  37.9 7.2 %collective-permute-start.7 = (f32[128,256]{1,0:T(8,128)S(1)}, f32[128,256]{1,0:T(8,128)S(1)}, u32[]{:S(2)}, u32[]{:S(2)}) collective-permute-start(f32[128,256]{1,0:T(8,128)S(1)} %get-tuple-element.75), channel_id=1, source_target_pairs={{0,768},{1,769},{2,770},{3,771},{4,772},{5,773},{6,774},{7,775},{8... | collective-permute-start | bytes 393224 | tf_op jit(solution)/shard_map/ppermute | solution.py:127
  40.5 4.5 %collective-permute-start.8 = (f32[128,256]{1,0:T(8,128)S(1)}, f32[128,256]{1,0:T(8,128)S(1)}, u32[]{:S(2)}, u32[]{:S(2)}) collective-permute-start(f32[128,256]{1,0:T(8,128)S(1)} %get-tuple-element.76), channel_id=1, source_target_pairs={{0,256},{1,257},{2,258},{3,259},{4,260},{5,261},{6,262},{7,263},{8... | collective-permute-start | bytes 393224 | tf_op jit(solution)/shard_map/ppermute | solution.py:127

commit v6 on v5

--- a/solution.py
+++ b/solution.py
@@ -72,11 +72,16 @@
     weights[16:] = heard[size:, :]
 
 
-def split_kernel(left, same, cross):
+def split_kernel(left, same, cross, held, sems):
     side = lax.axis_index("layer") & 1
     half = same.shape[1]
-    for out, begin in ((same, side * half), (cross, (1 - side) * half)):
-        out[...] = left[:, pl.ds(pl.multiple_of(begin, half), half)]
+    copies = [pltpu.make_async_copy(left.at[slot], held.at[slot], sems.at[slot]) for slot in range(2)]
+    for copy in copies:
+        copy.start()
+    for slot in range(2):
+        copies[slot].wait()
+        for out, begin in ((same, side * half), (cross, (1 - side) * half)):
+            out[slot] = held[slot, pl.ds(pl.multiple_of(begin, half), half)]
 
 
 def hold_kernel(*refs):
@@ -140,8 +145,9 @@
     pieces = pl.pallas_call(
         split_kernel,
         out_shape=(jax.ShapeDtypeStruct((slots, half, cols), f32),) * 2,
-        in_specs=[vmem],
+        in_specs=[anywhere],
         out_specs=(vmem,) * 2,
+        scratch_shapes=[pltpu.VMEM((slots, rows, cols), f32), pltpu.SemaphoreType.DMA((2,))],
         compiler_params=PARAMS,
         cost_estimate=pl.CostEstimate(flops=1 << 10, bytes_accessed=1 << 20, transcendentals=0),
         name="split",
@@ -211,6 +217,7 @@
         )(right_own, right_mate)
 
     base, weights, right_rest = guarded(beside, left, right)
+    (right_first,) = hold(right_first)
     right_high, right_low = guarded(middle, right_first, right_rest)
     own, core_out, chip_out, far_out = pl.pallas_call(
         second_kernel,

time: 46.3 us -> 45.3 us (0.978)
  other arithmetic: 1.12 us -> 0.07 us
    select_n x1, other arithmetic: 1.12 us -> 0.07 us  [middle(): jnp.where(lax.axis_index('col') == last_col, right_rest, right_first)]
    ppermute x9, starting transfers between devices: 33.5 us -> 33.1 us  [permute(): return lax.ppermute(value, names, pairs)]
  transfers between devices with their start and end apart: 9 -> 9, of which waited for: 4 -> 4; matrix products, arithmetic and copies ran while one was open for 2% -> 0% of each run, Pallas kernels for 7% -> 7%
where the time goes in v6:
time: 45.3 us; the launch traced here: 44.9 us
  starting transfers between devices  33.1 us (73%)
  waiting for transfers between devices  5.47 us (12%)
  Pallas kernels  4.71 us (10%)
  between operations  0.79 us (2%)
  local copies, waits for them, and re-layouts  0.68 us (2%)
    ppermute x9, starting transfers between devices, permute(): return lax.ppermute(value, names, pairs)  33.1 us
    ppermute x9, waiting for transfers between devices, permute(): return lax.ppermute(value, names, pairs)  5.47 us
    pallas_call x1, Pallas kernels, early(): pl.pallas_call(first_kernel, out_shape=(jax.ShapeDtypeStruct((4 * half +...  1.91 us
    pallas_call x1, Pallas kernels, local(): pl.pallas_call(split_kernel, out_shape=(jax.ShapeDtypeStruct((slots, half...  1.07 us
  transfers between devices with their start and end apart: 9, of which 4 were waited for; matrix products, arithmetic and copies ran while one was open for 0% of the time, Pallas kernels for 7%

profile of v6, /device:TPU:1, one launch (start us, length us, event | category | flops | bytes accessed | tf_op | source)
XLA Modules:
  0.0 44.9 jit_solution(12646947463186001037)
XLA Ops:
  0.0 4.0 %collective-permute-start.5 = (f32[2,256,256]{2,1,0:T(8,128)}, f32[2,256,256]{2,1,0:T(8,128)S(1)}, u32[]{:S(2)}, u32[]{:S(2)}) collective-permute-start(f32[2,256,256]{2,1,0:T(8,128)} %bitcast.5), channel_id=1, source_target_pairs={{0,32},{1,33},{2,34},{3,35},{4,36},{5,37},{6,38},{7,39},{8,40},{9,... | collective-permute-start | bytes 1572872 | tf_op jit(solution)/shard_map/ppermute | solution.py:132
  4.0 1.1 %split.1 = (f32[2,128,256]{2,1,0:T(8,128)S(1)}, f32[2,128,256]{2,1,0:T(8,128)S(1)}) custom-call(f32[2,256,256]{2,1,0:T(8,128)} %bitcast.3), custom_call_target="tpu_custom_call" | custom-call | flops 1024 | bytes 1048576 | tf_op jit(solution)/shard_map/split/pallas_call | solution.py:145
  5.1 3.5 %collective-permute-start.3 = (f32[2,128,256]{2,1,0:T(8,128)S(1)}, f32[2,128,256]{2,1,0:T(8,128)S(1)}, u32[]{:S(2)}, u32[]{:S(2)}) collective-permute-start(f32[2,128,256]{2,1,0:T(8,128)S(1)} %get-tuple-element.67), channel_id=1, source_target_pairs={{0,1},{1,2},{2,3},{3,4},{4,5},{5,6},{6,7},{7,8},{8,9},{9,10},{10,1... | collective-permute-start | bytes 786440 | tf_op jit(solution)/shard_map/ppermute | solution.py:132
  8.7 4.7 %collective-permute-start.4 = (f32[2,128,256]{2,1,0:T(8,128)S(1)}, f32[2,128,256]{2,1,0:T(8,128)S(1)}, u32[]{:S(2)}, u32[]{:S(2)}) collective-permute-start(f32[2,128,256]{2,1,0:T(8,128)S(1)} %get-tuple-element.68), channel_id=1, source_target_pairs={{0,257},{1,258},{2,259},{3,260},{4,261},{5,262},{6,263},{7,264},{8... | collective-permute-start | bytes 786440 | tf_op jit(solution)/shard_map/ppermute | solution.py:132
  13.3 0.0 copy-start.1
  13.3 0.0 copy-start.2
  13.4 0.0 copy-start
  13.4 0.0 copy-start.3
  13.4 0.6 %copy-done.1 = s32[1,1,1,2,12]{4,3,2,1,0:T(2,128)S(1)} copy-done((s32[1,1,1,2,12]{4,3,2,1,0:T(2,128)S(1)}, s32[1,1,1,2,12]{4,3,2,1,0:T(2,128)}, u32[]{:S(2)}) %copy-start.1) | copy-done | bytes 120
  14.0 0.0 copy-done.2
  14.0 0.0 copy-done
  14.0 0.0 copy-done.3
  14.1 13.9 %conditional.3 = (f32[512,256]{1,0:T(8,128)S(1)}, f32[32,256]{1,0:T(8,128)S(1)}, f32[2,256,256]{2,1,0:T(8,128)S(1)}) conditional(s32[]{:T(128)} %convert_element_type.7, () %tuple.28, (pred[]{:T(512)}, s32[1,1,1,2,12]{4,3,2,1,0:T(2,128)S(1)}, s32[1,1,1,2,12]{4,3,2,1,0:T(2,128)S(1)}, s32[1,1,1,2,12]{4,3,2,1,0:T(2,128)S(1)}, ...), branch_computations={%region_0.0_spmd, %region_1.0_spmd} | conditional | flops 403046400 | bytes 10027173 | solution.py:164
  14.1 0.7 %collective-permute-start.1 = (f32[2,256,256]{2,1,0:T(8,128)}, f32[2,256,256]{2,1,0:T(8,128)S(1)}, u32[]{:S(2)}, u32[]{:S(2)}) collective-permute-start(f32[2,256,256]{2,1,0:T(8,128)} %get-tuple-element.49), channel_id=1, source_target_pairs={{31,63},{63,95},{95,127},{127,159},{159,191},{191,223},{223,255},{... | collective-permute-start | bytes 1572872 | tf_op jit(solution)/shard_map/cond/branch_1_fun/ppermute | solution.py:132
  14.7 13.1 %conditional = ((f32[512,256]{1,0:T(8,128)S(1)}, f32[32,256]{1,0:T(8,128)S(1)})) conditional(s32[]{:T(128)} %convert_element_type.1, () %tuple.19, (s32[1,1,1,2,12]{4,3,2,1,0:T(2,128)S(1)}, s32[1,1,1,2,12]{4,3,2,1,0:T(2,128)S(1)}, s32[1,1,1,2,12]{4,3,2,1,0:T(2,128)S(1)}, s32[1,1,1,2]{3,2,1,0:T(1,128)S(1)}, f32[2,256,256]{2,1,0:T(8,128)}, ...), branch_computations={%region_2.0_spmd, %region_3.0_spmd} | conditional | flops 402784256 | bytes 5832752 | solution.py:164
  14.8 1.9 %first_step.1 = (f32[528,256]{1,0:T(8,128)S(1)}, f32[528,256]{1,0:T(8,128)S(1)}) custom-call(s32[1,1,1,2,12]{4,3,2,1,0:T(2,128)S(1)} %get-tuple-element.35.li, s32[1,1,1,2,12]{4,3,2,1,0:T(2,128)S(1)} %get-tuple-element.36.ri, s32[1,1,1,2,12]{4,3,2,1,0:T(2,128)S(1)} %get-tuple-element.37.ti, s32[1,1,1,2]{3,2,1,0:T(1,128)S(1)} %get-tuple-element.38.counts, ...), custom_call_target="tpu_custom_call" | custom-call | flops 402653184 | bytes 2097152 | tf_op jit(solution)/shard_map/cond/branch_1_fun/cond/branch_1_fun/first_step/pallas_call | solution.py:178
  16.7 9.6 %collective-permute-start = (f32[528,256]{1,0:T(8,128)S(1)}, f32[528,256]{1,0:T(8,128)S(1)}, u32[]{:S(2)}, u32[]{:S(2)}) collective-permute-start(f32[528,256]{1,0:T(8,128)S(1)} %get-tuple-element.42), channel_id=1, source_target_pairs={{0,256},{1,257},{2,258},{3,259},{4,260},{5,261},{6,262},{7,263},{8... | collective-permute-start | bytes 1622024 | tf_op jit(solution)/shard_map/cond/branch_1_fun/cond/branch_1_fun/ppermute | solution.py:132
  26.3 1.5 %collective-permute-done.heard = f32[528,256]{1,0:T(8,128)S(1)} collective-permute-done((f32[528,256]{1,0:T(8,128)S(1)}, f32[528,256]{1,0:T(8,128)S(1)}, u32[]{:S(2)}, u32[]{:S(2)}) %collective-permute-start) | collective-permute-done | bytes 540704 | tf_op jit(solution)/shard_map/cond/branch_1_fun/cond/branch_1_fun/ppermute | solution.py:132
  27.8 0.1 join.1
  27.9 0.0 collective-permute-done.1.refs_0_
  28.0 0.0 collective-permute-done.5.refs_0_
  28.0 4.8 %conditional.4 = ((bf16[4,256,256]{2,1,0:T(8,128)(2,1)S(1)}, bf16[4,256,256]{2,1,0:T(8,128)(2,1)S(1)})) conditional(s32[]{:T(128)} %convert_element_type.7, () %tuple.27, (f32[2,256,256]{2,1,0:T(8,128)S(1)}, f32[2,256,256]{2,1,0:T(8,128)S(1)}) %tuple.30), branch_computations={%region_4.0_spmd, %region_5.6_spmd} | conditional | flops 1179651 | bytes 5767246 | solution.py:164
  28.0 0.1 broadcast_select_fusion.right_own
  28.1 3.0 %collective-permute-start.2 = (f32[2,256,256]{2,1,0:T(8,128)S(1)}, f32[2,256,256]{2,1,0:T(8,128)S(1)}, u32[]{:S(2)}, u32[]{:S(2)}) collective-permute-start(f32[2,256,256]{2,1,0:T(8,128)S(1)} %broadcast_select_fusion.right_own), channel_id=1, source_target_pairs={{0,256},{1,257},{2,258},{3,259},{4,260},{5,261},{6,262},{7,263},{8... | collective-permute-start | bytes 1572872 | tf_op jit(solution)/shard_map/cond/branch_1_fun/ppermute | solution.py:132
  31.1 1.5 %collective-permute-done.2.right_mate = f32[2,256,256]{2,1,0:T(8,128)S(1)} collective-permute-done((f32[2,256,256]{2,1,0:T(8,128)S(1)}, f32[2,256,256]{2,1,0:T(8,128)S(1)}, u32[]{:S(2)}, u32[]{:S(2)}) %collective-permute-start.2) | collective-permute-done | bytes 524320 | tf_op jit(solution)/shard_map/cond/branch_1_fun/ppermute | solution.py:132
  32.6 0.2 ready.1
  32.8 0.0 collective-permute-done.3.left_own
  32.8 0.4 collective-permute-done.4.left_mate
  33.2 0.7 %second_step.1 = (f32[128,256]{1,0:T(8,128)S(1)}, f32[128,256]{1,0:T(8,128)S(1)}, f32[128,256]{1,0:T(8,128)S(1)}, f32[128,256]{1,0:T(8,128)S(1)}) custom-call(f32[2,128,256]{2,1,0:T(8,128)S(1)} %collective-permute-done.3.left_own, f32[2,128,256]{2,1,0:T(8,128)S(1)} %collective-permute-done.4.left_mate, ...), custom_call_target="tpu_custom_call" | custom-call | flops 402653184 | bytes 3145728 | tf_op jit(solution)/shard_map/second_step/pallas_call | solution.py:222
  33.9 3.1 %collective-permute-start.6 = (f32[128,256]{1,0:T(8,128)S(1)}, f32[128,256]{1,0:T(8,128)S(1)}, u32[]{:S(2)}, u32[]{:S(2)}) collective-permute-start(f32[128,256]{1,0:T(8,128)S(1)} %get-tuple-element.74), channel_id=1, source_target_pairs={{0,512},{1,513},{2,514},{3,515},{4,516},{5,517},{6,518},{7,519},{8... | collective-permute-start | bytes 393224 | tf_op jit(solution)/shard_map/ppermute | solution.py:132
  37.0 2.3 %collective-permute-start.7 = (f32[128,256]{1,0:T(8,128)S(1)}, f32[128,256]{1,0:T(8,128)S(1)}, u32[]{:S(2)}, u32[]{:S(2)}) collective-permute-start(f32[128,256]{1,0:T(8,128)S(1)} %get-tuple-element.75), channel_id=1, source_target_pairs={{0,768},{1,769},{2,770},{3,771},{4,772},{5,773},{6,774},{7,775},{8... | collective-permute-start | bytes 393224 | tf_op jit(solution)/shard_map/ppermute | solution.py:132
  39.3 2.1 %collective-permute-start.8 = (f32[128,256]{1,0:T(8,128)S(1)}, f32[128,256]{1,0:T(8,128)S(1)}, u32[]{:S(2)}, u32[]{:S(2)}) collective-permute-start(f32[128,256]{1,0:T(8,128)S(1)} %get-tuple-element.76), channel_id=1, source_target_pairs={{0,256},{1,257},{2,258},{3,259},{4,260},{5,261},{6,262},{7,263},{8... | collective-permute-start | bytes 393224 | tf_op jit(solution)/shard_map/ppermute | solution.py:132
  42.1 0.0 collective-permute-done.6.chip
  42.1 2.0 %collective-permute-done.7.far = f32[128,256]{1,0:T(8,128)S(1)} collective-permute-done((f32[128,256]{1,0:T(8,128)S(1)}, f32[128,256]{1,0:T(8,128)S(1)}, u32[]{:S(2)}, u32[]{:S(2)}) %collective-permute-start.7) | collective-permute-done | bytes 131104 | tf_op jit(solution)/shard_map/ppermute | solution.py:132
  44.1 0.0 collective-permute-done.8.core
  44.1 0.7 %last_sum.1 = f32[256,256]{1,0:T(8,128)} custom-call(s32[1,1,1]{2,1,0:T(1,128)S(6)} %copy.26.mask, f32[128,256]{1,0:T(8,128)S(1)} %collective-permute-done.6.chip, f32[128,256]{1,0:T(8,128)S(1)} %collective-permute-done.7.far, f32[128,256]{1,0:T(8,128)S(1)} %collective-permute-done.8.core, f32[128,256]{1,0:T(8,128)S(1)} %get-tuple-element.77.own), custom_call_target="tpu_custom_call" | custom-call | flops 262144 | bytes 1048576 | tf_op jit(solution)/shard_map/last_sum/pallas_call | solution.py:234
  (3 shorter events, 0.1 us)
Async XLA Ops:
  0.0 28.0 %collective-permute-start.5 = (f32[2,256,256]{2,1,0:T(8,128)}, f32[2,256,256]{2,1,0:T(8,128)S(1)}, u32[]{:S(2)}, u32[]{:S(2)}) collective-permute-start(f32[2,256,256]{2,1,0:T(8,128)} %bitcast.5), channel_id=1, source_target_pairs={{0,32},{1,33},{2,34},{3,35},{4,36},{5,37},{6,38},{7,39},{8,40},{9,... | collective-permute-start | bytes 1572872 | tf_op jit(solution)/shard_map/ppermute | solution.py:132
  5.1 27.7 %collective-permute-start.3 = (f32[2,128,256]{2,1,0:T(8,128)S(1)}, f32[2,128,256]{2,1,0:T(8,128)S(1)}, u32[]{:S(2)}, u32[]{:S(2)}) collective-permute-start(f32[2,128,256]{2,1,0:T(8,128)S(1)} %get-tuple-element.67), channel_id=1, source_target_pairs={{0,1},{1,2},{2,3},{3,4},{4,5},{5,6},{6,7},{7,8},{8,9},{9,10},{10,1... | collective-permute-start | bytes 786440 | tf_op jit(solution)/shard_map/ppermute | solution.py:132
  8.7 24.5 %collective-permute-start.4 = (f32[2,128,256]{2,1,0:T(8,128)S(1)}, f32[2,128,256]{2,1,0:T(8,128)S(1)}, u32[]{:S(2)}, u32[]{:S(2)}) collective-permute-start(f32[2,128,256]{2,1,0:T(8,128)S(1)} %get-tuple-element.68), channel_id=1, source_target_pairs={{0,257},{1,258},{2,259},{3,260},{4,261},{5,262},{6,263},{7,264},{8... | collective-permute-start | bytes 786440 | tf_op jit(solution)/shard_map/ppermute | solution.py:132
  13.3 0.7 %copy-start.1 = (s32[1,1,1,2,12]{4,3,2,1,0:T(2,128)S(1)}, s32[1,1,1,2,12]{4,3,2,1,0:T(2,128)}, u32[]{:S(2)}) copy-start(s32[1,1,1,2,12]{4,3,2,1,0:T(2,128)} %param.16) | copy-start | bytes 292
  13.3 0.7 %copy-start.2 = (s32[1,1,1,2,12]{4,3,2,1,0:T(2,128)S(1)}, s32[1,1,1,2,12]{4,3,2,1,0:T(2,128)}, u32[]{:S(2)}) copy-start(s32[1,1,1,2,12]{4,3,2,1,0:T(2,128)} %param.17) | copy-start | bytes 292
  13.4 0.7 %copy-start = (s32[1,1,1,2,12]{4,3,2,1,0:T(2,128)S(1)}, s32[1,1,1,2,12]{4,3,2,1,0:T(2,128)}, u32[]{:S(2)}) copy-start(s32[1,1,1,2,12]{4,3,2,1,0:T(2,128)} %param.15) | copy-start | bytes 292
  13.4 0.7 %copy-start.3 = (s32[1,1,1,2]{3,2,1,0:T(1,128)S(1)}, s32[1,1,1,2]{3,2,1,0:T(1,128)}, u32[]{:S(2)}) copy-start(s32[1,1,1,2]{3,2,1,0:T(1,128)} %param.18) | copy-start | bytes 28
  14.1 13.9 %collective-permute-start.1 = (f32[2,256,256]{2,1,0:T(8,128)}, f32[2,256,256]{2,1,0:T(8,128)S(1)}, u32[]{:S(2)}, u32[]{:S(2)}) collective-permute-start(f32[2,256,256]{2,1,0:T(8,128)} %get-tuple-element.49), channel_id=1, source_target_pairs={{31,63},{63,95},{95,127},{127,159},{159,191},{191,223},{223,255},{... | collective-permute-start | bytes 1572872 | tf_op jit(solution)/shard_map/cond/branch_1_fun/ppermute | solution.py:132
  16.7 11.1 %collective-permute-start = (f32[528,256]{1,0:T(8,128)S(1)}, f32[528,256]{1,0:T(8,128)S(1)}, u32[]{:S(2)}, u32[]{:S(2)}) collective-permute-start(f32[528,256]{1,0:T(8,128)S(1)} %get-tuple-element.42), channel_id=1, source_target_pairs={{0,256},{1,257},{2,258},{3,259},{4,260},{5,261},{6,262},{7,263},{8... | collective-permute-start | bytes 1622024 | tf_op jit(solution)/shard_map/cond/branch_1_fun/cond/branch_1_fun/ppermute | solution.py:132
  28.1 4.5 %collective-permute-start.2 = (f32[2,256,256]{2,1,0:T(8,128)S(1)}, f32[2,256,256]{2,1,0:T(8,128)S(1)}, u32[]{:S(2)}, u32[]{:S(2)}) collective-permute-start(f32[2,256,256]{2,1,0:T(8,128)S(1)} %broadcast_select_fusion.right_own), channel_id=1, source_target_pairs={{0,256},{1,257},{2,258},{3,259},{4,260},{5,261},{6,262},{7,263},{8... | collective-permute-start | bytes 1572872 | tf_op jit(solution)/shard_map/cond/branch_1_fun/ppermute | solution.py:132
  33.9 8.3 %collective-permute-start.6 = (f32[128,256]{1,0:T(8,128)S(1)}, f32[128,256]{1,0:T(8,128)S(1)}, u32[]{:S(2)}, u32[]{:S(2)}) collective-permute-start(f32[128,256]{1,0:T(8,128)S(1)} %get-tuple-element.74), channel_id=1, source_target_pairs={{0,512},{1,513},{2,514},{3,515},{4,516},{5,517},{6,518},{7,519},{8... | collective-permute-start | bytes 393224 | tf_op jit(solution)/shard_map/ppermute | solution.py:132
  37.0 7.2 %collective-permute-start.7 = (f32[128,256]{1,0:T(8,128)S(1)}, f32[128,256]{1,0:T(8,128)S(1)}, u32[]{:S(2)}, u32[]{:S(2)}) collective-permute-start(f32[128,256]{1,0:T(8,128)S(1)} %get-tuple-element.75), channel_id=1, source_target_pairs={{0,768},{1,769},{2,770},{3,771},{4,772},{5,773},{6,774},{7,775},{8... | collective-permute-start | bytes 393224 | tf_op jit(solution)/shard_map/ppermute | solution.py:132
  39.3 4.8 %collective-permute-start.8 = (f32[128,256]{1,0:T(8,128)S(1)}, f32[128,256]{1,0:T(8,128)S(1)}, u32[]{:S(2)}, u32[]{:S(2)}) collective-permute-start(f32[128,256]{1,0:T(8,128)S(1)} %get-tuple-element.76), channel_id=1, source_target_pairs={{0,256},{1,257},{2,258},{3,259},{4,260},{5,261},{6,262},{7,263},{8... | collective-permute-start | bytes 393224 | tf_op jit(solution)/shard_map/ppermute | solution.py:132

commit v7 on v4

--- a/solution.py
+++ b/solution.py
@@ -72,6 +72,17 @@
     weights[16:] = heard[size:, :]
 
 
+def cut_kernel(flip, left, piece, sems):
+    half = piece.shape[1]
+    side = (lax.axis_index("layer") & 1) ^ flip
+    rows = pl.ds(pl.multiple_of(side * half, half), half)
+    copies = [pltpu.make_async_copy(left.at[slot, rows], piece.at[slot], sems.at[slot]) for slot in range(2)]
+    for copy in copies:
+        copy.start()
+    for copy in copies:
+        copy.wait()
+
+
 def hold_kernel(*refs):
     for value, out in zip(refs[: len(refs) // 2], refs[len(refs) // 2 :]):
         out[...] = value[...]
@@ -83,13 +94,23 @@
         right_high[slot], right_low[slot] = halves(right)
 
 
-def second_kernel(left_own, left_mate, right_high, right_low, base, weights, *outs):
-    half = left_own.shape[1]
-    own = pair_products(left_own[...], right_high, right_low, (0, 1))
-    mate = pair_products(left_mate[...], right_high, right_low, (2, 3))
+def own_kernel(left, right_high, right_low, weights, base_far, part, base, sem):
+    copy = pltpu.make_async_copy(base_far, base, sem)
+    copy.start()
+    half = left.shape[1]
+    found = pair_products(left[...], right_high, right_low, (0, 1))
+    copy.wait()
+    for j in range(4):
+        rows = slice(j * half, (j + 1) * half)
+        part[rows, :] = combine(found, lambda k: weights[k : k + 1, :], j, base[rows, :])
+
+
+def mate_kernel(left, right_high, right_low, part, weights, *outs):
+    half = left.shape[1]
+    found = pair_products(left[...], right_high, right_low, (2, 3))
     for j in (2, 3, 1, 0):
-        total = combine(own, lambda k: weights[k : k + 1, :], j, base[j * half : (j + 1) * half, :])
-        outs[j][...] = combine(mate, lambda k: weights[16 + k : 17 + k, :], j, total)
+        rows = slice(j * half, (j + 1) * half)
+        outs[j][...] = combine(found, lambda k: weights[16 + k : 17 + k, :], j, part[rows, :])
 
 
 def last_kernel(mask, chip, far, core, own, out, held, sems):
@@ -126,17 +147,27 @@
     slots, rows, cols = left.shape
     half = rows // 2
     f32 = jnp.float32
-    core = lax.axis_index("layer") & 1
     vmem = pl.BlockSpec(memory_space=VMEM)
     smem = pl.BlockSpec(memory_space=SMEM)
     anywhere = pl.BlockSpec(memory_space=pl.ANY)
 
-    def piece(side):
-        return lax.dynamic_slice_in_dim(left, side * half, half, 1, allow_negative_indices=False)
-
-    right_first = permute(right, lambda l, r, c: (l, r + 1, c), lambda l, r, c: c == 0)
-    left_own = permute(piece(core), lambda l, r, c: (l, r, c + 1))
-    left_mate = permute(piece(1 - core), lambda l, r, c: (l ^ 1, r, c + 1))
+    def cut(flip):
+        return pl.pallas_call(
+            functools.partial(cut_kernel, flip),
+            out_shape=jax.ShapeDtypeStruct((slots, half, cols), f32),
+            in_specs=[anywhere],
+            out_specs=vmem,
+            scratch_shapes=[pltpu.SemaphoreType.DMA((2,))],
+            compiler_params=PARAMS,
+            cost_estimate=pl.CostEstimate(flops=1 << 10, bytes_accessed=1 << 19, transcendentals=0),
+            name="cut",
+        )(left)
+
+    last_col = lax.axis_size("col") - 1
+    right_first = permute(right, lambda l, r, c: (l, r + 1, c), lambda l, r, c: c != last_col)
+    same, cross = cut(0), cut(1)
+    left_own = permute(same, lambda l, r, c: (l, r, c + 1))
+    left_mate = permute(cross, lambda l, r, c: (l ^ 1, r, c + 1))
     within = lax.axis_index("layer") < lax.axis_size("layer")
 
     def guarded(branch, *args):
@@ -150,7 +181,7 @@
             in_specs=[vmem] * len(values),
             out_specs=(vmem,) * len(values),
             compiler_params=PARAMS,
-            cost_estimate=pl.CostEstimate(flops=1 << 17, bytes_accessed=1 << 20, transcendentals=0),
+            cost_estimate=pl.CostEstimate(flops=1 << 10, bytes_accessed=1 << 10, transcendentals=0),
             name="hold",
         )(*values)
 
@@ -177,14 +208,14 @@
         )(keep, heard)
 
     def beside(left, right):
-        right_rest = permute(right, lambda l, r, c: (l, r + 1, c), lambda l, r, c: c != 0)
+        right_rest = permute(right, lambda l, r, c: (l, r + 1, c), lambda l, r, c: c == last_col)
         base, weights = guarded(early, left, right)
         base, weights = hold(base, weights)
         (right_rest,) = hold(right_rest)
         return base, weights, right_rest
 
     def middle(right_first, right_rest):
-        right_own = jnp.where(lax.axis_index("col") == 0, right_first, right_rest)
+        right_own = jnp.where(lax.axis_index("col") == last_col, right_rest, right_first)
         right_mate = permute(right_own, lambda l, r, c: (l ^ 1, r, c))
         return pl.pallas_call(
             ready_kernel,
@@ -192,24 +223,36 @@
             in_specs=[vmem] * 2,
             out_specs=(vmem,) * 2,
             compiler_params=PARAMS,
-            cost_estimate=pl.CostEstimate(flops=1 << 20, bytes_accessed=2 << 20, transcendentals=0),
+            cost_estimate=pl.CostEstimate(flops=1 << 10, bytes_accessed=1 << 10, transcendentals=0),
             name="ready",
         )(right_own, right_mate)
 
     base, weights, right_rest = guarded(beside, left, right)
+    (right_first,) = hold(right_first)
     right_high, right_low = guarded(middle, right_first, right_rest)
+    part = pl.pallas_call(
+        own_kernel,
+        out_shape=jax.ShapeDtypeStruct((4 * half, cols), f32),
+        in_specs=[vmem] * 4 + [anywhere],
+        out_specs=vmem,
+        scratch_shapes=[pltpu.VMEM((4 * half, cols), f32), pltpu.SemaphoreType.DMA],
+        compiler_params=PARAMS,
+        cost_estimate=pl.CostEstimate(flops=3 << 26, bytes_accessed=2 << 20, transcendentals=0),
+        name="own_layer",
+    )(left_own, right_high, right_low, weights, base)
     own, core_out, chip_out, far_out = pl.pallas_call(
-        second_kernel,
+        mate_kernel,
         out_shape=(jax.ShapeDtypeStruct((half, cols), f32),) * 4,
-        in_specs=[vmem] * 6,
+        in_specs=[vmem] * 5,
         out_specs=(vmem,) * 4,
         compiler_params=PARAMS,
-        cost_estimate=pl.CostEstimate(flops=6 << 26, bytes_accessed=3 << 20, transcendentals=0),
-        name="second_step",
-    )(left_own, left_mate, right_high, right_low, base, weights)
+        cost_estimate=pl.CostEstimate(flops=3 << 26, bytes_accessed=2 << 20, transcendentals=0),
+        name="mate_layer",
+    )(left_mate, right_high, right_low, part, weights)
     chip_in = permute(chip_out, lambda l, r, c: (l ^ 2, r, c))
     far_in = permute(far_out, lambda l, r, c: (l ^ 3, r, c))
     core_in = permute(core_out, lambda l, r, c: (l ^ 1, r, c))
+    chip_in, far_in = hold(chip_in, far_in)
     result = pl.pallas_call(
         last_kernel,
         out_shape=jax.ShapeDtypeStruct((rows, cols), f32),

time: 49.1 us -> 46.1 us (0.939)
  the two profiles are of different devices: /device:TPU:353 before, /device:TPU:1 now
where the time goes in v7:
time: 46.1 us; the launch traced here: 45.7 us
  starting transfers between devices  32.7 us (71%)
  Pallas kernels  6.8 us (15%)
  waiting for transfers between devices  4.57 us (10%)
  between operations  0.84 us (2%)
  local copies, waits for them, and re-layouts  0.66 us (1%)
    ppermute x9, starting transfers between devices, permute(): return lax.ppermute(value, names, pairs)  32.7 us
    ppermute x9, waiting for transfers between devices, permute(): return lax.ppermute(value, names, pairs)  4.57 us
    pallas_call x1, Pallas kernels, early(): pl.pallas_call(first_kernel, out_shape=(jax.ShapeDtypeStruct((4 * half +...  1.75 us
    pallas_call x2, Pallas kernels, cut(): pl.pallas_call(functools.partial(cut_kernel, flip), out_shape=jax.ShapeDt...  1.37 us
    pallas_call x1, Pallas kernels, local(): pl.pallas_call(own_kernel, out_shape=jax.ShapeDtypeStruct((4 * half, cols...  1.33 us
    pallas_call x4, Pallas kernels, hold(): pl.pallas_call(hold_kernel, out_shape=tuple((jax.ShapeDtypeStruct(v.shape...  0.93 us
  transfers between devices with their start and end apart: 9, of which 3 were waited for; matrix products, arithmetic and copies ran while one was open for 0% of the time, Pallas kernels for 12%

profile of v7, /device:TPU:1, one launch (start us, length us, event | category | flops | bytes accessed | tf_op | source)
XLA Modules:
  0.0 45.7 jit_solution(1552785838238887992)
XLA Ops:
  0.0 0.0 copy-start
  0.0 4.2 %collective-permute-start.4 = (f32[2,256,256]{2,1,0:T(8,128)}, f32[2,256,256]{2,1,0:T(8,128)S(1)}, u32[]{:S(2)}, u32[]{:S(2)}) collective-permute-start(f32[2,256,256]{2,1,0:T(8,128)} %bitcast.1), channel_id=1, source_target_pairs={{0,32},{1,33},{2,34},{3,35},{4,36},{5,37},{6,38},{7,39},{8,40},{9,... | collective-permute-start | bytes 1572872 | tf_op jit(solution)/shard_map/ppermute | solution.py:141
  4.2 1.0 %cut.3 = f32[2,128,256]{2,1,0:T(8,128)S(1)} custom-call(f32[2,256,256]{2,1,0:T(8,128)} %bitcast.3), custom_call_target="tpu_custom_call" | custom-call | flops 1024 | bytes 524288 | tf_op jit(solution)/shard_map/cut/pallas_call | solution.py:155
  5.2 3.5 %collective-permute-start.5 = (f32[2,128,256]{2,1,0:T(8,128)S(1)}, f32[2,128,256]{2,1,0:T(8,128)S(1)}, u32[]{:S(2)}, u32[]{:S(2)}) collective-permute-start(f32[2,128,256]{2,1,0:T(8,128)S(1)} %cut.3), channel_id=1, source_target_pairs={{0,1},{1,2},{2,3},{3,4},{4,5},{5,6},{6,7},{7,8},{8,9},{9,10},{10,1... | collective-permute-start | bytes 786440 | tf_op jit(solution)/shard_map/ppermute | solution.py:141
  8.7 0.0 copy-done
  8.7 0.0 copy-start.2
  8.7 0.0 copy-start.3
  8.8 0.4 cut.2
  9.1 4.7 %collective-permute-start.3 = (f32[2,128,256]{2,1,0:T(8,128)S(1)}, f32[2,128,256]{2,1,0:T(8,128)S(1)}, u32[]{:S(2)}, u32[]{:S(2)}) collective-permute-start(f32[2,128,256]{2,1,0:T(8,128)S(1)} %cut.2), channel_id=1, source_target_pairs={{0,257},{1,258},{2,259},{3,260},{4,261},{5,262},{6,263},{7,264},{8... | collective-permute-start | bytes 786440 | tf_op jit(solution)/shard_map/ppermute | solution.py:141
  13.8 0.0 copy-start.1
  13.8 0.0 copy-start.4
  13.8 0.0 copy-done.2
  13.8 0.0 copy-done.3
  13.9 0.6 %copy-done.1 = s32[1,1,1,2,12]{4,3,2,1,0:T(2,128)S(1)} copy-done((s32[1,1,1,2,12]{4,3,2,1,0:T(2,128)S(1)}, s32[1,1,1,2,12]{4,3,2,1,0:T(2,128)}, u32[]{:S(2)}) %copy-start.1) | copy-done | bytes 120
  14.5 0.0 copy-done.4
  14.5 14.5 %conditional.3 = (f32[512,256]{1,0:T(8,128)}, f32[32,256]{1,0:T(8,128)S(1)}, f32[2,256,256]{2,1,0:T(8,128)S(1)}) conditional(s32[]{:T(128)} %convert_element_type.7, () %tuple.28, (pred[]{:T(512)}, s32[1,1,1,2,12]{4,3,2,1,0:T(2,128)S(1)}, s32[1,1,1,2,12]{4,3,2,1,0:T(2,128)S(1)}, s32[1,1,1,2,12]{4,3,2,1,0:T(2,128)S(1)}, s32[1,1,1,2]{3,2,1,0:T(1,128)S(1)}, ...), branch_computations={%region_0.0_spmd, %region_1.0_spmd} | conditional | flops 402786304 | bytes 7932069 | solution.py:175
  14.5 0.7 %collective-permute-start.1 = (f32[2,256,256]{2,1,0:T(8,128)}, f32[2,256,256]{2,1,0:T(8,128)S(1)}, u32[]{:S(2)}, u32[]{:S(2)}) collective-permute-start(f32[2,256,256]{2,1,0:T(8,128)} %get-tuple-element.49), channel_id=1, source_target_pairs={{31,63},{63,95},{95,127},{127,159},{159,191},{191,223},{223,255},{... | collective-permute-start | bytes 1572872 | tf_op jit(solution)/shard_map/cond/branch_1_fun/ppermute | solution.py:141
  15.2 13.0 %conditional = ((f32[512,256]{1,0:T(8,128)S(1)}, f32[32,256]{1,0:T(8,128)S(1)})) conditional(s32[]{:T(128)} %convert_element_type.1, () %tuple.19, (s32[1,1,1,2,12]{4,3,2,1,0:T(2,128)S(1)}, s32[1,1,1,2,12]{4,3,2,1,0:T(2,128)S(1)}, s32[1,1,1,2,12]{4,3,2,1,0:T(2,128)S(1)}, s32[1,1,1,2]{3,2,1,0:T(1,128)S(1)}, f32[2,256,256]{2,1,0:T(8,128)S(1)}, ...), branch_computations={%region_2.0_spmd, %region_3.0_spmd} | conditional | flops 402784256 | bytes 5832752 | solution.py:175
  15.2 1.8 %first_step.1 = (f32[528,256]{1,0:T(8,128)S(1)}, f32[528,256]{1,0:T(8,128)S(1)}) custom-call(s32[1,1,1,2,12]{4,3,2,1,0:T(2,128)S(1)} %get-tuple-element.35.li, s32[1,1,1,2,12]{4,3,2,1,0:T(2,128)S(1)} %get-tuple-element.36.ri, s32[1,1,1,2,12]{4,3,2,1,0:T(2,128)S(1)} %get-tuple-element.37.ti, s32[1,1,1,2]{3,2,1,0:T(1,128)S(1)} %get-tuple-element.38.counts, ...), custom_call_target="tpu_custom_call" | custom-call | flops 402653184 | bytes 2097152 | tf_op jit(solution)/shard_map/cond/branch_1_fun/cond/branch_1_fun/first_step/pallas_call | solution.py:189
  17.0 9.6 %collective-permute-start = (f32[528,256]{1,0:T(8,128)S(1)}, f32[528,256]{1,0:T(8,128)S(1)}, u32[]{:S(2)}, u32[]{:S(2)}) collective-permute-start(f32[528,256]{1,0:T(8,128)S(1)} %get-tuple-element.42), channel_id=1, source_target_pairs={{0,256},{1,257},{2,258},{3,259},{4,260},{5,261},{6,262},{7,263},{8... | collective-permute-start | bytes 1622024 | tf_op jit(solution)/shard_map/cond/branch_1_fun/cond/branch_1_fun/ppermute | solution.py:141
  26.5 1.5 %collective-permute-done.heard = f32[528,256]{1,0:T(8,128)S(1)} collective-permute-done((f32[528,256]{1,0:T(8,128)S(1)}, f32[528,256]{1,0:T(8,128)S(1)}, u32[]{:S(2)}, u32[]{:S(2)}) %collective-permute-start) | collective-permute-done | bytes 540704 | tf_op jit(solution)/shard_map/cond/branch_1_fun/cond/branch_1_fun/ppermute | solution.py:141
  28.1 0.1 join.1
  28.1 0.8 %hold.4 = (f32[512,256]{1,0:T(8,128)}, f32[32,256]{1,0:T(8,128)S(1)}) custom-call(f32[512,256]{1,0:T(8,128)S(1)} %get-tuple-element.50.refs_0_, f32[32,256]{1,0:T(8,128)S(1)} %get-tuple-element.51.refs_1_), custom_call_target="tpu_custom_call" | custom-call | flops 1024 | bytes 1024 | tf_op jit(solution)/shard_map/cond/branch_1_fun/hold/pallas_call | solution.py:178
  29.0 0.0 collective-permute-done.1.refs_0_
  29.0 0.0 collective-permute-done.4.refs_0_
  29.1 4.1 %conditional.4 = ((bf16[4,256,256]{2,1,0:T(8,128)(2,1)S(1)}, bf16[4,256,256]{2,1,0:T(8,128)(2,1)S(1)})) conditional(s32[]{:T(128)} %convert_element_type.7, () %tuple.27, (f32[2,256,256]{2,1,0:T(8,128)S(1)}, f32[2,256,256]{2,1,0:T(8,128)S(1)}) %tuple.30), branch_computations={%region_4.0_spmd, %region_5.6_spmd} | conditional | flops 132099 | bytes 3671118 | solution.py:175
  29.1 0.1 broadcast_select_fusion.right_own
  29.2 2.3 %collective-permute-start.2 = (f32[2,256,256]{2,1,0:T(8,128)S(1)}, f32[2,256,256]{2,1,0:T(8,128)S(1)}, u32[]{:S(2)}, u32[]{:S(2)}) collective-permute-start(f32[2,256,256]{2,1,0:T(8,128)S(1)} %broadcast_select_fusion.right_own), channel_id=1, source_target_pairs={{0,256},{1,257},{2,258},{3,259},{4,260},{5,261},{6,262},{7,263},{8... | collective-permute-start | bytes 1572872 | tf_op jit(solution)/shard_map/cond/branch_1_fun/ppermute | solution.py:141
  31.5 1.5 %collective-permute-done.2.right_mate = f32[2,256,256]{2,1,0:T(8,128)S(1)} collective-permute-done((f32[2,256,256]{2,1,0:T(8,128)S(1)}, f32[2,256,256]{2,1,0:T(8,128)S(1)}, u32[]{:S(2)}, u32[]{:S(2)}) %collective-permute-start.2) | collective-permute-done | bytes 524320 | tf_op jit(solution)/shard_map/cond/branch_1_fun/ppermute | solution.py:141
  33.0 0.2 ready.1
  33.1 0.0 collective-permute-done.5.left
  33.2 1.3 %own_layer.1.part = f32[512,256]{1,0:T(8,128)S(1)} custom-call(f32[2,128,256]{2,1,0:T(8,128)S(1)} %collective-permute-done.5.left, bf16[4,256,256]{2,1,0:T(8,128)(2,1)S(1)} %get-tuple-element.68.right_high, bf16[4,256,256]{2,1,0:T(8,128)(2,1)S(1)} %get-tuple-element.69.right_low, f32[32,256]{1,0:T(8,128)S(1)} %get-tuple-element.70.weights, ...), custom_call_target="tpu_custom_call" | custom-call | flops 201326592 | bytes 2097152 | tf_op jit(solution)/shard_map/own_layer/pallas_call | solution.py:233
  34.5 0.0 collective-permute-done.3.left
  34.5 0.5 %mate_layer.1 = (f32[128,256]{1,0:T(8,128)S(1)}, f32[128,256]{1,0:T(8,128)S(1)}, f32[128,256]{1,0:T(8,128)S(1)}, f32[128,256]{1,0:T(8,128)S(1)}) custom-call(f32[2,128,256]{2,1,0:T(8,128)S(1)} %collective-permute-done.3.left, bf16[4,256,256]{2,1,0:T(8,128)(2,1)S(1)} %get-tuple-element.68.right_high, bf16[4,256,256]{2,1,0:T(8,128)(2,1)S(1)} %get-tuple-element.69.right_low, ...), custom_call_target="tpu_custom_call" | custom-call | flops 201326592 | bytes 2097152 | tf_op jit(solution)/shard_map/mate_layer/pallas_call | solution.py:243
  35.0 1.9 %collective-permute-start.6 = (f32[128,256]{1,0:T(8,128)S(1)}, f32[128,256]{1,0:T(8,128)S(1)}, u32[]{:S(2)}, u32[]{:S(2)}) collective-permute-start(f32[128,256]{1,0:T(8,128)S(1)} %get-tuple-element.72), channel_id=1, source_target_pairs={{0,512},{1,513},{2,514},{3,515},{4,516},{5,517},{6,518},{7,519},{8... | collective-permute-start | bytes 393224 | tf_op jit(solution)/shard_map/ppermute | solution.py:141
  36.9 3.9 %collective-permute-start.7 = (f32[128,256]{1,0:T(8,128)S(1)}, f32[128,256]{1,0:T(8,128)S(1)}, u32[]{:S(2)}, u32[]{:S(2)}) collective-permute-start(f32[128,256]{1,0:T(8,128)S(1)} %get-tuple-element.73), channel_id=1, source_target_pairs={{0,768},{1,769},{2,770},{3,771},{4,772},{5,773},{6,774},{7,775},{8... | collective-permute-start | bytes 393224 | tf_op jit(solution)/shard_map/ppermute | solution.py:141
  40.8 1.9 %collective-permute-start.8 = (f32[128,256]{1,0:T(8,128)S(1)}, f32[128,256]{1,0:T(8,128)S(1)}, u32[]{:S(2)}, u32[]{:S(2)}) collective-permute-start(f32[128,256]{1,0:T(8,128)S(1)} %get-tuple-element.76), channel_id=1, source_target_pairs={{0,256},{1,257},{2,258},{3,259},{4,260},{5,261},{6,262},{7,263},{8... | collective-permute-start | bytes 393224 | tf_op jit(solution)/shard_map/ppermute | solution.py:141
  43.4 0.0 collective-permute-done.6.refs_0_
  43.4 1.5 %collective-permute-done.7.refs_1_ = f32[128,256]{1,0:T(8,128)S(1)} collective-permute-done((f32[128,256]{1,0:T(8,128)S(1)}, f32[128,256]{1,0:T(8,128)S(1)}, u32[]{:S(2)}, u32[]{:S(2)}) %collective-permute-start.7) | collective-permute-done | bytes 131104 | tf_op jit(solution)/shard_map/ppermute | solution.py:141
  44.9 0.0 collective-permute-done.8.core
  44.9 0.7 %last_sum.1 = f32[256,256]{1,0:T(8,128)} custom-call(s32[1,1,1]{2,1,0:T(1,128)S(6)} %copy.26.mask, f32[128,256]{1,0:T(8,128)S(1)} %get-tuple-element.74.chip, f32[128,256]{1,0:T(8,128)S(1)} %get-tuple-element.75.far, f32[128,256]{1,0:T(8,128)S(1)} %collective-permute-done.8.core, f32[128,256]{1,0:T(8,128)S(1)} %get-tuple-element.77.own), custom_call_target="tpu_custom_call" | custom-call | flops 262144 | bytes 1048576 | tf_op jit(solution)/shard_map/last_sum/pallas_call | solution.py:256
  (3 shorter events, 0.1 us)
Async XLA Ops:
  0.0 8.7 %copy-start = (f32[1,1,1,2,256,256]{5,4,3,2,1,0:T(8,128)S(1)}, f32[1,1,1,2,256,256]{5,4,3,2,1,0:T(8,128)}, u32[]{:S(2)}) copy-start(f32[1,1,1,2,256,256]{5,4,3,2,1,0:T(8,128)} %param.13) | copy-start | bytes 1572868
  0.0 29.0 %collective-permute-start.4 = (f32[2,256,256]{2,1,0:T(8,128)}, f32[2,256,256]{2,1,0:T(8,128)S(1)}, u32[]{:S(2)}, u32[]{:S(2)}) collective-permute-start(f32[2,256,256]{2,1,0:T(8,128)} %bitcast.1), channel_id=1, source_target_pairs={{0,32},{1,33},{2,34},{3,35},{4,36},{5,37},{6,38},{7,39},{8,40},{9,... | collective-permute-start | bytes 1572872 | tf_op jit(solution)/shard_map/ppermute | solution.py:141
  5.2 28.0 %collective-permute-start.5 = (f32[2,128,256]{2,1,0:T(8,128)S(1)}, f32[2,128,256]{2,1,0:T(8,128)S(1)}, u32[]{:S(2)}, u32[]{:S(2)}) collective-permute-start(f32[2,128,256]{2,1,0:T(8,128)S(1)} %cut.3), channel_id=1, source_target_pairs={{0,1},{1,2},{2,3},{3,4},{4,5},{5,6},{6,7},{7,8},{8,9},{9,10},{10,1... | collective-permute-start | bytes 786440 | tf_op jit(solution)/shard_map/ppermute | solution.py:141
  8.7 5.1 %copy-start.2 = (s32[1,1,1,2,12]{4,3,2,1,0:T(2,128)S(1)}, s32[1,1,1,2,12]{4,3,2,1,0:T(2,128)}, u32[]{:S(2)}) copy-start(s32[1,1,1,2,12]{4,3,2,1,0:T(2,128)} %param.16) | copy-start | bytes 292
  8.7 5.1 %copy-start.3 = (s32[1,1,1,2,12]{4,3,2,1,0:T(2,128)S(1)}, s32[1,1,1,2,12]{4,3,2,1,0:T(2,128)}, u32[]{:S(2)}) copy-start(s32[1,1,1,2,12]{4,3,2,1,0:T(2,128)} %param.17) | copy-start | bytes 292
  9.1 25.4 %collective-permute-start.3 = (f32[2,128,256]{2,1,0:T(8,128)S(1)}, f32[2,128,256]{2,1,0:T(8,128)S(1)}, u32[]{:S(2)}, u32[]{:S(2)}) collective-permute-start(f32[2,128,256]{2,1,0:T(8,128)S(1)} %cut.2), channel_id=1, source_target_pairs={{0,257},{1,258},{2,259},{3,260},{4,261},{5,262},{6,263},{7,264},{8... | collective-permute-start | bytes 786440 | tf_op jit(solution)/shard_map/ppermute | solution.py:141
  13.8 0.7 %copy-start.1 = (s32[1,1,1,2,12]{4,3,2,1,0:T(2,128)S(1)}, s32[1,1,1,2,12]{4,3,2,1,0:T(2,128)}, u32[]{:S(2)}) copy-start(s32[1,1,1,2,12]{4,3,2,1,0:T(2,128)} %param.15) | copy-start | bytes 292
  13.8 0.7 %copy-start.4 = (s32[1,1,1,2]{3,2,1,0:T(1,128)S(1)}, s32[1,1,1,2]{3,2,1,0:T(1,128)}, u32[]{:S(2)}) copy-start(s32[1,1,1,2]{3,2,1,0:T(1,128)} %param.18) | copy-start | bytes 28
  14.5 14.5 %collective-permute-start.1 = (f32[2,256,256]{2,1,0:T(8,128)}, f32[2,256,256]{2,1,0:T(8,128)S(1)}, u32[]{:S(2)}, u32[]{:S(2)}) collective-permute-start(f32[2,256,256]{2,1,0:T(8,128)} %get-tuple-element.49), channel_id=1, source_target_pairs={{31,63},{63,95},{95,127},{127,159},{159,191},{191,223},{223,255},{... | collective-permute-start | bytes 1572872 | tf_op jit(solution)/shard_map/cond/branch_1_fun/ppermute | solution.py:141
  17.0 11.1 %collective-permute-start = (f32[528,256]{1,0:T(8,128)S(1)}, f32[528,256]{1,0:T(8,128)S(1)}, u32[]{:S(2)}, u32[]{:S(2)}) collective-permute-start(f32[528,256]{1,0:T(8,128)S(1)} %get-tuple-element.42), channel_id=1, source_target_pairs={{0,256},{1,257},{2,258},{3,259},{4,260},{5,261},{6,262},{7,263},{8... | collective-permute-start | bytes 1622024 | tf_op jit(solution)/shard_map/cond/branch_1_fun/cond/branch_1_fun/ppermute | solution.py:141
  29.2 3.8 %collective-permute-start.2 = (f32[2,256,256]{2,1,0:T(8,128)S(1)}, f32[2,256,256]{2,1,0:T(8,128)S(1)}, u32[]{:S(2)}, u32[]{:S(2)}) collective-permute-start(f32[2,256,256]{2,1,0:T(8,128)S(1)} %broadcast_select_fusion.right_own), channel_id=1, source_target_pairs={{0,256},{1,257},{2,258},{3,259},{4,260},{5,261},{6,262},{7,263},{8... | collective-permute-start | bytes 1572872 | tf_op jit(solution)/shard_map/cond/branch_1_fun/ppermute | solution.py:141
  35.0 8.4 %collective-permute-start.6 = (f32[128,256]{1,0:T(8,128)S(1)}, f32[128,256]{1,0:T(8,128)S(1)}, u32[]{:S(2)}, u32[]{:S(2)}) collective-permute-start(f32[128,256]{1,0:T(8,128)S(1)} %get-tuple-element.72), channel_id=1, source_target_pairs={{0,512},{1,513},{2,514},{3,515},{4,516},{5,517},{6,518},{7,519},{8... | collective-permute-start | bytes 393224 | tf_op jit(solution)/shard_map/ppermute | solution.py:141
  36.9 8.0 %collective-permute-start.7 = (f32[128,256]{1,0:T(8,128)S(1)}, f32[128,256]{1,0:T(8,128)S(1)}, u32[]{:S(2)}, u32[]{:S(2)}) collective-permute-start(f32[128,256]{1,0:T(8,128)S(1)} %get-tuple-element.73), channel_id=1, source_target_pairs={{0,768},{1,769},{2,770},{3,771},{4,772},{5,773},{6,774},{7,775},{8... | collective-permute-start | bytes 393224 | tf_op jit(solution)/shard_map/ppermute | solution.py:141
  40.8 4.1 %collective-permute-start.8 = (f32[128,256]{1,0:T(8,128)S(1)}, f32[128,256]{1,0:T(8,128)S(1)}, u32[]{:S(2)}, u32[]{:S(2)}) collective-permute-start(f32[128,256]{1,0:T(8,128)S(1)} %get-tuple-element.76), channel_id=1, source_target_pairs={{0,256},{1,257},{2,258},{3,259},{4,260},{5,261},{6,262},{7,263},{8... | collective-permute-start | bytes 393224 | tf_op jit(solution)/shard_map/ppermute | solution.py:141

commit v8 on v6

--- a/solution.py
+++ b/solution.py
@@ -31,8 +31,11 @@
     count, rows, depth = left.shape
     high, low = halves(left.reshape(count * rows, depth))
     found = []
+    stacked = jnp.concatenate([high, low], axis=0)
+    size = count * rows
     for slot in slots:
-        both = dot(high, right_high[slot]) + (dot(high, right_low[slot]) + dot(low, right_high[slot]))
+        first = dot(stacked, right_high[slot])
+        both = first[:size] + (dot(high, right_low[slot]) + first[size:])
         found.append([both[l * rows : (l + 1) * rows] for l in range(count)])
     return found
 
@@ -95,13 +98,20 @@
         right_high[slot], right_low[slot] = halves(right)
 
 
-def second_kernel(left_own, left_mate, right_high, right_low, base, weights, *outs):
-    half = left_own.shape[1]
-    own = pair_products(left_own[...], right_high, right_low, (0, 1))
-    mate = pair_products(left_mate[...], right_high, right_low, (2, 3))
+def own_kernel(left, right_high, right_low, base, weights, part):
+    half = left.shape[1]
+    found = pair_products(left[...], right_high, right_low, (0, 1))
+    for j in range(4):
+        rows = slice(j * half, (j + 1) * half)
+        part[rows, :] = combine(found, lambda k: weights[k : k + 1, :], j, base[rows, :])
+
+
+def mate_kernel(left, right_high, right_low, part, weights, *outs):
+    half = left.shape[1]
+    found = pair_products(left[...], right_high, right_low, (2, 3))
     for j in (2, 3, 1, 0):
-        total = combine(own, lambda k: weights[k : k + 1, :], j, base[j * half : (j + 1) * half, :])
-        outs[j][...] = combine(mate, lambda k: weights[16 + k : 17 + k, :], j, total)
+        rows = slice(j * half, (j + 1) * half)
+        outs[j][...] = combine(found, lambda k: weights[16 + k : 17 + k, :], j, part[rows, :])
 
 
 def last_kernel(mask, chip, far, core, own, out, held, sems):
@@ -218,19 +228,30 @@
 
     base, weights, right_rest = guarded(beside, left, right)
     (right_first,) = hold(right_first)
+    base, weights = hold(base, weights)
     right_high, right_low = guarded(middle, right_first, right_rest)
+    part = pl.pallas_call(
+        own_kernel,
+        out_shape=jax.ShapeDtypeStruct((4 * half, cols), f32),
+        in_specs=[vmem] * 5,
+        out_specs=vmem,
+        compiler_params=PARAMS,
+        cost_estimate=pl.CostEstimate(flops=3 << 26, bytes_accessed=2 << 20, transcendentals=0),
+        name="own_layer",
+    )(left_own, right_high, right_low, base, weights)
     own, core_out, chip_out, far_out = pl.pallas_call(
-        second_kernel,
+        mate_kernel,
         out_shape=(jax.ShapeDtypeStruct((half, cols), f32),) * 4,
-        in_specs=[vmem] * 6,
+        in_specs=[vmem] * 5,
         out_specs=(vmem,) * 4,
         compiler_params=PARAMS,
-        cost_estimate=pl.CostEstimate(flops=6 << 26, bytes_accessed=3 << 20, transcendentals=0),
-        name="second_step",
-    )(left_own, left_mate, right_high, right_low, base, weights)
+        cost_estimate=pl.CostEstimate(flops=3 << 26, bytes_accessed=2 << 20, transcendentals=0),
+        name="mate_layer",
+    )(left_mate, right_high, right_low, part, weights)
     chip_in = permute(chip_out, lambda l, r, c: (l ^ 2, r, c))
     far_in = permute(far_out, lambda l, r, c: (l ^ 3, r, c))
     core_in = permute(core_out, lambda l, r, c: (l ^ 1, r, c))
+    chip_in, far_in = hold(chip_in, far_in)
     result = pl.pallas_call(
         last_kernel,
         out_shape=jax.ShapeDtypeStruct((rows, cols), f32),

time: 45.3 us -> 45.1 us (level)
  waiting for transfers between devices: 5.47 us -> 4.84 us
    ppermute x9, waiting for transfers between devices: 5.47 us -> 4.84 us  [permute(): return lax.ppermute(value, names, pairs)]
    pallas_call x1 -> x2, Pallas kernels: 0.68 us -> 0.92 us  [the longest x1 0.46 us: local(): pl.pallas_call(mate_kernel, out_shape=(jax.ShapeDtypeStruct((half, cols),...]
  transfers between devices with their start and end apart: 9 -> 9, of which waited for: 4 -> 3; matrix products, arithmetic and copies ran while one was open for 0% -> 0% of each run, Pallas kernels for 7% -> 9%
where the time goes in v8:
time: 45.1 us; the launch traced here: 44.7 us
  starting transfers between devices  33.1 us (73%)
  Pallas kernels  5.06 us (11%)
  waiting for transfers between devices  4.84 us (11%)
  between operations  0.82 us (2%)
  local copies, waits for them, and re-layouts  0.68 us (2%)
    ppermute x9, starting transfers between devices, permute(): return lax.ppermute(value, names, pairs)  33.1 us
    ppermute x9, waiting for transfers between devices, permute(): return lax.ppermute(value, names, pairs)  4.84 us
    pallas_call x1, Pallas kernels, early(): pl.pallas_call(first_kernel, out_shape=(jax.ShapeDtypeStruct((4 * half +...  1.96 us
    pallas_call x1, Pallas kernels, local(): pl.pallas_call(split_kernel, out_shape=(jax.ShapeDtypeStruct((slots, half...  1.07 us
  transfers between devices with their start and end apart: 9, of which 3 were waited for; matrix products, arithmetic and copies ran while one was open for 0% of the time, Pallas kernels for 9%

profile of v8, /device:TPU:1, one launch (start us, length us, event | category | flops | bytes accessed | tf_op | source)
XLA Modules:
  0.0 44.7 jit_solution(4636450432127972548)
XLA Ops:
  0.0 4.0 %collective-permute-start.4 = (f32[2,256,256]{2,1,0:T(8,128)}, f32[2,256,256]{2,1,0:T(8,128)S(1)}, u32[]{:S(2)}, u32[]{:S(2)}) collective-permute-start(f32[2,256,256]{2,1,0:T(8,128)} %bitcast.5), channel_id=1, source_target_pairs={{0,32},{1,33},{2,34},{3,35},{4,36},{5,37},{6,38},{7,39},{8,40},{9,... | collective-permute-start | bytes 1572872 | tf_op jit(solution)/shard_map/ppermute | solution.py:142
  4.0 1.1 %split.1 = (f32[2,128,256]{2,1,0:T(8,128)S(1)}, f32[2,128,256]{2,1,0:T(8,128)S(1)}) custom-call(f32[2,256,256]{2,1,0:T(8,128)} %bitcast.3), custom_call_target="tpu_custom_call" | custom-call | flops 1024 | bytes 1048576 | tf_op jit(solution)/shard_map/split/pallas_call | solution.py:155
  5.1 3.5 %collective-permute-start.5 = (f32[2,128,256]{2,1,0:T(8,128)S(1)}, f32[2,128,256]{2,1,0:T(8,128)S(1)}, u32[]{:S(2)}, u32[]{:S(2)}) collective-permute-start(f32[2,128,256]{2,1,0:T(8,128)S(1)} %get-tuple-element.75), channel_id=1, source_target_pairs={{0,1},{1,2},{2,3},{3,4},{4,5},{5,6},{6,7},{7,8},{8,9},{9,10},{10,1... | collective-permute-start | bytes 786440 | tf_op jit(solution)/shard_map/ppermute | solution.py:142
  8.7 4.7 %collective-permute-start.3 = (f32[2,128,256]{2,1,0:T(8,128)S(1)}, f32[2,128,256]{2,1,0:T(8,128)S(1)}, u32[]{:S(2)}, u32[]{:S(2)}) collective-permute-start(f32[2,128,256]{2,1,0:T(8,128)S(1)} %get-tuple-element.71), channel_id=1, source_target_pairs={{0,257},{1,258},{2,259},{3,260},{4,261},{5,262},{6,263},{7,264},{8... | collective-permute-start | bytes 786440 | tf_op jit(solution)/shard_map/ppermute | solution.py:142
  13.3 0.0 copy-start.1
  13.3 0.0 copy-start.2
  13.4 0.0 copy-start
  13.4 0.0 copy-start.3
  13.4 0.6 %copy-done.1 = s32[1,1,1,2,12]{4,3,2,1,0:T(2,128)S(1)} copy-done((s32[1,1,1,2,12]{4,3,2,1,0:T(2,128)S(1)}, s32[1,1,1,2,12]{4,3,2,1,0:T(2,128)}, u32[]{:S(2)}) %copy-start.1) | copy-done | bytes 120
  14.0 0.0 copy-done.2
  14.0 0.0 copy-done
  14.0 0.0 copy-done.3
  14.1 13.9 %conditional.3 = (f32[512,256]{1,0:T(8,128)S(1)}, f32[32,256]{1,0:T(8,128)S(1)}, f32[2,256,256]{2,1,0:T(8,128)S(1)}) conditional(s32[]{:T(128)} %convert_element_type.7, () %tuple.28, (pred[]{:T(512)}, s32[1,1,1,2,12]{4,3,2,1,0:T(2,128)S(1)}, s32[1,1,1,2,12]{4,3,2,1,0:T(2,128)S(1)}, s32[1,1,1,2,12]{4,3,2,1,0:T(2,128)S(1)}, ...), branch_computations={%region_0.0_spmd, %region_1.0_spmd} | conditional | flops 403046400 | bytes 10027173 | solution.py:174
  14.1 0.7 %collective-permute-start.1 = (f32[2,256,256]{2,1,0:T(8,128)}, f32[2,256,256]{2,1,0:T(8,128)S(1)}, u32[]{:S(2)}, u32[]{:S(2)}) collective-permute-start(f32[2,256,256]{2,1,0:T(8,128)} %get-tuple-element.49), channel_id=1, source_target_pairs={{31,63},{63,95},{95,127},{127,159},{159,191},{191,223},{223,255},{... | collective-permute-start | bytes 1572872 | tf_op jit(solution)/shard_map/cond/branch_1_fun/ppermute | solution.py:142
  14.7 13.2 %conditional = ((f32[512,256]{1,0:T(8,128)S(1)}, f32[32,256]{1,0:T(8,128)S(1)})) conditional(s32[]{:T(128)} %convert_element_type.1, () %tuple.19, (s32[1,1,1,2,12]{4,3,2,1,0:T(2,128)S(1)}, s32[1,1,1,2,12]{4,3,2,1,0:T(2,128)S(1)}, s32[1,1,1,2,12]{4,3,2,1,0:T(2,128)S(1)}, s32[1,1,1,2]{3,2,1,0:T(1,128)S(1)}, f32[2,256,256]{2,1,0:T(8,128)}, ...), branch_computations={%region_2.0_spmd, %region_3.0_spmd} | conditional | flops 402784256 | bytes 5832752 | solution.py:174
  14.8 2.0 %first_step.1 = (f32[528,256]{1,0:T(8,128)S(1)}, f32[528,256]{1,0:T(8,128)S(1)}) custom-call(s32[1,1,1,2,12]{4,3,2,1,0:T(2,128)S(1)} %get-tuple-element.35.li, s32[1,1,1,2,12]{4,3,2,1,0:T(2,128)S(1)} %get-tuple-element.36.ri, s32[1,1,1,2,12]{4,3,2,1,0:T(2,128)S(1)} %get-tuple-element.37.ti, s32[1,1,1,2]{3,2,1,0:T(1,128)S(1)} %get-tuple-element.38.counts, ...), custom_call_target="tpu_custom_call" | custom-call | flops 402653184 | bytes 2097152 | tf_op jit(solution)/shard_map/cond/branch_1_fun/cond/branch_1_fun/first_step/pallas_call | solution.py:188
  16.7 9.6 %collective-permute-start = (f32[528,256]{1,0:T(8,128)S(1)}, f32[528,256]{1,0:T(8,128)S(1)}, u32[]{:S(2)}, u32[]{:S(2)}) collective-permute-start(f32[528,256]{1,0:T(8,128)S(1)} %get-tuple-element.42), channel_id=1, source_target_pairs={{0,256},{1,257},{2,258},{3,259},{4,260},{5,261},{6,262},{7,263},{8... | collective-permute-start | bytes 1622024 | tf_op jit(solution)/shard_map/cond/branch_1_fun/cond/branch_1_fun/ppermute | solution.py:142
  26.3 1.5 %collective-permute-done.heard = f32[528,256]{1,0:T(8,128)S(1)} collective-permute-done((f32[528,256]{1,0:T(8,128)S(1)}, f32[528,256]{1,0:T(8,128)S(1)}, u32[]{:S(2)}, u32[]{:S(2)}) %collective-permute-start) | collective-permute-done | bytes 540704 | tf_op jit(solution)/shard_map/cond/branch_1_fun/cond/branch_1_fun/ppermute | solution.py:142
  27.8 0.1 join.1
  27.9 0.0 collective-permute-done.1.refs_0_
  28.0 0.0 collective-permute-done.4.refs_0_
  28.1 4.7 %conditional.4 = ((bf16[4,256,256]{2,1,0:T(8,128)(2,1)S(1)}, bf16[4,256,256]{2,1,0:T(8,128)(2,1)S(1)})) conditional(s32[]{:T(128)} %convert_element_type.7, () %tuple.27, (f32[2,256,256]{2,1,0:T(8,128)S(1)}, f32[2,256,256]{2,1,0:T(8,128)S(1)}) %tuple.30), branch_computations={%region_4.0_spmd, %region_5.6_spmd} | conditional | flops 1179651 | bytes 5767246 | solution.py:174
  28.1 0.1 broadcast_select_fusion.right_own
  28.2 2.9 %collective-permute-start.2 = (f32[2,256,256]{2,1,0:T(8,128)S(1)}, f32[2,256,256]{2,1,0:T(8,128)S(1)}, u32[]{:S(2)}, u32[]{:S(2)}) collective-permute-start(f32[2,256,256]{2,1,0:T(8,128)S(1)} %broadcast_select_fusion.right_own), channel_id=1, source_target_pairs={{0,256},{1,257},{2,258},{3,259},{4,260},{5,261},{6,262},{7,263},{8... | collective-permute-start | bytes 1572872 | tf_op jit(solution)/shard_map/cond/branch_1_fun/ppermute | solution.py:142
  31.1 1.5 %collective-permute-done.2.right_mate = f32[2,256,256]{2,1,0:T(8,128)S(1)} collective-permute-done((f32[2,256,256]{2,1,0:T(8,128)S(1)}, f32[2,256,256]{2,1,0:T(8,128)S(1)}, u32[]{:S(2)}, u32[]{:S(2)}) %collective-permute-start.2) | collective-permute-done | bytes 524320 | tf_op jit(solution)/shard_map/cond/branch_1_fun/ppermute | solution.py:142
  32.6 0.2 ready.1
  32.8 0.0 collective-permute-done.5.left
  32.8 0.5 %own_layer.1.part = f32[512,256]{1,0:T(8,128)S(1)} custom-call(f32[2,128,256]{2,1,0:T(8,128)S(1)} %collective-permute-done.5.left, bf16[4,256,256]{2,1,0:T(8,128)(2,1)S(1)} %get-tuple-element.73.right_high, bf16[4,256,256]{2,1,0:T(8,128)(2,1)S(1)} %get-tuple-element.74.right_low, f32[512,256]{1,0:T(8,128)S(1)} %get-tuple-element.78.base, ...), custom_call_target="tpu_custom_call" | custom-call | flops 201326592 | bytes 2097152 | tf_op jit(solution)/shard_map/own_layer/pallas_call | solution.py:233
  33.2 0.0 collective-permute-done.3.left
  33.3 0.5 %mate_layer.1 = (f32[128,256]{1,0:T(8,128)S(1)}, f32[128,256]{1,0:T(8,128)S(1)}, f32[128,256]{1,0:T(8,128)S(1)}, f32[128,256]{1,0:T(8,128)S(1)}) custom-call(f32[2,128,256]{2,1,0:T(8,128)S(1)} %collective-permute-done.3.left, bf16[4,256,256]{2,1,0:T(8,128)(2,1)S(1)} %get-tuple-element.73.right_high, bf16[4,256,256]{2,1,0:T(8,128)(2,1)S(1)} %get-tuple-element.74.right_low, ...), custom_call_target="tpu_custom_call" | custom-call | flops 201326592 | bytes 2097152 | tf_op jit(solution)/shard_map/mate_layer/pallas_call | solution.py:242
  33.7 3.0 %collective-permute-start.6 = (f32[128,256]{1,0:T(8,128)S(1)}, f32[128,256]{1,0:T(8,128)S(1)}, u32[]{:S(2)}, u32[]{:S(2)}) collective-permute-start(f32[128,256]{1,0:T(8,128)S(1)} %get-tuple-element.80), channel_id=1, source_target_pairs={{0,512},{1,513},{2,514},{3,515},{4,516},{5,517},{6,518},{7,519},{8... | collective-permute-start | bytes 393224 | tf_op jit(solution)/shard_map/ppermute | solution.py:142
  36.8 2.8 %collective-permute-start.7 = (f32[128,256]{1,0:T(8,128)S(1)}, f32[128,256]{1,0:T(8,128)S(1)}, u32[]{:S(2)}, u32[]{:S(2)}) collective-permute-start(f32[128,256]{1,0:T(8,128)S(1)} %get-tuple-element.81), channel_id=1, source_target_pairs={{0,768},{1,769},{2,770},{3,771},{4,772},{5,773},{6,774},{7,775},{8... | collective-permute-start | bytes 393224 | tf_op jit(solution)/shard_map/ppermute | solution.py:142
  39.6 1.9 %collective-permute-start.8 = (f32[128,256]{1,0:T(8,128)S(1)}, f32[128,256]{1,0:T(8,128)S(1)}, u32[]{:S(2)}, u32[]{:S(2)}) collective-permute-start(f32[128,256]{1,0:T(8,128)S(1)} %get-tuple-element.84), channel_id=1, source_target_pairs={{0,256},{1,257},{2,258},{3,259},{4,260},{5,261},{6,262},{7,263},{8... | collective-permute-start | bytes 393224 | tf_op jit(solution)/shard_map/ppermute | solution.py:142
  42.1 0.0 collective-permute-done.6.refs_0_
  42.1 1.8 %collective-permute-done.7.refs_1_ = f32[128,256]{1,0:T(8,128)S(1)} collective-permute-done((f32[128,256]{1,0:T(8,128)S(1)}, f32[128,256]{1,0:T(8,128)S(1)}, u32[]{:S(2)}, u32[]{:S(2)}) %collective-permute-start.7) | collective-permute-done | bytes 131104 | tf_op jit(solution)/shard_map/ppermute | solution.py:142
  43.9 0.0 collective-permute-done.8.core
  43.9 0.7 %last_sum.1 = f32[256,256]{1,0:T(8,128)} custom-call(s32[1,1,1]{2,1,0:T(1,128)S(6)} %copy.26.mask, f32[128,256]{1,0:T(8,128)S(1)} %get-tuple-element.82.chip, f32[128,256]{1,0:T(8,128)S(1)} %get-tuple-element.83.far, f32[128,256]{1,0:T(8,128)S(1)} %collective-permute-done.8.core, f32[128,256]{1,0:T(8,128)S(1)} %get-tuple-element.85.own), custom_call_target="tpu_custom_call" | custom-call | flops 262144 | bytes 1048576 | tf_op jit(solution)/shard_map/last_sum/pallas_call | solution.py:255
  (5 shorter events, 0.2 us)
Async XLA Ops:
  0.0 28.0 %collective-permute-start.4 = (f32[2,256,256]{2,1,0:T(8,128)}, f32[2,256,256]{2,1,0:T(8,128)S(1)}, u32[]{:S(2)}, u32[]{:S(2)}) collective-permute-start(f32[2,256,256]{2,1,0:T(8,128)} %bitcast.5), channel_id=1, source_target_pairs={{0,32},{1,33},{2,34},{3,35},{4,36},{5,37},{6,38},{7,39},{8,40},{9,... | collective-permute-start | bytes 1572872 | tf_op jit(solution)/shard_map/ppermute | solution.py:142
  5.1 27.7 %collective-permute-start.5 = (f32[2,128,256]{2,1,0:T(8,128)S(1)}, f32[2,128,256]{2,1,0:T(8,128)S(1)}, u32[]{:S(2)}, u32[]{:S(2)}) collective-permute-start(f32[2,128,256]{2,1,0:T(8,128)S(1)} %get-tuple-element.75), channel_id=1, source_target_pairs={{0,1},{1,2},{2,3},{3,4},{4,5},{5,6},{6,7},{7,8},{8,9},{9,10},{10,1... | collective-permute-start | bytes 786440 | tf_op jit(solution)/shard_map/ppermute | solution.py:142
  8.7 24.6 %collective-permute-start.3 = (f32[2,128,256]{2,1,0:T(8,128)S(1)}, f32[2,128,256]{2,1,0:T(8,128)S(1)}, u32[]{:S(2)}, u32[]{:S(2)}) collective-permute-start(f32[2,128,256]{2,1,0:T(8,128)S(1)} %get-tuple-element.71), channel_id=1, source_target_pairs={{0,257},{1,258},{2,259},{3,260},{4,261},{5,262},{6,263},{7,264},{8... | collective-permute-start | bytes 786440 | tf_op jit(solution)/shard_map/ppermute | solution.py:142
  13.3 0.7 %copy-start.1 = (s32[1,1,1,2,12]{4,3,2,1,0:T(2,128)S(1)}, s32[1,1,1,2,12]{4,3,2,1,0:T(2,128)}, u32[]{:S(2)}) copy-start(s32[1,1,1,2,12]{4,3,2,1,0:T(2,128)} %param.16) | copy-start | bytes 292
  13.3 0.7 %copy-start.2 = (s32[1,1,1,2,12]{4,3,2,1,0:T(2,128)S(1)}, s32[1,1,1,2,12]{4,3,2,1,0:T(2,128)}, u32[]{:S(2)}) copy-start(s32[1,1,1,2,12]{4,3,2,1,0:T(2,128)} %param.17) | copy-start | bytes 292
  13.4 0.7 %copy-start = (s32[1,1,1,2,12]{4,3,2,1,0:T(2,128)S(1)}, s32[1,1,1,2,12]{4,3,2,1,0:T(2,128)}, u32[]{:S(2)}) copy-start(s32[1,1,1,2,12]{4,3,2,1,0:T(2,128)} %param.15) | copy-start | bytes 292
  13.4 0.7 %copy-start.3 = (s32[1,1,1,2]{3,2,1,0:T(1,128)S(1)}, s32[1,1,1,2]{3,2,1,0:T(1,128)}, u32[]{:S(2)}) copy-start(s32[1,1,1,2]{3,2,1,0:T(1,128)} %param.18) | copy-start | bytes 28
  14.1 13.9 %collective-permute-start.1 = (f32[2,256,256]{2,1,0:T(8,128)}, f32[2,256,256]{2,1,0:T(8,128)S(1)}, u32[]{:S(2)}, u32[]{:S(2)}) collective-permute-start(f32[2,256,256]{2,1,0:T(8,128)} %get-tuple-element.49), channel_id=1, source_target_pairs={{31,63},{63,95},{95,127},{127,159},{159,191},{191,223},{223,255},{... | collective-permute-start | bytes 1572872 | tf_op jit(solution)/shard_map/cond/branch_1_fun/ppermute | solution.py:142
  16.7 11.1 %collective-permute-start = (f32[528,256]{1,0:T(8,128)S(1)}, f32[528,256]{1,0:T(8,128)S(1)}, u32[]{:S(2)}, u32[]{:S(2)}) collective-permute-start(f32[528,256]{1,0:T(8,128)S(1)} %get-tuple-element.42), channel_id=1, source_target_pairs={{0,256},{1,257},{2,258},{3,259},{4,260},{5,261},{6,262},{7,263},{8... | collective-permute-start | bytes 1622024 | tf_op jit(solution)/shard_map/cond/branch_1_fun/cond/branch_1_fun/ppermute | solution.py:142
  28.2 4.4 %collective-permute-start.2 = (f32[2,256,256]{2,1,0:T(8,128)S(1)}, f32[2,256,256]{2,1,0:T(8,128)S(1)}, u32[]{:S(2)}, u32[]{:S(2)}) collective-permute-start(f32[2,256,256]{2,1,0:T(8,128)S(1)} %broadcast_select_fusion.right_own), channel_id=1, source_target_pairs={{0,256},{1,257},{2,258},{3,259},{4,260},{5,261},{6,262},{7,263},{8... | collective-permute-start | bytes 1572872 | tf_op jit(solution)/shard_map/cond/branch_1_fun/ppermute | solution.py:142
  33.7 8.4 %collective-permute-start.6 = (f32[128,256]{1,0:T(8,128)S(1)}, f32[128,256]{1,0:T(8,128)S(1)}, u32[]{:S(2)}, u32[]{:S(2)}) collective-permute-start(f32[128,256]{1,0:T(8,128)S(1)} %get-tuple-element.80), channel_id=1, source_target_pairs={{0,512},{1,513},{2,514},{3,515},{4,516},{5,517},{6,518},{7,519},{8... | collective-permute-start | bytes 393224 | tf_op jit(solution)/shard_map/ppermute | solution.py:142
  36.8 7.2 %collective-permute-start.7 = (f32[128,256]{1,0:T(8,128)S(1)}, f32[128,256]{1,0:T(8,128)S(1)}, u32[]{:S(2)}, u32[]{:S(2)}) collective-permute-start(f32[128,256]{1,0:T(8,128)S(1)} %get-tuple-element.81), channel_id=1, source_target_pairs={{0,768},{1,769},{2,770},{3,771},{4,772},{5,773},{6,774},{7,775},{8... | collective-permute-start | bytes 393224 | tf_op jit(solution)/shard_map/ppermute | solution.py:142
  39.6 4.4 %collective-permute-start.8 = (f32[128,256]{1,0:T(8,128)S(1)}, f32[128,256]{1,0:T(8,128)S(1)}, u32[]{:S(2)}, u32[]{:S(2)}) collective-permute-start(f32[128,256]{1,0:T(8,128)S(1)} %get-tuple-element.84), channel_id=1, source_target_pairs={{0,256},{1,257},{2,258},{3,259},{4,260},{5,261},{6,262},{7,263},{8... | collective-permute-start | bytes 393224 | tf_op jit(solution)/shard_map/ppermute | solution.py:142

commit v9 on v8

--- a/solution.py
+++ b/solution.py
@@ -106,12 +106,11 @@
         part[rows, :] = combine(found, lambda k: weights[k : k + 1, :], j, base[rows, :])
 
 
-def mate_kernel(left, right_high, right_low, part, weights, *outs):
+def mate_kernel(blocks, left, right_high, right_low, part, weights, *outs):
     half = left.shape[1]
     found = pair_products(left[...], right_high, right_low, (2, 3))
-    for j in (2, 3, 1, 0):
-        rows = slice(j * half, (j + 1) * half)
-        outs[j][...] = combine(found, lambda k: weights[16 + k : 17 + k, :], j, part[rows, :])
+    for j, out in zip(blocks, outs):
+        out[...] = combine(found, lambda k: weights[16 + k : 17 + k, :], j, part[j * half : (j + 1) * half, :])
 
 
 def last_kernel(mask, chip, far, core, own, out, held, sems):
@@ -239,15 +238,19 @@
         cost_estimate=pl.CostEstimate(flops=3 << 26, bytes_accessed=2 << 20, transcendentals=0),
         name="own_layer",
     )(left_own, right_high, right_low, base, weights)
-    own, core_out, chip_out, far_out = pl.pallas_call(
-        mate_kernel,
-        out_shape=(jax.ShapeDtypeStruct((half, cols), f32),) * 4,
-        in_specs=[vmem] * 5,
-        out_specs=(vmem,) * 4,
-        compiler_params=PARAMS,
-        cost_estimate=pl.CostEstimate(flops=3 << 26, bytes_accessed=2 << 20, transcendentals=0),
-        name="mate_layer",
-    )(left_mate, right_high, right_low, part, weights)
+    def mate(*blocks):
+        return pl.pallas_call(
+            functools.partial(mate_kernel, blocks),
+            out_shape=(jax.ShapeDtypeStruct((half, cols), f32),) * 2,
+            in_specs=[vmem] * 5,
+            out_specs=(vmem,) * 2,
+            compiler_params=PARAMS,
+            cost_estimate=pl.CostEstimate(flops=3 << 26, bytes_accessed=2 << 20, transcendentals=0),
+            name="mate_layer",
+        )(left_mate, right_high, right_low, part, weights)
+
+    chip_out, far_out = mate(2, 3)
+    own, core_out = mate(0, 1)
     chip_in = permute(chip_out, lambda l, r, c: (l ^ 2, r, c))
     far_in = permute(far_out, lambda l, r, c: (l ^ 3, r, c))
     core_in = permute(core_out, lambda l, r, c: (l ^ 1, r, c))

time: 45.1 us -> 45 us (level)
  transfers between devices with their start and end apart: 9 -> 9, of which waited for: 3 -> 3; matrix products, arithmetic and copies ran while one was open for 0% -> 0% of each run, Pallas kernels for 9% -> 10%
where the time goes in v9:
time: 45 us; the launch traced here: 44.6 us
  starting transfers between devices  33.1 us (74%)
  Pallas kernels  5.35 us (12%)
  waiting for transfers between devices  4.45 us (10%)
  between operations  0.83 us (2%)
  local copies, waits for them, and re-layouts  0.68 us (2%)
    ppermute x9, starting transfers between devices, permute(): return lax.ppermute(value, names, pairs)  33.1 us
    ppermute x9, waiting for transfers between devices, permute(): return lax.ppermute(value, names, pairs)  4.45 us
    pallas_call x1, Pallas kernels, early(): pl.pallas_call(first_kernel, out_shape=(jax.ShapeDtypeStruct((4 * half +...  1.96 us
    pallas_call x1, Pallas kernels, local(): pl.pallas_call(split_kernel, out_shape=(jax.ShapeDtypeStruct((slots, half...  1.07 us
  transfers between devices with their start and end apart: 9, of which 3 were waited for; matrix products, arithmetic and copies ran while one was open for 0% of the time, Pallas kernels for 10%

profile of v9, /device:TPU:1, one launch (start us, length us, event | category | flops | bytes accessed | tf_op | source)
XLA Modules:
  0.0 44.6 jit_solution(6565514701832597374)
XLA Ops:
  0.0 4.0 %collective-permute-start.4 = (f32[2,256,256]{2,1,0:T(8,128)}, f32[2,256,256]{2,1,0:T(8,128)S(1)}, u32[]{:S(2)}, u32[]{:S(2)}) collective-permute-start(f32[2,256,256]{2,1,0:T(8,128)} %bitcast.5), channel_id=1, source_target_pairs={{0,32},{1,33},{2,34},{3,35},{4,36},{5,37},{6,38},{7,39},{8,40},{9,... | collective-permute-start | bytes 1572872 | tf_op jit(solution)/shard_map/ppermute | solution.py:141
  4.0 1.1 %split.1 = (f32[2,128,256]{2,1,0:T(8,128)S(1)}, f32[2,128,256]{2,1,0:T(8,128)S(1)}) custom-call(f32[2,256,256]{2,1,0:T(8,128)} %bitcast.3), custom_call_target="tpu_custom_call" | custom-call | flops 1024 | bytes 1048576 | tf_op jit(solution)/shard_map/split/pallas_call | solution.py:154
  5.1 3.5 %collective-permute-start.5 = (f32[2,128,256]{2,1,0:T(8,128)S(1)}, f32[2,128,256]{2,1,0:T(8,128)S(1)}, u32[]{:S(2)}, u32[]{:S(2)}) collective-permute-start(f32[2,128,256]{2,1,0:T(8,128)S(1)} %get-tuple-element.75), channel_id=1, source_target_pairs={{0,1},{1,2},{2,3},{3,4},{4,5},{5,6},{6,7},{7,8},{8,9},{9,10},{10,1... | collective-permute-start | bytes 786440 | tf_op jit(solution)/shard_map/ppermute | solution.py:141
  8.7 4.7 %collective-permute-start.3 = (f32[2,128,256]{2,1,0:T(8,128)S(1)}, f32[2,128,256]{2,1,0:T(8,128)S(1)}, u32[]{:S(2)}, u32[]{:S(2)}) collective-permute-start(f32[2,128,256]{2,1,0:T(8,128)S(1)} %get-tuple-element.71), channel_id=1, source_target_pairs={{0,257},{1,258},{2,259},{3,260},{4,261},{5,262},{6,263},{7,264},{8... | collective-permute-start | bytes 786440 | tf_op jit(solution)/shard_map/ppermute | solution.py:141
  13.3 0.0 copy-start.1
  13.3 0.0 copy-start.2
  13.4 0.0 copy-start
  13.4 0.0 copy-start.3
  13.4 0.6 %copy-done.1 = s32[1,1,1,2,12]{4,3,2,1,0:T(2,128)S(1)} copy-done((s32[1,1,1,2,12]{4,3,2,1,0:T(2,128)S(1)}, s32[1,1,1,2,12]{4,3,2,1,0:T(2,128)}, u32[]{:S(2)}) %copy-start.1) | copy-done | bytes 120
  14.0 0.0 copy-done.2
  14.0 0.0 copy-done
  14.0 0.0 copy-done.3
  14.1 13.9 %conditional.3 = (f32[512,256]{1,0:T(8,128)S(1)}, f32[32,256]{1,0:T(8,128)S(1)}, f32[2,256,256]{2,1,0:T(8,128)S(1)}) conditional(s32[]{:T(128)} %convert_element_type.7, () %tuple.28, (pred[]{:T(512)}, s32[1,1,1,2,12]{4,3,2,1,0:T(2,128)S(1)}, s32[1,1,1,2,12]{4,3,2,1,0:T(2,128)S(1)}, s32[1,1,1,2,12]{4,3,2,1,0:T(2,128)S(1)}, ...), branch_computations={%region_0.0_spmd, %region_1.0_spmd} | conditional | flops 403046400 | bytes 10027173 | solution.py:173
  14.1 0.7 %collective-permute-start.1 = (f32[2,256,256]{2,1,0:T(8,128)}, f32[2,256,256]{2,1,0:T(8,128)S(1)}, u32[]{:S(2)}, u32[]{:S(2)}) collective-permute-start(f32[2,256,256]{2,1,0:T(8,128)} %get-tuple-element.49), channel_id=1, source_target_pairs={{31,63},{63,95},{95,127},{127,159},{159,191},{191,223},{223,255},{... | collective-permute-start | bytes 1572872 | tf_op jit(solution)/shard_map/cond/branch_1_fun/ppermute | solution.py:141
  14.7 13.2 %conditional = ((f32[512,256]{1,0:T(8,128)S(1)}, f32[32,256]{1,0:T(8,128)S(1)})) conditional(s32[]{:T(128)} %convert_element_type.1, () %tuple.19, (s32[1,1,1,2,12]{4,3,2,1,0:T(2,128)S(1)}, s32[1,1,1,2,12]{4,3,2,1,0:T(2,128)S(1)}, s32[1,1,1,2,12]{4,3,2,1,0:T(2,128)S(1)}, s32[1,1,1,2]{3,2,1,0:T(1,128)S(1)}, f32[2,256,256]{2,1,0:T(8,128)}, ...), branch_computations={%region_2.0_spmd, %region_3.0_spmd} | conditional | flops 402784256 | bytes 5832752 | solution.py:173
  14.8 2.0 %first_step.1 = (f32[528,256]{1,0:T(8,128)S(1)}, f32[528,256]{1,0:T(8,128)S(1)}) custom-call(s32[1,1,1,2,12]{4,3,2,1,0:T(2,128)S(1)} %get-tuple-element.35.li, s32[1,1,1,2,12]{4,3,2,1,0:T(2,128)S(1)} %get-tuple-element.36.ri, s32[1,1,1,2,12]{4,3,2,1,0:T(2,128)S(1)} %get-tuple-element.37.ti, s32[1,1,1,2]{3,2,1,0:T(1,128)S(1)} %get-tuple-element.38.counts, ...), custom_call_target="tpu_custom_call" | custom-call | flops 402653184 | bytes 2097152 | tf_op jit(solution)/shard_map/cond/branch_1_fun/cond/branch_1_fun/first_step/pallas_call | solution.py:187
  16.7 9.6 %collective-permute-start = (f32[528,256]{1,0:T(8,128)S(1)}, f32[528,256]{1,0:T(8,128)S(1)}, u32[]{:S(2)}, u32[]{:S(2)}) collective-permute-start(f32[528,256]{1,0:T(8,128)S(1)} %get-tuple-element.42), channel_id=1, source_target_pairs={{0,256},{1,257},{2,258},{3,259},{4,260},{5,261},{6,262},{7,263},{8... | collective-permute-start | bytes 1622024 | tf_op jit(solution)/shard_map/cond/branch_1_fun/cond/branch_1_fun/ppermute | solution.py:141
  26.3 1.5 %collective-permute-done.heard = f32[528,256]{1,0:T(8,128)S(1)} collective-permute-done((f32[528,256]{1,0:T(8,128)S(1)}, f32[528,256]{1,0:T(8,128)S(1)}, u32[]{:S(2)}, u32[]{:S(2)}) %collective-permute-start) | collective-permute-done | bytes 540704 | tf_op jit(solution)/shard_map/cond/branch_1_fun/cond/branch_1_fun/ppermute | solution.py:141
  27.8 0.1 join.1
  27.9 0.0 collective-permute-done.1.refs_0_
  28.0 0.0 collective-permute-done.4.refs_0_
  28.1 4.7 %conditional.4 = ((bf16[4,256,256]{2,1,0:T(8,128)(2,1)S(1)}, bf16[4,256,256]{2,1,0:T(8,128)(2,1)S(1)})) conditional(s32[]{:T(128)} %convert_element_type.7, () %tuple.27, (f32[2,256,256]{2,1,0:T(8,128)S(1)}, f32[2,256,256]{2,1,0:T(8,128)S(1)}) %tuple.30), branch_computations={%region_4.0_spmd, %region_5.6_spmd} | conditional | flops 1179651 | bytes 5767246 | solution.py:173
  28.1 0.1 broadcast_select_fusion.right_own
  28.2 2.9 %collective-permute-start.2 = (f32[2,256,256]{2,1,0:T(8,128)S(1)}, f32[2,256,256]{2,1,0:T(8,128)S(1)}, u32[]{:S(2)}, u32[]{:S(2)}) collective-permute-start(f32[2,256,256]{2,1,0:T(8,128)S(1)} %broadcast_select_fusion.right_own), channel_id=1, source_target_pairs={{0,256},{1,257},{2,258},{3,259},{4,260},{5,261},{6,262},{7,263},{8... | collective-permute-start | bytes 1572872 | tf_op jit(solution)/shard_map/cond/branch_1_fun/ppermute | solution.py:141
  31.1 1.5 %collective-permute-done.2.right_mate = f32[2,256,256]{2,1,0:T(8,128)S(1)} collective-permute-done((f32[2,256,256]{2,1,0:T(8,128)S(1)}, f32[2,256,256]{2,1,0:T(8,128)S(1)}, u32[]{:S(2)}, u32[]{:S(2)}) %collective-permute-start.2) | collective-permute-done | bytes 524320 | tf_op jit(solution)/shard_map/cond/branch_1_fun/ppermute | solution.py:141
  32.6 0.2 ready.1
  32.8 0.0 collective-permute-done.5.left
  32.8 0.5 %own_layer.1.part = f32[512,256]{1,0:T(8,128)S(1)} custom-call(f32[2,128,256]{2,1,0:T(8,128)S(1)} %collective-permute-done.5.left, bf16[4,256,256]{2,1,0:T(8,128)(2,1)S(1)} %get-tuple-element.73.right_high, bf16[4,256,256]{2,1,0:T(8,128)(2,1)S(1)} %get-tuple-element.74.right_low, f32[512,256]{1,0:T(8,128)S(1)} %get-tuple-element.78.base, ...), custom_call_target="tpu_custom_call" | custom-call | flops 201326592 | bytes 2097152 | tf_op jit(solution)/shard_map/own_layer/pallas_call | solution.py:232
  33.2 0.0 collective-permute-done.3.left
  33.3 0.4 mate_layer.2
  33.6 3.0 %collective-permute-start.6 = (f32[128,256]{1,0:T(8,128)S(1)}, f32[128,256]{1,0:T(8,128)S(1)}, u32[]{:S(2)}, u32[]{:S(2)}) collective-permute-start(f32[128,256]{1,0:T(8,128)S(1)} %get-tuple-element.80), channel_id=1, source_target_pairs={{0,512},{1,513},{2,514},{3,515},{4,516},{5,517},{6,518},{7,519},{8... | collective-permute-start | bytes 393224 | tf_op jit(solution)/shard_map/ppermute | solution.py:141
  36.7 2.8 %collective-permute-start.7 = (f32[128,256]{1,0:T(8,128)S(1)}, f32[128,256]{1,0:T(8,128)S(1)}, u32[]{:S(2)}, u32[]{:S(2)}) collective-permute-start(f32[128,256]{1,0:T(8,128)S(1)} %get-tuple-element.81), channel_id=1, source_target_pairs={{0,768},{1,769},{2,770},{3,771},{4,772},{5,773},{6,774},{7,775},{8... | collective-permute-start | bytes 393224 | tf_op jit(solution)/shard_map/ppermute | solution.py:141
  39.5 0.4 mate_layer.3
  39.9 1.9 %collective-permute-start.8 = (f32[128,256]{1,0:T(8,128)S(1)}, f32[128,256]{1,0:T(8,128)S(1)}, u32[]{:S(2)}, u32[]{:S(2)}) collective-permute-start(f32[128,256]{1,0:T(8,128)S(1)} %get-tuple-element.84), channel_id=1, source_target_pairs={{0,256},{1,257},{2,258},{3,259},{4,260},{5,261},{6,262},{7,263},{8... | collective-permute-start | bytes 393224 | tf_op jit(solution)/shard_map/ppermute | solution.py:141
  42.4 0.0 collective-permute-done.6.refs_0_
  42.5 1.4 %collective-permute-done.7.refs_1_ = f32[128,256]{1,0:T(8,128)S(1)} collective-permute-done((f32[128,256]{1,0:T(8,128)S(1)}, f32[128,256]{1,0:T(8,128)S(1)}, u32[]{:S(2)}, u32[]{:S(2)}) %collective-permute-start.7) | collective-permute-done | bytes 131104 | tf_op jit(solution)/shard_map/ppermute | solution.py:141
  43.9 0.0 collective-permute-done.8.core
  43.9 0.7 %last_sum.1 = f32[256,256]{1,0:T(8,128)} custom-call(s32[1,1,1]{2,1,0:T(1,128)S(6)} %copy.26.mask, f32[128,256]{1,0:T(8,128)S(1)} %get-tuple-element.82.chip, f32[128,256]{1,0:T(8,128)S(1)} %get-tuple-element.83.far, f32[128,256]{1,0:T(8,128)S(1)} %collective-permute-done.8.core, f32[128,256]{1,0:T(8,128)S(1)} %get-tuple-element.85.own), custom_call_target="tpu_custom_call" | custom-call | flops 262144 | bytes 1048576 | tf_op jit(solution)/shard_map/last_sum/pallas_call | solution.py:258
  (5 shorter events, 0.2 us)
Async XLA Ops:
  0.0 28.0 %collective-permute-start.4 = (f32[2,256,256]{2,1,0:T(8,128)}, f32[2,256,256]{2,1,0:T(8,128)S(1)}, u32[]{:S(2)}, u32[]{:S(2)}) collective-permute-start(f32[2,256,256]{2,1,0:T(8,128)} %bitcast.5), channel_id=1, source_target_pairs={{0,32},{1,33},{2,34},{3,35},{4,36},{5,37},{6,38},{7,39},{8,40},{9,... | collective-permute-start | bytes 1572872 | tf_op jit(solution)/shard_map/ppermute | solution.py:141
  5.1 27.7 %collective-permute-start.5 = (f32[2,128,256]{2,1,0:T(8,128)S(1)}, f32[2,128,256]{2,1,0:T(8,128)S(1)}, u32[]{:S(2)}, u32[]{:S(2)}) collective-permute-start(f32[2,128,256]{2,1,0:T(8,128)S(1)} %get-tuple-element.75), channel_id=1, source_target_pairs={{0,1},{1,2},{2,3},{3,4},{4,5},{5,6},{6,7},{7,8},{8,9},{9,10},{10,1... | collective-permute-start | bytes 786440 | tf_op jit(solution)/shard_map/ppermute | solution.py:141
  8.7 24.6 %collective-permute-start.3 = (f32[2,128,256]{2,1,0:T(8,128)S(1)}, f32[2,128,256]{2,1,0:T(8,128)S(1)}, u32[]{:S(2)}, u32[]{:S(2)}) collective-permute-start(f32[2,128,256]{2,1,0:T(8,128)S(1)} %get-tuple-element.71), channel_id=1, source_target_pairs={{0,257},{1,258},{2,259},{3,260},{4,261},{5,262},{6,263},{7,264},{8... | collective-permute-start | bytes 786440 | tf_op jit(solution)/shard_map/ppermute | solution.py:141
  13.3 0.7 %copy-start.1 = (s32[1,1,1,2,12]{4,3,2,1,0:T(2,128)S(1)}, s32[1,1,1,2,12]{4,3,2,1,0:T(2,128)}, u32[]{:S(2)}) copy-start(s32[1,1,1,2,12]{4,3,2,1,0:T(2,128)} %param.16) | copy-start | bytes 292
  13.3 0.7 %copy-start.2 = (s32[1,1,1,2,12]{4,3,2,1,0:T(2,128)S(1)}, s32[1,1,1,2,12]{4,3,2,1,0:T(2,128)}, u32[]{:S(2)}) copy-start(s32[1,1,1,2,12]{4,3,2,1,0:T(2,128)} %param.17) | copy-start | bytes 292
  13.4 0.7 %copy-start = (s32[1,1,1,2,12]{4,3,2,1,0:T(2,128)S(1)}, s32[1,1,1,2,12]{4,3,2,1,0:T(2,128)}, u32[]{:S(2)}) copy-start(s32[1,1,1,2,12]{4,3,2,1,0:T(2,128)} %param.15) | copy-start | bytes 292
  13.4 0.7 %copy-start.3 = (s32[1,1,1,2]{3,2,1,0:T(1,128)S(1)}, s32[1,1,1,2]{3,2,1,0:T(1,128)}, u32[]{:S(2)}) copy-start(s32[1,1,1,2]{3,2,1,0:T(1,128)} %param.18) | copy-start | bytes 28
  14.1 13.9 %collective-permute-start.1 = (f32[2,256,256]{2,1,0:T(8,128)}, f32[2,256,256]{2,1,0:T(8,128)S(1)}, u32[]{:S(2)}, u32[]{:S(2)}) collective-permute-start(f32[2,256,256]{2,1,0:T(8,128)} %get-tuple-element.49), channel_id=1, source_target_pairs={{31,63},{63,95},{95,127},{127,159},{159,191},{191,223},{223,255},{... | collective-permute-start | bytes 1572872 | tf_op jit(solution)/shard_map/cond/branch_1_fun/ppermute | solution.py:141
  16.7 11.1 %collective-permute-start = (f32[528,256]{1,0:T(8,128)S(1)}, f32[528,256]{1,0:T(8,128)S(1)}, u32[]{:S(2)}, u32[]{:S(2)}) collective-permute-start(f32[528,256]{1,0:T(8,128)S(1)} %get-tuple-element.42), channel_id=1, source_target_pairs={{0,256},{1,257},{2,258},{3,259},{4,260},{5,261},{6,262},{7,263},{8... | collective-permute-start | bytes 1622024 | tf_op jit(solution)/shard_map/cond/branch_1_fun/cond/branch_1_fun/ppermute | solution.py:141
  28.2 4.4 %collective-permute-start.2 = (f32[2,256,256]{2,1,0:T(8,128)S(1)}, f32[2,256,256]{2,1,0:T(8,128)S(1)}, u32[]{:S(2)}, u32[]{:S(2)}) collective-permute-start(f32[2,256,256]{2,1,0:T(8,128)S(1)} %broadcast_select_fusion.right_own), channel_id=1, source_target_pairs={{0,256},{1,257},{2,258},{3,259},{4,260},{5,261},{6,262},{7,263},{8... | collective-permute-start | bytes 1572872 | tf_op jit(solution)/shard_map/cond/branch_1_fun/ppermute | solution.py:141
  33.6 8.8 %collective-permute-start.6 = (f32[128,256]{1,0:T(8,128)S(1)}, f32[128,256]{1,0:T(8,128)S(1)}, u32[]{:S(2)}, u32[]{:S(2)}) collective-permute-start(f32[128,256]{1,0:T(8,128)S(1)} %get-tuple-element.80), channel_id=1, source_target_pairs={{0,512},{1,513},{2,514},{3,515},{4,516},{5,517},{6,518},{7,519},{8... | collective-permute-start | bytes 393224 | tf_op jit(solution)/shard_map/ppermute | solution.py:141
  36.7 7.2 %collective-permute-start.7 = (f32[128,256]{1,0:T(8,128)S(1)}, f32[128,256]{1,0:T(8,128)S(1)}, u32[]{:S(2)}, u32[]{:S(2)}) collective-permute-start(f32[128,256]{1,0:T(8,128)S(1)} %get-tuple-element.81), channel_id=1, source_target_pairs={{0,768},{1,769},{2,770},{3,771},{4,772},{5,773},{6,774},{7,775},{8... | collective-permute-start | bytes 393224 | tf_op jit(solution)/shard_map/ppermute | solution.py:141
  39.9 4.0 %collective-permute-start.8 = (f32[128,256]{1,0:T(8,128)S(1)}, f32[128,256]{1,0:T(8,128)S(1)}, u32[]{:S(2)}, u32[]{:S(2)}) collective-permute-start(f32[128,256]{1,0:T(8,128)S(1)} %get-tuple-element.84), channel_id=1, source_target_pairs={{0,256},{1,257},{2,258},{3,259},{4,260},{5,261},{6,262},{7,263},{8... | collective-permute-start | bytes 393224 | tf_op jit(solution)/shard_map/ppermute | solution.py:141

commit v10 on v8

--- a/solution.py
+++ b/solution.py
@@ -75,16 +75,17 @@
     weights[16:] = heard[size:, :]
 
 
-def split_kernel(left, same, cross, held, sems):
+def split_kernel(left, same, cross, sems):
     side = lax.axis_index("layer") & 1
     half = same.shape[1]
-    copies = [pltpu.make_async_copy(left.at[slot], held.at[slot], sems.at[slot]) for slot in range(2)]
+    copies = []
+    for out, half_at in ((same, side), (cross, 1 - side)):
+        rows = pl.ds(pl.multiple_of(half_at * half, half), half)
+        for slot in range(2):
+            copies.append(pltpu.make_async_copy(left.at[slot, rows], out.at[slot], sems.at[len(copies)]))
+            copies[-1].start()
     for copy in copies:
-        copy.start()
-    for slot in range(2):
-        copies[slot].wait()
-        for out, begin in ((same, side * half), (cross, (1 - side) * half)):
-            out[slot] = held[slot, pl.ds(pl.multiple_of(begin, half), half)]
+        copy.wait()
 
 
 def hold_kernel(*refs):
@@ -157,7 +158,7 @@
         out_shape=(jax.ShapeDtypeStruct((slots, half, cols), f32),) * 2,
         in_specs=[anywhere],
         out_specs=(vmem,) * 2,
-        scratch_shapes=[pltpu.VMEM((slots, rows, cols), f32), pltpu.SemaphoreType.DMA((2,))],
+        scratch_shapes=[pltpu.SemaphoreType.DMA((4,))],
         compiler_params=PARAMS,
         cost_estimate=pl.CostEstimate(flops=1 << 10, bytes_accessed=1 << 20, transcendentals=0),
         name="split",

time: 45.1 us -> 45.2 us (level)
  no operation moved by 1% of the time
where the time goes in v10:
time: 45.2 us; the launch traced here: 44.8 us
  starting transfers between devices  33.1 us (73%)
  Pallas kernels  5.13 us (11%)
  waiting for transfers between devices  4.91 us (11%)
  between operations  0.82 us (2%)
  local copies, waits for them, and re-layouts  0.68 us (2%)
    ppermute x9, starting transfers between devices, permute(): return lax.ppermute(value, names, pairs)  33.1 us
    ppermute x9, waiting for transfers between devices, permute(): return lax.ppermute(value, names, pairs)  4.91 us
    pallas_call x1, Pallas kernels, early(): pl.pallas_call(first_kernel, out_shape=(jax.ShapeDtypeStruct((4 * half +...  1.96 us
    pallas_call x1, Pallas kernels, local(): pl.pallas_call(split_kernel, out_shape=(jax.ShapeDtypeStruct((slots, half...  1.14 us
  transfers between devices with their start and end apart: 9, of which 3 were waited for; matrix products, arithmetic and copies ran while one was open for 0% of the time, Pallas kernels for 9%

profile of v10, /device:TPU:1, one launch (start us, length us, event | category | flops | bytes accessed | tf_op | source)
XLA Modules:
  0.0 44.8 jit_solution(29565564333198789)
XLA Ops:
  0.0 4.0 %collective-permute-start.4 = (f32[2,256,256]{2,1,0:T(8,128)}, f32[2,256,256]{2,1,0:T(8,128)S(1)}, u32[]{:S(2)}, u32[]{:S(2)}) collective-permute-start(f32[2,256,256]{2,1,0:T(8,128)} %bitcast.5), channel_id=1, source_target_pairs={{0,32},{1,33},{2,34},{3,35},{4,36},{5,37},{6,38},{7,39},{8,40},{9,... | collective-permute-start | bytes 1572872 | tf_op jit(solution)/shard_map/ppermute | solution.py:143
  4.0 1.1 %split.1 = (f32[2,128,256]{2,1,0:T(8,128)S(1)}, f32[2,128,256]{2,1,0:T(8,128)S(1)}) custom-call(f32[2,256,256]{2,1,0:T(8,128)} %bitcast.3), custom_call_target="tpu_custom_call" | custom-call | flops 1024 | bytes 1048576 | tf_op jit(solution)/shard_map/split/pallas_call | solution.py:156
  5.2 3.5 %collective-permute-start.5 = (f32[2,128,256]{2,1,0:T(8,128)S(1)}, f32[2,128,256]{2,1,0:T(8,128)S(1)}, u32[]{:S(2)}, u32[]{:S(2)}) collective-permute-start(f32[2,128,256]{2,1,0:T(8,128)S(1)} %get-tuple-element.75), channel_id=1, source_target_pairs={{0,1},{1,2},{2,3},{3,4},{4,5},{5,6},{6,7},{7,8},{8,9},{9,10},{10,1... | collective-permute-start | bytes 786440 | tf_op jit(solution)/shard_map/ppermute | solution.py:143
  8.7 4.7 %collective-permute-start.3 = (f32[2,128,256]{2,1,0:T(8,128)S(1)}, f32[2,128,256]{2,1,0:T(8,128)S(1)}, u32[]{:S(2)}, u32[]{:S(2)}) collective-permute-start(f32[2,128,256]{2,1,0:T(8,128)S(1)} %get-tuple-element.71), channel_id=1, source_target_pairs={{0,257},{1,258},{2,259},{3,260},{4,261},{5,262},{6,263},{7,264},{8... | collective-permute-start | bytes 786440 | tf_op jit(solution)/shard_map/ppermute | solution.py:143
  13.4 0.0 copy-start.1
  13.4 0.0 copy-start.2
  13.4 0.0 copy-start
  13.4 0.0 copy-start.3
  13.5 0.6 %copy-done.1 = s32[1,1,1,2,12]{4,3,2,1,0:T(2,128)S(1)} copy-done((s32[1,1,1,2,12]{4,3,2,1,0:T(2,128)S(1)}, s32[1,1,1,2,12]{4,3,2,1,0:T(2,128)}, u32[]{:S(2)}) %copy-start.1) | copy-done | bytes 120
  14.1 0.0 copy-done.2
  14.1 0.0 copy-done
  14.1 0.0 copy-done.3
  14.1 13.9 %conditional.3 = (f32[512,256]{1,0:T(8,128)S(1)}, f32[32,256]{1,0:T(8,128)S(1)}, f32[2,256,256]{2,1,0:T(8,128)S(1)}) conditional(s32[]{:T(128)} %convert_element_type.7, () %tuple.28, (pred[]{:T(512)}, s32[1,1,1,2,12]{4,3,2,1,0:T(2,128)S(1)}, s32[1,1,1,2,12]{4,3,2,1,0:T(2,128)S(1)}, s32[1,1,1,2,12]{4,3,2,1,0:T(2,128)S(1)}, ...), branch_computations={%region_0.0_spmd, %region_1.0_spmd} | conditional | flops 403046400 | bytes 10027173 | solution.py:175
  14.1 0.7 %collective-permute-start.1 = (f32[2,256,256]{2,1,0:T(8,128)}, f32[2,256,256]{2,1,0:T(8,128)S(1)}, u32[]{:S(2)}, u32[]{:S(2)}) collective-permute-start(f32[2,256,256]{2,1,0:T(8,128)} %get-tuple-element.49), channel_id=1, source_target_pairs={{31,63},{63,95},{95,127},{127,159},{159,191},{191,223},{223,255},{... | collective-permute-start | bytes 1572872 | tf_op jit(solution)/shard_map/cond/branch_1_fun/ppermute | solution.py:143
  14.8 13.2 %conditional = ((f32[512,256]{1,0:T(8,128)S(1)}, f32[32,256]{1,0:T(8,128)S(1)})) conditional(s32[]{:T(128)} %convert_element_type.1, () %tuple.19, (s32[1,1,1,2,12]{4,3,2,1,0:T(2,128)S(1)}, s32[1,1,1,2,12]{4,3,2,1,0:T(2,128)S(1)}, s32[1,1,1,2,12]{4,3,2,1,0:T(2,128)S(1)}, s32[1,1,1,2]{3,2,1,0:T(1,128)S(1)}, f32[2,256,256]{2,1,0:T(8,128)}, ...), branch_computations={%region_2.0_spmd, %region_3.0_spmd} | conditional | flops 402784256 | bytes 5832752 | solution.py:175
  14.8 2.0 %first_step.1 = (f32[528,256]{1,0:T(8,128)S(1)}, f32[528,256]{1,0:T(8,128)S(1)}) custom-call(s32[1,1,1,2,12]{4,3,2,1,0:T(2,128)S(1)} %get-tuple-element.35.li, s32[1,1,1,2,12]{4,3,2,1,0:T(2,128)S(1)} %get-tuple-element.36.ri, s32[1,1,1,2,12]{4,3,2,1,0:T(2,128)S(1)} %get-tuple-element.37.ti, s32[1,1,1,2]{3,2,1,0:T(1,128)S(1)} %get-tuple-element.38.counts, ...), custom_call_target="tpu_custom_call" | custom-call | flops 402653184 | bytes 2097152 | tf_op jit(solution)/shard_map/cond/branch_1_fun/cond/branch_1_fun/first_step/pallas_call | solution.py:189
  16.8 9.6 %collective-permute-start = (f32[528,256]{1,0:T(8,128)S(1)}, f32[528,256]{1,0:T(8,128)S(1)}, u32[]{:S(2)}, u32[]{:S(2)}) collective-permute-start(f32[528,256]{1,0:T(8,128)S(1)} %get-tuple-element.42), channel_id=1, source_target_pairs={{0,256},{1,257},{2,258},{3,259},{4,260},{5,261},{6,262},{7,263},{8... | collective-permute-start | bytes 1622024 | tf_op jit(solution)/shard_map/cond/branch_1_fun/cond/branch_1_fun/ppermute | solution.py:143
  26.4 1.5 %collective-permute-done.heard = f32[528,256]{1,0:T(8,128)S(1)} collective-permute-done((f32[528,256]{1,0:T(8,128)S(1)}, f32[528,256]{1,0:T(8,128)S(1)}, u32[]{:S(2)}, u32[]{:S(2)}) %collective-permute-start) | collective-permute-done | bytes 540704 | tf_op jit(solution)/shard_map/cond/branch_1_fun/cond/branch_1_fun/ppermute | solution.py:143
  27.9 0.1 join.1
  28.0 0.0 collective-permute-done.1.refs_0_
  28.1 0.0 collective-permute-done.4.refs_0_
  28.2 4.6 %conditional.4 = ((bf16[4,256,256]{2,1,0:T(8,128)(2,1)S(1)}, bf16[4,256,256]{2,1,0:T(8,128)(2,1)S(1)})) conditional(s32[]{:T(128)} %convert_element_type.7, () %tuple.27, (f32[2,256,256]{2,1,0:T(8,128)S(1)}, f32[2,256,256]{2,1,0:T(8,128)S(1)}) %tuple.30), branch_computations={%region_4.0_spmd, %region_5.6_spmd} | conditional | flops 1179651 | bytes 5767246 | solution.py:175
  28.2 0.1 broadcast_select_fusion.right_own
  28.3 2.8 %collective-permute-start.2 = (f32[2,256,256]{2,1,0:T(8,128)S(1)}, f32[2,256,256]{2,1,0:T(8,128)S(1)}, u32[]{:S(2)}, u32[]{:S(2)}) collective-permute-start(f32[2,256,256]{2,1,0:T(8,128)S(1)} %broadcast_select_fusion.right_own), channel_id=1, source_target_pairs={{0,256},{1,257},{2,258},{3,259},{4,260},{5,261},{6,262},{7,263},{8... | collective-permute-start | bytes 1572872 | tf_op jit(solution)/shard_map/cond/branch_1_fun/ppermute | solution.py:143
  31.1 1.5 %collective-permute-done.2.right_mate = f32[2,256,256]{2,1,0:T(8,128)S(1)} collective-permute-done((f32[2,256,256]{2,1,0:T(8,128)S(1)}, f32[2,256,256]{2,1,0:T(8,128)S(1)}, u32[]{:S(2)}, u32[]{:S(2)}) %collective-permute-start.2) | collective-permute-done | bytes 524320 | tf_op jit(solution)/shard_map/cond/branch_1_fun/ppermute | solution.py:143
  32.6 0.2 ready.1
  32.8 0.0 collective-permute-done.5.left
  32.8 0.5 %own_layer.1.part = f32[512,256]{1,0:T(8,128)S(1)} custom-call(f32[2,128,256]{2,1,0:T(8,128)S(1)} %collective-permute-done.5.left, bf16[4,256,256]{2,1,0:T(8,128)(2,1)S(1)} %get-tuple-element.73.right_high, bf16[4,256,256]{2,1,0:T(8,128)(2,1)S(1)} %get-tuple-element.74.right_low, f32[512,256]{1,0:T(8,128)S(1)} %get-tuple-element.78.base, ...), custom_call_target="tpu_custom_call" | custom-call | flops 201326592 | bytes 2097152 | tf_op jit(solution)/shard_map/own_layer/pallas_call | solution.py:234
  33.2 0.0 collective-permute-done.3.left
  33.3 0.5 %mate_layer.1 = (f32[128,256]{1,0:T(8,128)S(1)}, f32[128,256]{1,0:T(8,128)S(1)}, f32[128,256]{1,0:T(8,128)S(1)}, f32[128,256]{1,0:T(8,128)S(1)}) custom-call(f32[2,128,256]{2,1,0:T(8,128)S(1)} %collective-permute-done.3.left, bf16[4,256,256]{2,1,0:T(8,128)(2,1)S(1)} %get-tuple-element.73.right_high, bf16[4,256,256]{2,1,0:T(8,128)(2,1)S(1)} %get-tuple-element.74.right_low, ...), custom_call_target="tpu_custom_call" | custom-call | flops 201326592 | bytes 2097152 | tf_op jit(solution)/shard_map/mate_layer/pallas_call | solution.py:243
  33.7 3.1 %collective-permute-start.6 = (f32[128,256]{1,0:T(8,128)S(1)}, f32[128,256]{1,0:T(8,128)S(1)}, u32[]{:S(2)}, u32[]{:S(2)}) collective-permute-start(f32[128,256]{1,0:T(8,128)S(1)} %get-tuple-element.80), channel_id=1, source_target_pairs={{0,512},{1,513},{2,514},{3,515},{4,516},{5,517},{6,518},{7,519},{8... | collective-permute-start | bytes 393224 | tf_op jit(solution)/shard_map/ppermute | solution.py:143
  36.8 2.7 %collective-permute-start.7 = (f32[128,256]{1,0:T(8,128)S(1)}, f32[128,256]{1,0:T(8,128)S(1)}, u32[]{:S(2)}, u32[]{:S(2)}) collective-permute-start(f32[128,256]{1,0:T(8,128)S(1)} %get-tuple-element.81), channel_id=1, source_target_pairs={{0,768},{1,769},{2,770},{3,771},{4,772},{5,773},{6,774},{7,775},{8... | collective-permute-start | bytes 393224 | tf_op jit(solution)/shard_map/ppermute | solution.py:143
  39.6 1.9 %collective-permute-start.8 = (f32[128,256]{1,0:T(8,128)S(1)}, f32[128,256]{1,0:T(8,128)S(1)}, u32[]{:S(2)}, u32[]{:S(2)}) collective-permute-start(f32[128,256]{1,0:T(8,128)S(1)} %get-tuple-element.84), channel_id=1, source_target_pairs={{0,256},{1,257},{2,258},{3,259},{4,260},{5,261},{6,262},{7,263},{8... | collective-permute-start | bytes 393224 | tf_op jit(solution)/shard_map/ppermute | solution.py:143
  42.1 0.0 collective-permute-done.6.refs_0_
  42.1 1.8 %collective-permute-done.7.refs_1_ = f32[128,256]{1,0:T(8,128)S(1)} collective-permute-done((f32[128,256]{1,0:T(8,128)S(1)}, f32[128,256]{1,0:T(8,128)S(1)}, u32[]{:S(2)}, u32[]{:S(2)}) %collective-permute-start.7) | collective-permute-done | bytes 131104 | tf_op jit(solution)/shard_map/ppermute | solution.py:143
  44.0 0.0 collective-permute-done.8.core
  44.0 0.7 %last_sum.1 = f32[256,256]{1,0:T(8,128)} custom-call(s32[1,1,1]{2,1,0:T(1,128)S(6)} %copy.26.mask, f32[128,256]{1,0:T(8,128)S(1)} %get-tuple-element.82.chip, f32[128,256]{1,0:T(8,128)S(1)} %get-tuple-element.83.far, f32[128,256]{1,0:T(8,128)S(1)} %collective-permute-done.8.core, f32[128,256]{1,0:T(8,128)S(1)} %get-tuple-element.85.own), custom_call_target="tpu_custom_call" | custom-call | flops 262144 | bytes 1048576 | tf_op jit(solution)/shard_map/last_sum/pallas_call | solution.py:256
  (5 shorter events, 0.2 us)
Async XLA Ops:
  0.0 28.1 %collective-permute-start.4 = (f32[2,256,256]{2,1,0:T(8,128)}, f32[2,256,256]{2,1,0:T(8,128)S(1)}, u32[]{:S(2)}, u32[]{:S(2)}) collective-permute-start(f32[2,256,256]{2,1,0:T(8,128)} %bitcast.5), channel_id=1, source_target_pairs={{0,32},{1,33},{2,34},{3,35},{4,36},{5,37},{6,38},{7,39},{8,40},{9,... | collective-permute-start | bytes 1572872 | tf_op jit(solution)/shard_map/ppermute | solution.py:143
  5.2 27.6 %collective-permute-start.5 = (f32[2,128,256]{2,1,0:T(8,128)S(1)}, f32[2,128,256]{2,1,0:T(8,128)S(1)}, u32[]{:S(2)}, u32[]{:S(2)}) collective-permute-start(f32[2,128,256]{2,1,0:T(8,128)S(1)} %get-tuple-element.75), channel_id=1, source_target_pairs={{0,1},{1,2},{2,3},{3,4},{4,5},{5,6},{6,7},{7,8},{8,9},{9,10},{10,1... | collective-permute-start | bytes 786440 | tf_op jit(solution)/shard_map/ppermute | solution.py:143
  8.7 24.5 %collective-permute-start.3 = (f32[2,128,256]{2,1,0:T(8,128)S(1)}, f32[2,128,256]{2,1,0:T(8,128)S(1)}, u32[]{:S(2)}, u32[]{:S(2)}) collective-permute-start(f32[2,128,256]{2,1,0:T(8,128)S(1)} %get-tuple-element.71), channel_id=1, source_target_pairs={{0,257},{1,258},{2,259},{3,260},{4,261},{5,262},{6,263},{7,264},{8... | collective-permute-start | bytes 786440 | tf_op jit(solution)/shard_map/ppermute | solution.py:143
  13.4 0.7 %copy-start.1 = (s32[1,1,1,2,12]{4,3,2,1,0:T(2,128)S(1)}, s32[1,1,1,2,12]{4,3,2,1,0:T(2,128)}, u32[]{:S(2)}) copy-start(s32[1,1,1,2,12]{4,3,2,1,0:T(2,128)} %param.16) | copy-start | bytes 292
  13.4 0.7 %copy-start.2 = (s32[1,1,1,2,12]{4,3,2,1,0:T(2,128)S(1)}, s32[1,1,1,2,12]{4,3,2,1,0:T(2,128)}, u32[]{:S(2)}) copy-start(s32[1,1,1,2,12]{4,3,2,1,0:T(2,128)} %param.17) | copy-start | bytes 292
  13.4 0.7 %copy-start = (s32[1,1,1,2,12]{4,3,2,1,0:T(2,128)S(1)}, s32[1,1,1,2,12]{4,3,2,1,0:T(2,128)}, u32[]{:S(2)}) copy-start(s32[1,1,1,2,12]{4,3,2,1,0:T(2,128)} %param.15) | copy-start | bytes 292
  13.4 0.7 %copy-start.3 = (s32[1,1,1,2]{3,2,1,0:T(1,128)S(1)}, s32[1,1,1,2]{3,2,1,0:T(1,128)}, u32[]{:S(2)}) copy-start(s32[1,1,1,2]{3,2,1,0:T(1,128)} %param.18) | copy-start | bytes 28
  14.1 13.9 %collective-permute-start.1 = (f32[2,256,256]{2,1,0:T(8,128)}, f32[2,256,256]{2,1,0:T(8,128)S(1)}, u32[]{:S(2)}, u32[]{:S(2)}) collective-permute-start(f32[2,256,256]{2,1,0:T(8,128)} %get-tuple-element.49), channel_id=1, source_target_pairs={{31,63},{63,95},{95,127},{127,159},{159,191},{191,223},{223,255},{... | collective-permute-start | bytes 1572872 | tf_op jit(solution)/shard_map/cond/branch_1_fun/ppermute | solution.py:143
  16.8 11.1 %collective-permute-start = (f32[528,256]{1,0:T(8,128)S(1)}, f32[528,256]{1,0:T(8,128)S(1)}, u32[]{:S(2)}, u32[]{:S(2)}) collective-permute-start(f32[528,256]{1,0:T(8,128)S(1)} %get-tuple-element.42), channel_id=1, source_target_pairs={{0,256},{1,257},{2,258},{3,259},{4,260},{5,261},{6,262},{7,263},{8... | collective-permute-start | bytes 1622024 | tf_op jit(solution)/shard_map/cond/branch_1_fun/cond/branch_1_fun/ppermute | solution.py:143
  28.3 4.3 %collective-permute-start.2 = (f32[2,256,256]{2,1,0:T(8,128)S(1)}, f32[2,256,256]{2,1,0:T(8,128)S(1)}, u32[]{:S(2)}, u32[]{:S(2)}) collective-permute-start(f32[2,256,256]{2,1,0:T(8,128)S(1)} %broadcast_select_fusion.right_own), channel_id=1, source_target_pairs={{0,256},{1,257},{2,258},{3,259},{4,260},{5,261},{6,262},{7,263},{8... | collective-permute-start | bytes 1572872 | tf_op jit(solution)/shard_map/cond/branch_1_fun/ppermute | solution.py:143
  33.7 8.4 %collective-permute-start.6 = (f32[128,256]{1,0:T(8,128)S(1)}, f32[128,256]{1,0:T(8,128)S(1)}, u32[]{:S(2)}, u32[]{:S(2)}) collective-permute-start(f32[128,256]{1,0:T(8,128)S(1)} %get-tuple-element.80), channel_id=1, source_target_pairs={{0,512},{1,513},{2,514},{3,515},{4,516},{5,517},{6,518},{7,519},{8... | collective-permute-start | bytes 393224 | tf_op jit(solution)/shard_map/ppermute | solution.py:143
  36.8 7.2 %collective-permute-start.7 = (f32[128,256]{1,0:T(8,128)S(1)}, f32[128,256]{1,0:T(8,128)S(1)}, u32[]{:S(2)}, u32[]{:S(2)}) collective-permute-start(f32[128,256]{1,0:T(8,128)S(1)} %get-tuple-element.81), channel_id=1, source_target_pairs={{0,768},{1,769},{2,770},{3,771},{4,772},{5,773},{6,774},{7,775},{8... | collective-permute-start | bytes 393224 | tf_op jit(solution)/shard_map/ppermute | solution.py:143
  39.6 4.5 %collective-permute-start.8 = (f32[128,256]{1,0:T(8,128)S(1)}, f32[128,256]{1,0:T(8,128)S(1)}, u32[]{:S(2)}, u32[]{:S(2)}) collective-permute-start(f32[128,256]{1,0:T(8,128)S(1)} %get-tuple-element.84), channel_id=1, source_target_pairs={{0,256},{1,257},{2,258},{3,259},{4,260},{5,261},{6,262},{7,263},{8... | collective-permute-start | bytes 393224 | tf_op jit(solution)/shard_map/ppermute | solution.py:143
